TPU v7x, 512 devices: a whole 4x4x16 slice. The times are simulated.
512 devices in a mesh: gx: 16 (over z), gy: 8 (over y, core), gz: 4 (over x).
Axes of the slice: x: 4, y: 4, z: 16, core: 2. Of those that a mesh axis runs over, the one named last changes fastest.
Arguments:
- frac_positions: float32 [16, 16, 8, 3, 128], P('gx', 'gy', 'gz'), may hold values from 0 to 1
- shielding: float32 [16, 16, 8, 128], P('gx', 'gy', 'gz'), may hold values from 0.5 to 0.9
- hardness: float32 [16, 16, 8, 128], P('gx', 'gy', 'gz'), may hold values from 14 to 20
- electroneg: float32 [16, 16, 8, 128], P('gx', 'gy', 'gz'), may hold values from 3 to 9
- counts: int32 [16, 16, 8], P('gx', 'gy', 'gz'), may hold values from 64 to 128, as said below
- neighbor_list: int32 [16, 16, 8, 13], P('gx', 'gy', 'gz'), may hold values from -1 to 12, as said below
Outputs:
- charges: float32 [16, 16, 8, 128], P('gx', 'gy', 'gz')
- residual: float32 [2, 16, 16, 8, 128], P(None, 'gx', 'gy', 'gz')
Inputs may be any that keep to these rules, and one draw needn't show every extreme that they name: `counts`: some cell holds exactly 64 atoms and some cell exactly 128. `neighbor_list`: each cell's row lists 9 to 13 distinct codes of 0 to 12 first, and -1 in the remaining entries; some row lists all 13 codes and some row only 9.
All inputs are finite; a program needn't handle non-finite values.
Results may differ from a plain program's by a relative error of at most 0.0003.
Values sent between devices are 32-bit elements; how exact they have to be, the bound alone decides.
No kernel may reach another device: no remote copies, remote signals or barrier semaphores. Data moves between devices by JAX's collectives and lax.ppermute only.
A program may use at most 64 MiB of HBM per device.

v0:
```python
import jax
import jax.numpy as jnp
from jax import lax
from jax.sharding import PartitionSpec as P

ITERS = 4


CUTOFF = 10.0
COULOMB = 14.4
HALF_SHELL = [
    (0, 0, 1),
    (0, 1, -1),
    (0, 1, 0),
    (0, 1, 1),
    (1, -1, -1),
    (1, -1, 0),
    (1, -1, 1),
    (1, 0, -1),
    (1, 0, 0),
    (1, 0, 1),
    (1, 1, -1),
    (1, 1, 0),
    (1, 1, 1),
]


def shifted(value, axis, steps):
    count = lax.axis_size(axis)
    pairs = [(source, (source + steps) % count) for source in range(count)]
    return lax.ppermute(value, axis, pairs)


def pair_tile(place_i, shield_i, mask_i, place_j, shield_j, mask_j, offset):
    square = jnp.zeros(place_i.shape[:-2] + (place_i.shape[-1], place_j.shape[-1]), jnp.float32)
    for component in range(3):
        apart = (
            offset[component] + place_j[..., component, None, :] - place_i[..., component, :, None]
        ) * CUTOFF
        square = square + apart * apart
    radius = jnp.sqrt(square)
    ratio = radius / CUTOFF
    fourth = ratio * ratio * ratio * ratio
    taper = 1.0 + fourth * (-35.0 + ratio * (84.0 + ratio * (-70.0 + 20.0 * ratio)))
    screen = (shield_i[..., :, None] * shield_j[..., None, :]) ** (-1.5)
    coulomb = COULOMB * taper / jnp.cbrt(square * radius + screen)
    return jnp.where(ratio < 1.0, coulomb, 0.0) * mask_i[..., :, None] * mask_j[..., None, :]


def window(array, start, sizes):
    return array[
        start[0] : start[0] + sizes[0],
        start[1] : start[1] + sizes[1],
        start[2] : start[2] + sizes[2],
    ]


def window_rhs(array, start, sizes):
    return array[
        :,
        start[0] : start[0] + sizes[0],
        start[1] : start[1] + sizes[1],
        start[2] : start[2] + sizes[2],
    ]


def upper_geometry(packed):
    arrived = shifted(packed, "gx", -1)
    packed = jnp.concatenate([packed, arrived], axis=0)
    arrived = shifted(packed[:, :1], "gy", -1)
    packed = jnp.concatenate([packed, arrived], axis=1)
    arrived = shifted(packed[:, :, :1], "gz", -1)
    packed = jnp.concatenate([packed, arrived], axis=2)
    return jnp.pad(packed, ((1, 0), (1, 0), (1, 0), (0, 0), (0, 0)))


def upper_ghosts(field):
    arrived = shifted(field, "gx", -1)
    field = jnp.concatenate([field, arrived], axis=1)
    arrived = shifted(field[:, :, :1], "gy", -1)
    field = jnp.concatenate([field, arrived], axis=2)
    arrived = shifted(field[:, :, :, :1], "gz", -1)
    field = jnp.concatenate([field, arrived], axis=3)
    return jnp.pad(field, ((0, 0), (1, 0), (1, 0), (1, 0), (0, 0)))


def return_partials(partial_value, sizes):
    cells_x, cells_y, cells_z = sizes
    rim = partial_value[:, cells_x + 1, 1:, 1:]
    arrived = shifted(rim, "gx", 1)
    partial_value = partial_value.at[:, 1, 1:, 1:].add(arrived)
    rim = partial_value[:, 1 : cells_x + 1, cells_y + 1, 1:]
    arrived = shifted(rim, "gy", 1)
    partial_value = partial_value.at[:, 1 : cells_x + 1, 1, 1:].add(arrived)
    rim = partial_value[:, 1 : cells_x + 1, 1 : cells_y + 1, cells_z + 1]
    arrived = shifted(rim, "gz", 1)
    partial_value = partial_value.at[:, 1 : cells_x + 1, 1 : cells_y + 1, 1].add(arrived)
    return partial_value[:, 1 : cells_x + 1, 1 : cells_y + 1, 1 : cells_z + 1]


def inner(first, second):
    return jnp.sum(first * second, axis=(1, 2, 3, 4))


def squares(residual):
    return lax.psum(inner(residual, residual), ("gx", "gy", "gz"))


def shards(frac_positions, shielding, hardness, electroneg, counts, neighbor_list):
    sizes = counts.shape
    slots = hardness.shape[-1]
    masks = (lax.broadcasted_iota(jnp.int32, hardness.shape, 3) < counts[..., None]).astype(
        jnp.float32
    )
    codes = jnp.arange(13, dtype=jnp.int32)
    flags = jnp.any(neighbor_list[..., :, None] == codes, axis=-2).astype(jnp.float32)
    flag_row = jnp.pad(flags, ((0, 0), (0, 0), (0, 0), (0, slots - 13)))
    packed = jnp.concatenate(
        [frac_positions, shielding[:, :, :, None], masks[:, :, :, None], flag_row[:, :, :, None]],
        axis=3,
    )
    packed = upper_geometry(packed)
    places_e = packed[:, :, :, 0:3]
    shields_e = packed[:, :, :, 3]
    masks_e = packed[:, :, :, 4]
    flags_e = packed[:, :, :, 5, :13]
    identity = jnp.eye(slots, dtype=jnp.float32)
    self_tile = pair_tile(
        frac_positions,
        shielding,
        masks,
        frac_positions,
        shielding,
        masks,
        jnp.zeros((3,), jnp.float32),
    ) * (1.0 - identity)
    diagonal = (hardness * masks)[None]
    starts_i = [(1 + max(-o[0], 0), 1 + max(-o[1], 0), 1 + max(-o[2], 0)) for o in HALF_SHELL]
    starts_j = [(1 + max(o[0], 0), 1 + max(o[1], 0), 1 + max(o[2], 0)) for o in HALF_SHELL]
    vectors = HALF_SHELL
    chosen = [window(flags_e, starts_i[number], sizes)[..., number] for number in range(13)]

    def stacked(array, starts):
        return jnp.stack([window(array, start, sizes) for start in starts])

    def build(items):
        place_i, shield_i, mask_i, place_j, shield_j, mask_j, picked, vector = items
        return (
            pair_tile(place_i, shield_i, mask_i, place_j, shield_j, mask_j, vector)
            * picked[..., None, None]
        )

    tiles = lax.map(
        build,
        (
            stacked(places_e, starts_i),
            stacked(shields_e, starts_i),
            stacked(masks_e, starts_i),
            stacked(places_e, starts_j),
            stacked(shields_e, starts_j),
            stacked(masks_e, starts_j),
            jnp.stack(chosen),
            jnp.array(vectors, jnp.float32),
        ),
    )

    def operate(field):
        extended = upper_ghosts(field)
        result = diagonal * field + jnp.einsum(
            "abcij,rabcj->rabci", self_tile, field, precision=lax.Precision.HIGHEST
        )
        from_j = jnp.stack([window_rhs(extended, start, sizes) for start in starts_j])
        from_i = jnp.stack([window_rhs(extended, start, sizes) for start in starts_i])
        to_i = jnp.einsum("kabcij,krabcj->krabci", tiles, from_j, precision=lax.Precision.HIGHEST)
        to_j = jnp.einsum("kabcij,krabci->krabcj", tiles, from_i, precision=lax.Precision.HIGHEST)
        partial_value = jnp.zeros_like(extended)
        for number in range(13):
            first = starts_i[number]
            second = starts_j[number]
            partial_value = partial_value.at[
                :,
                first[0] : first[0] + sizes[0],
                first[1] : first[1] + sizes[1],
                first[2] : first[2] + sizes[2],
            ].add(to_i[number])
            partial_value = partial_value.at[
                :,
                second[0] : second[0] + sizes[0],
                second[1] : second[1] + sizes[1],
                second[2] : second[2] + sizes[2],
            ].add(to_j[number])
        return result + return_partials(partial_value, sizes)

    def spread(vector):
        return vector[:, None, None, None, None]

    right = jnp.stack([-electroneg * masks, -masks], axis=0)
    solution = jnp.zeros_like(right)
    residual = right
    direction = right
    norm_now = squares(residual)
    for step in range(ITERS):
        image = operate(direction)
        alpha = norm_now / lax.psum(inner(direction, image), ("gx", "gy", "gz"))
        solution = solution + spread(alpha) * direction
        residual = residual - spread(alpha) * image
        norm_next = squares(residual)
        direction = residual + spread(norm_next / norm_now) * direction
        norm_now = norm_next
    totals = lax.psum(jnp.sum(solution, axis=(1, 2, 3, 4)), ("gx", "gy", "gz"))
    charges = solution[0] - totals[0] / totals[1] * solution[1]
    return (charges, residual)


def solution(mesh):
    placed = (
        P("gx", "gy", "gz", None, None),
        P("gx", "gy", "gz", None),
        P("gx", "gy", "gz", None),
        P("gx", "gy", "gz", None),
        P("gx", "gy", "gz"),
        P("gx", "gy", "gz", None),
    )
    return jax.shard_map(
        shards,
        mesh=mesh,
        in_specs=placed,
        out_specs=(P("gx", "gy", "gz", None), P(None, "gx", "gy", "gz", None)),
        check_vma=False,
    )
```

profile of v0, /device:TPU:1, one launch (start us, length us, event | category | flops | bytes accessed | tf_op | source)
XLA Modules:
  0.0 1088.8 jit_solution(673713911514920669)
XLA Ops:
  2.9 11.9 %collective-permute-start.3 = (f32[1,2,2,6,128]{4,2,1,3,0:T(2,128)S(1)}, f32[1,2,2,6,128]{4,2,1,3,0:T(2,128)S(1)}, u32[]{:S(2)}, u32[]{:S(2)}) collective-permute-start(f32[1,2,2,6,128]{4,2,1,3,0:T(2,128)S(1)} %pad_maximum_fusion.7), channel_id=1, source_target_pairs={{0,480},{32,0},{64,32},{96,64},{128,96},{160,128},{192,160},{224,1... | collective-permute-start | bytes 36872 | tf_op jit(solution)/shard_map/ppermute | solution.py:31
  25.9 4.4 collective-permute-start.2
  58.2 79.6 %while.129 = (s32[]{:T(128)}, f32[13,1,2,2,128,128]{5,4,3,2,1,0:T(8,128)S(1)}, f32[13,1,2,2,3,128]{5,3,2,4,1,0:T(2,128)}, f32[13,1,2,2,3,128]{5,3,2,4,1,0:T(2,12...) while((s32[]{:T(128)}, ...), condition=%wide.region_4.5_spmd.clone, body=%wide.region_3.4_spmd.sunk.clone.sunk | while | flops 2164226 | bytes 349417 | solution.py:153
  137.9 6.2 fusion.36
  144.1 3.0 fusion.39
  149.5 3.7 collective-permute-done.6
  159.2 3.6 collective-permute-done.8
  164.2 102.1 %all-reduce.6 = (f32[2]{0:T(128)S(1)}, f32[2]{0:T(128)S(1)}) all-reduce(f32[2]{0:T(128)S(1)} %get-tuple-element.1577, f32[2]{0:T(128)S(1)} %get-tuple-element.1576), channel_id=1, replica_groups=mesh['gx'=16,'gy'=8,'gz'=4] {'gx','gy','gz'}, use_global_device_ids=true, to_apply=%region_1.2 | all-reduce | flops 4 | bytes 32 | tf_op jit(solution)/shard_map/psum | solution.py:106
  266.4 100.3 %psum.65 = f32[2]{0:T(128)S(1)} all-reduce(f32[2]{0:T(128)S(1)} %get-tuple-element.1634), channel_id=1, replica_groups=mesh['gx'=16,'gy'=8,'gz'=4] {'gx','gy','gz'}, use_global_device_ids=true, to_apply=%region_8.9 | all-reduce | flops 2 | bytes 16 | tf_op jit(solution)/shard_map/psum | solution.py:106
  366.8 2.8 collective-permute-start.9
  375.1 3.1 collective-permute-start.11
  379.7 5.4 fusion.42
  385.2 3.0 fusion.45
  391.3 2.9 collective-permute-done.12
  399.3 3.5 collective-permute-done.14
  404.2 102.6 %psum.66 = f32[2]{0:T(128)S(1)} all-reduce(f32[2]{0:T(128)S(1)} %get-tuple-element.1714), channel_id=1, replica_groups=mesh['gx'=16,'gy'=8,'gz'=4] {'gx','gy','gz'}, use_global_device_ids=true, to_apply=%region_10.11 | all-reduce | flops 2 | bytes 16 | tf_op jit(solution)/shard_map/psum | solution.py:204
  507.0 99.6 %psum.67 = f32[2]{0:T(128)S(1)} all-reduce(f32[2]{0:T(128)S(1)} %get-tuple-element.1622), channel_id=1, replica_groups=mesh['gx'=16,'gy'=8,'gz'=4] {'gx','gy','gz'}, use_global_device_ids=true, to_apply=%region_12.13 | all-reduce | flops 2 | bytes 16 | tf_op jit(solution)/shard_map/psum | solution.py:106
  606.7 2.9 collective-permute-start.15
  614.4 3.2 collective-permute-start.17
  619.1 5.4 fusion.48
  624.5 3.0 fusion.51
  630.6 2.9 collective-permute-done.18
  638.7 3.5 collective-permute-done.20
  643.5 102.7 %psum.68 = f32[2]{0:T(128)S(1)} all-reduce(f32[2]{0:T(128)S(1)} %get-tuple-element.1716), channel_id=1, replica_groups=mesh['gx'=16,'gy'=8,'gz'=4] {'gx','gy','gz'}, use_global_device_ids=true, to_apply=%region_14.15 | all-reduce | flops 2 | bytes 16 | tf_op jit(solution)/shard_map/psum | solution.py:204
  746.4 99.6 %psum.69 = f32[2]{0:T(128)S(1)} all-reduce(f32[2]{0:T(128)S(1)} %get-tuple-element.1610), channel_id=1, replica_groups=mesh['gx'=16,'gy'=8,'gz'=4] {'gx','gy','gz'}, use_global_device_ids=true, to_apply=%region_16.17 | all-reduce | flops 2 | bytes 16 | tf_op jit(solution)/shard_map/psum | solution.py:106
  853.8 3.4 collective-permute-start.23
  858.5 5.4 fusion.54
  863.9 3.0 fusion.57
  870.0 2.9 collective-permute-done.24
  878.1 3.5 collective-permute-done.26
  883.0 102.7 %psum.70 = f32[2]{0:T(128)S(1)} all-reduce(f32[2]{0:T(128)S(1)} %get-tuple-element.1718), channel_id=1, replica_groups=mesh['gx'=16,'gy'=8,'gz'=4] {'gx','gy','gz'}, use_global_device_ids=true, to_apply=%region_18.19 | all-reduce | flops 2 | bytes 16 | tf_op jit(solution)/shard_map/psum | solution.py:204
  985.8 99.6 %psum.71 = f32[2]{0:T(128)S(1)} all-reduce(f32[2]{0:T(128)S(1)} %get-tuple-element.1598), channel_id=1, replica_groups=mesh['gx'=16,'gy'=8,'gz'=4] {'gx','gy','gz'}, use_global_device_ids=true, to_apply=%region_20.21 | all-reduce | flops 2 | bytes 16 | tf_op jit(solution)/shard_map/psum | solution.py:210
  (538 shorter events, 183.1 us)
Async XLA Ops:
  2.9 27.4 %collective-permute-start.3 = (f32[1,2,2,6,128]{4,2,1,3,0:T(2,128)S(1)}, f32[1,2,2,6,128]{4,2,1,3,0:T(2,128)S(1)}, u32[]{:S(2)}, u32[]{:S(2)}) collective-permute-start(f32[1,2,2,6,128]{4,2,1,3,0:T(2,128)S(1)} %pad_maximum_fusion.7), channel_id=1, source_target_pairs={{0,480},{32,0},{64,32},{96,64},{128,96},{160,128},{192,160},{224,1... | collective-permute-start | bytes 36872 | tf_op jit(solution)/shard_map/ppermute | solution.py:31
  17.0 4.4 collective-permute-start
  21.3 4.6 collective-permute-start.1
  25.9 5.3 collective-permute-start.2
  31.0 3.1 collective-permute-start.4
  34.9 4.5 collective-permute-start.5
  38.0 12.9 %copy-start.2 = (f32[13,2,1,2,2,128]{5,1,4,3,2,0:T(2,128)}, f32[13,2,1,2,2,128]{5,1,4,3,2,0:T(2,128)S(1)}, u32[]{:S(2)}) copy-start(f32[13,2,1,2,2,128]{5,1,4,3,2,0:T(2,128)S(1)} %get-tuple-element.1704) | copy-start | bytes 159748
  57.6 86.5 %copy-start.3 = (f32[13,2,1,2,2,128]{5,1,4,3,2,0:T(2,128)S(1)}, f32[13,2,1,2,2,128]{5,1,4,3,2,0:T(2,128)}, u32[]{:S(2)}) copy-start(f32[13,2,1,2,2,128]{5,1,4,3,2,0:T(2,128)} %copy-done.2) | copy-start | bytes 159748
  137.9 17.7 %copy-start.6 = (s32[1,2,2]{2,1,0:T(2,128)S(1)}, s32[1,2,2]{2,1,0:T(2,128)}, u32[]{:S(2)}) copy-start(s32[1,2,2]{2,1,0:T(2,128)} %param.245) | copy-start | bytes 52
  137.9 24.9 %copy-start.1 = (f32[1,2,2,128]{3,2,1,0:T(2,128)S(1)}, f32[1,2,2,128]{3,2,1,0:T(2,128)}, u32[]{:S(2)}) copy-start(f32[1,2,2,128]{3,2,1,0:T(2,128)} %param.242) | copy-start | bytes 6148
  137.9 24.9 %copy-start.11 = (f32[2,2,128]{2,1,0:T(2,128)S(1)}, f32[2,2,128]{2,1,0:T(2,128)}, u32[]{:S(2)}) copy-start(f32[2,2,128]{2,1,0:T(2,128)} %get-tuple-element.1708) | copy-start | bytes 6148
  147.5 5.6 collective-permute-start.6
  153.2 4.0 collective-permute-start.7
  157.3 5.5 collective-permute-start.8
  366.8 4.3 collective-permute-start.9
  371.2 3.9 collective-permute-start.10
  375.1 4.4 collective-permute-start.11
  388.5 5.6 collective-permute-start.12
  394.2 3.1 collective-permute-start.13
  397.3 5.5 collective-permute-start.14
  606.7 4.3 collective-permute-start.15
  611.0 3.4 collective-permute-start.16
  614.4 4.4 collective-permute-start.17
  627.9 5.6 collective-permute-start.18
  633.5 3.1 collective-permute-start.19
  636.6 5.5 collective-permute-start.20
  846.1 4.3 collective-permute-start.21
  850.5 3.4 collective-permute-start.22
  853.8 4.4 collective-permute-start.23
  867.3 5.6 collective-permute-start.24
  872.9 3.1 collective-permute-start.25
  876.0 5.5 collective-permute-start.26
  (7 other events, 20.8 us)
where the time goes:
time: 1100 us; the launch traced here: 1090 us
  blocking collectives  809 us (74%)
  starting transfers between devices  74.8 us (7%)
  local copies, waits for them, and re-layouts  63.4 us (6%)
  waiting for transfers between devices  50.2 us (5%)
  other arithmetic  47.5 us (4%)
  matrix products  39.8 us (4%)
    psum x4, blocking collectives, squares(): return lax.psum(inner(residual, residual), ('gx', 'gy', 'gz'))  402 us
    psum x3, blocking collectives, shards(): alpha = norm_now / lax.psum(inner(direction, image), ('gx', 'gy', 'gz'))  308 us
    psum x1, blocking collectives, shards(): totals = lax.psum(jnp.sum(solution, axis=(1, 2, 3, 4)), ('gx', 'gy', 'gz'))  99.6 us
    ppermute x27, starting transfers between devices, shifted(): return lax.ppermute(value, axis, pairs)  74.8 us
    ppermute x27, waiting for transfers between devices, shifted(): return lax.ppermute(value, axis, pairs)  50.2 us
    sub x13, other arithmetic, pair_tile(): offset[component] + place_j[..., component, None, :]  24.6 us
    dot_general x4, matrix products, operate(): jnp.einsum('kabcij,krabcj->krabci', tiles, from_j, precision=lax.Precisio...  22.4 us
  transfers between devices with their start and end apart: 27, of which 25 were waited for; matrix products, arithmetic and copies ran while one was open for 0% of the time, Pallas kernels for 0%

commit v1 on v0

v1 whole, which is shorter than its diff:
```python
import functools

import jax
import jax.numpy as jnp
from jax import lax
from jax.experimental import pallas as pl
from jax.experimental.pallas import tpu as pltpu
from jax.sharding import PartitionSpec as P

CODES = {
    (0, 0, 1): 0,
    (0, 1, -1): 1,
    (0, 1, 0): 2,
    (0, 1, 1): 3,
    (1, -1, -1): 4,
    (1, -1, 0): 5,
    (1, -1, 1): 6,
    (1, 0, -1): 7,
    (1, 0, 0): 8,
    (1, 0, 1): 9,
    (1, 1, -1): 10,
    (1, 1, 0): 11,
    (1, 1, 1): 12,
}
SHELL = [(x, y, z) for x in (-1, 0, 1) for y in (-1, 0, 1) for z in (-1, 0, 1)]

SHIFT = (220.0, 110.0, 145.0, 140.0)
SCALE = (60.0, 70.0, 70.0, 70.0)
BACK = (0.0, 0.7, 1.0, 1.0)
PAIRS = [(i, j) for i in range(4) for j in range(i, 5)]
VMEM = pl.BlockSpec(memory_space=pltpu.VMEM)
PARAMS = pltpu.CompilerParams(vmem_limit_bytes=24 * 1024 * 1024)


def cell_index(x, y, z):
    return (x * 4 + y) * 4 + z


OWN = [cell_index(1, 1 + y, 1 + z) for y in range(2) for z in range(2)]


def spread(row):
    return jnp.broadcast_to(row, (8, 128))


def reduce_rows(total_ref, image_ref):
    for field in range(8):
        block = total_ref[field * 16 : (field + 1) * 16].reshape(128, 128)
        image_ref[field : field + 1, :] = jnp.sum(block.T, axis=0, keepdims=True)


def next_basis(step, image, field, before, mask, hard):
    value = image * mask + hard * field
    value = (value - SHIFT[step] * field) * (1.0 / SCALE[step])
    if BACK[step]:
        value = value - BACK[step] * before
    return value


def tile_kernel(packed_ref, hard_ref, tiles_ref, field_ref, next_ref, aux_ref, rows, cols, amp, total, image):
    lane_row = lax.broadcasted_iota(jnp.int32, (1, 128), 1)
    for x in range(3):
        for y in range(4):
            for z in range(4):
                cell = cell_index(x, y, z)
                block = packed_ref[cell]
                for number, shift in enumerate((x - 1.0, y - 1.0, z - 1.0)):
                    rows[cell, number] = spread(block[number : number + 1] + shift)
                for number in range(3, 6):
                    rows[cell, number] = spread(block[number : number + 1])
    for own, cell in enumerate(OWN):
        y, z = 1 + own // 2, 1 + own % 2
        for number in range(4):
            column = jnp.broadcast_to(rows[cell, number, 0:1, :], (128, 128)).T
            cols[own, number] = column.reshape(16, 8, 128)
        for number, offset in enumerate(SHELL):
            if offset in CODES:
                source, code = cell, CODES[offset]
            elif offset == (0, 0, 0):
                source = None
            else:
                source = cell_index(1 + offset[0], y + offset[1], z + offset[2])
                code = CODES[tuple(-value for value in offset)]
            if source is None:
                amp[own * 27 + number] = jnp.full((8, 128), 1.44, jnp.float32)
            else:
                flag = packed_ref[source, 6:7, code : code + 1]
                amp[own * 27 + number] = jnp.broadcast_to(1.44 * flag, (8, 128))

    sub = lax.broadcasted_iota(jnp.int32, (8, 128), 0)
    lane = lax.broadcasted_iota(jnp.int32, (8, 128), 1)

    def body(index, carry):
        own = index // 16
        chunk = index - own * 16
        base = (own // 2) * 4 + own % 2
        xi, yi, zi, si = [cols[own, number, chunk] for number in range(4)]
        sums = [jnp.zeros((8, 128), jnp.float32) for _ in range(2)]
        for number, offset in enumerate(SHELL):
            cell = base + cell_index(1 + offset[0], 1 + offset[1], 1 + offset[2])
            dx = rows[cell, 0] - xi
            dy = rows[cell, 1] - yi
            dz = rows[cell, 2] - zi
            square = jnp.maximum(dx * dx + dy * dy + dz * dz, 1e-30)
            ratio = square * lax.rsqrt(square)
            fourth = square * square
            taper = 1.0 + fourth * (-35.0 + ratio * (84.0 + ratio * (-70.0 + 20.0 * ratio)))
            cube = square * ratio + rows[cell, 3] * si
            value = taper * jnp.exp2(jnp.log(cube) * (-1.0 / (3.0 * 0.6931471805599453)))
            value = value * amp[own * 27 + number]
            keep = square < 1.0
            if offset == (0, 0, 0):
                keep = keep & (sub + chunk * 8 != lane)
            value = jnp.where(keep, value, 0.0)
            tiles_ref[(own * 27 + number) * 16 + chunk] = value
            for system in range(2):
                sums[system] = sums[system] + value * rows[cell, 4 + system]
        for system in range(2):
            total[(system * 4 + own) * 16 + chunk] = sums[system]
        return carry

    lax.fori_loop(0, 64, body, 0)
    reduce_rows(total, image)
    for own, cell in enumerate(OWN):
        for system in range(2):
            row = system * 4 + own
            field_ref[row : row + 1] = packed_ref[cell, 4 + system : 5 + system]
            aux_ref[row : row + 1] = -packed_ref[cell, 5:6]
            aux_ref[8 + row : 9 + row] = hard_ref[own : own + 1] * -packed_ref[cell, 5:6]
    field = field_ref[...]
    next_ref[...] = next_basis(0, image[...], field, None, aux_ref[0:8], aux_ref[8:16])


def run_tiles(packed, hard):
    shape = functools.partial(jax.ShapeDtypeStruct, dtype=jnp.float32)
    return pl.pallas_call(
        tile_kernel,
        out_shape=(shape((108 * 16, 8, 128)), shape((8, 128)), shape((8, 128)), shape((16, 128))),
        in_specs=[VMEM, VMEM],
        out_specs=(VMEM, VMEM, VMEM, VMEM),
        scratch_shapes=[
            pltpu.VMEM((48, 6, 8, 128), jnp.float32),
            pltpu.VMEM((4, 4, 16, 8, 128), jnp.float32),
            pltpu.VMEM((108, 8, 128), jnp.float32),
            pltpu.VMEM((128, 8, 128), jnp.float32),
            pltpu.VMEM((8, 128), jnp.float32),
        ],
        compiler_params=PARAMS,
        name="tiles",
    )(packed, hard)


def gram_row(fields):
    entries = [fields[i] * fields[j] for i, j in PAIRS] + fields[:4]
    lane = lax.broadcasted_iota(jnp.int32, (1, 128), 1)
    row = jnp.zeros((1, 128), jnp.float32)
    for number, entry in enumerate(entries):
        for system in range(2):
            part = jnp.sum(entry[system * 4 : system * 4 + 4], axis=0, keepdims=True)
            part = jnp.sum(part, axis=1, keepdims=True)
            row = row + jnp.where(lane == 2 * number + system, part, 0.0)
    return row


def apply_kernel(step, last, tiles_ref, halo_ref, aux_ref, *refs):
    count = step + 1
    fields = [ref for ref in refs[:count]]
    next_ref = refs[count]
    rest = refs[count + 1 :]
    if last:
        gram_ref, rest = rest[0], rest[1:]
    rows, total, image = rest
    for system in range(2):
        for cell in range(48):
            rows[cell * 2 + system] = spread(halo_ref[system * 48 + cell : system * 48 + cell + 1])

    def body(index, carry):
        own = index // 4
        group = index - own * 4
        base = (own // 2) * 4 + own % 2
        sums = [[jnp.zeros((8, 128), jnp.float32) for _ in range(4)] for _ in range(2)]
        for number, offset in enumerate(SHELL):
            cell = base + cell_index(1 + offset[0], 1 + offset[1], 1 + offset[2])
            right = [rows[cell * 2 + system] for system in range(2)]
            for part in range(4):
                tile = tiles_ref[(own * 27 + number) * 16 + group * 4 + part]
                for system in range(2):
                    sums[system][part] = sums[system][part] + tile * right[system]
        for system in range(2):
            for part in range(4):
                total[(system * 4 + own) * 16 + group * 4 + part] = sums[system][part]
        return carry

    lax.fori_loop(0, 16, body, 0)
    reduce_rows(total, image)
    values = [field[...] for field in fields]
    new = next_basis(step, image[...], values[-1], values[-2], aux_ref[0:8], aux_ref[8:16])
    next_ref[...] = new
    if last:
        gram_ref[...] = gram_row(values + [new])


def run_apply(step, last, tiles, halo, aux, fields):
    shape = functools.partial(jax.ShapeDtypeStruct, dtype=jnp.float32)
    outs = (shape((8, 128)), shape((1, 128))) if last else (shape((8, 128)),)
    return pl.pallas_call(
        functools.partial(apply_kernel, step, last),
        out_shape=outs,
        in_specs=[VMEM] * (3 + len(fields)),
        out_specs=tuple(VMEM for _ in outs),
        scratch_shapes=[
            pltpu.VMEM((96, 8, 128), jnp.float32),
            pltpu.VMEM((128, 8, 128), jnp.float32),
            pltpu.VMEM((8, 128), jnp.float32),
        ],
        compiler_params=PARAMS,
        name=f"apply{step}",
    )(tiles, halo, aux, *fields)


def combine(coefs, fields):
    value = coefs[0] * fields[0]
    for coef, field in zip(coefs[1:], fields[1:]):
        value = value + coef * field
    return value


def finish_kernel(gram_ref, w0, w1, w2, w3, w4, charges_ref, residual_ref):
    fields = [ref[...] for ref in (w0, w1, w2, w3, w4)]
    summed = spread(jnp.sum(gram_ref[...], axis=0, keepdims=True))
    lane = lax.broadcasted_iota(jnp.int32, (8, 128), 1)
    system = lax.broadcasted_iota(jnp.int32, (8, 128), 0) // 4

    def entry(number):
        picked = jnp.where(lane == 2 * number + system, summed, 0.0)
        return jnp.broadcast_to(jnp.sum(picked, axis=1, keepdims=True), (8, 128))

    gram = {}
    for number, (i, j) in enumerate(PAIRS):
        gram[i, j] = gram[j, i] = entry(number)
    totals = [entry(len(PAIRS) + number) for number in range(4)]

    def dot(left, right):
        result = None
        for i, a in enumerate(left):
            part = None
            for j, b in enumerate(right):
                term = gram[i, j] * b
                part = term if part is None else part + term
            result = a * part if result is None else result + a * part
        return result

    def multiply(vector):
        size = len(vector)
        out = []
        for row in range(size + 1):
            value = None
            if row >= 1:
                value = SCALE[row - 1] * vector[row - 1]
            if row < size:
                term = SHIFT[row] * vector[row]
                value = term if value is None else value + term
            if row + 1 < size:
                value = value + SCALE[row + 1] * BACK[row + 1] * vector[row + 1]
            out.append(value)
        return out

    one = jnp.ones((8, 128), jnp.float32)
    residual = [one]
    direction = [one]
    answer = []
    norm_now = gram[0, 0]
    for step in range(4):
        image = multiply(direction)
        alpha = norm_now / dot(direction, image)
        answer = [
            alpha * d if k >= len(answer) else answer[k] + alpha * d for k, d in enumerate(direction)
        ]
        residual = [
            residual[k] - alpha * value if k < len(residual) else -alpha * value
            for k, value in enumerate(image)
        ]
        if step == 3:
            break
        norm_next = dot(residual, residual)
        ratio = norm_next / norm_now
        direction = [
            value + ratio * direction[k] if k < len(direction) else value
            for k, value in enumerate(residual)
        ]
        norm_now = norm_next
    residual_ref[...] = combine(residual, fields)
    solution = combine(answer, fields[:4])
    total = combine(answer, totals)
    charges_ref[...] = solution[0:4] - total[0:4] / total[4:8] * solution[4:8]


def run_finish(gathered, fields):
    shape = functools.partial(jax.ShapeDtypeStruct, dtype=jnp.float32)
    return pl.pallas_call(
        finish_kernel,
        out_shape=(shape((4, 128)), shape((8, 128))),
        in_specs=[VMEM] * 6,
        out_specs=(VMEM, VMEM),
        compiler_params=PARAMS,
        name="finish",
    )(gathered, *fields)


X = ("xa", "xb")


def swap(value):
    return lax.ppermute(value, "core", [(0, 1), (1, 0)])


def opposite(value, axes, count):
    pairs = []
    for place in range(count):
        pairs.append((place * 2, (place + 1) % count * 2))
        pairs.append((place * 2 + 1, (place - 1) % count * 2 + 1))
    return lax.ppermute(value, axes, pairs)


def opposite_last(value, axis, count):
    pairs = []
    for place in range(count):
        pairs.append((place, (place + 1) % count))
        pairs.append((count + place, count + (place - 1) % count))
    return lax.ppermute(value, ("core", axis), pairs)


def edge_swap(value, count):
    pairs = []
    for place in range(count):
        pairs.append((place * 2 + 1, (place + 1) % count * 2))
        pairs.append(((place + 1) % count * 2, place * 2 + 1))
    return lax.ppermute(value, ("yc", "core"), pairs)


def ordered(core, mine, other, axis):
    first = jnp.where(core == 0, mine, other)
    second = jnp.where(core == 0, other, mine)
    return first, second


def exchange(value, dim, core, sizes, form):
    count_x, count_y, count_z = sizes
    lead = (slice(None),) * dim
    sent = jnp.where(core == 0, value[lead + (slice(None), slice(0, 1))], value[lead + (slice(None), slice(1, 2))])
    edge = edge_swap(sent, count_y)
    low = jnp.concatenate([edge, value], axis=dim + 1)
    high = jnp.concatenate([value, edge], axis=dim + 1)
    three = jnp.where(core == 0, low, high)
    other = swap(three)
    first, second = ordered(core, three, other, dim + 1)
    six = jnp.concatenate([first, second], axis=dim + 1)
    arrived = opposite(six, X + ("core",), count_x)
    other = swap(arrived)
    first, second = ordered(core, arrived, other, dim)
    layers = jnp.concatenate([first, six, second], axis=dim)
    if form == "pair":
        sent = jnp.where(
            core == 0,
            layers[lead + (slice(None), slice(None), slice(1, 2))],
            layers[lead + (slice(None), slice(None), slice(0, 1))],
        )
        arrived = opposite_last(sent, "gz", count_z)
        other = swap(arrived)
        first, second = ordered(core, arrived, other, dim)
        block = jnp.concatenate([first, layers, second], axis=dim + 2)
        return jnp.where(
            core == 0,
            block[lead + (slice(None), slice(0, 4))],
            block[lead + (slice(None), slice(2, 6))],
        )
    own = jnp.where(
        core == 0,
        layers[lead + (slice(None), slice(0, 4))],
        layers[lead + (slice(None), slice(2, 6))],
    )
    every = spread_all(own, "gz", count_z)
    here = lax.axis_index("gz")
    below = lax.dynamic_index_in_dim(every, lax.rem(here + count_z - 1, count_z), 0, keepdims=False)
    above = lax.dynamic_index_in_dim(every, lax.rem(here + 1, count_z), 0, keepdims=False)
    return jnp.concatenate(
        [
            below[lead + (slice(None), slice(None), slice(1, 2))],
            own,
            above[lead + (slice(None), slice(None), slice(0, 1))],
        ],
        axis=dim + 2,
    )


def spread_all(value, axes, count):
    sent = jnp.broadcast_to(value[None], (count,) + value.shape)
    return lax.all_to_all(sent, axes, 0, 0)


def shards(frac_positions, shielding, hardness, electroneg, counts, neighbor_list):
    wide, narrow = lax.axis_size("xa"), lax.axis_size("xb")
    count_y, count_z = lax.axis_size("yc"), lax.axis_size("gz")
    sizes = (wide * narrow, count_y, count_z)
    core = lax.axis_index("core")
    masks = (lax.broadcasted_iota(jnp.int32, hardness.shape, 3) < counts[..., None]).astype(
        jnp.float32
    )
    codes = jnp.arange(13, dtype=jnp.int32)
    flags = jnp.any(neighbor_list[..., :, None] == codes, axis=-2).astype(jnp.float32)
    flag_row = jnp.pad(flags, ((0, 0), (0, 0), (0, 0), (0, 115)))
    screen = (shielding**-1.5) * (1000.0**-0.5)
    packed = jnp.concatenate(
        [
            frac_positions,
            screen[:, :, :, None],
            (-electroneg * masks)[:, :, :, None],
            -masks[:, :, :, None],
            flag_row[:, :, :, None],
            jnp.zeros_like(flag_row)[:, :, :, None],
        ],
        axis=3,
    )
    packed = exchange(packed, 0, core, sizes, "pair").reshape(48, 8, 128)
    tiles, w0, w1, aux = run_tiles(packed, hardness.reshape(4, 128))
    fields = [w0, w1]
    for step, form in ((1, "pair"), (2, "all"), (3, "all")):
        halo = exchange(fields[-1].reshape(2, 1, 2, 2, 128), 1, core, sizes, form)
        outs = run_apply(step, step == 3, tiles, halo.reshape(96, 128), aux, fields)
        fields.append(outs[0])
    gram = outs[1]
    gram = jnp.sum(spread_all(gram, ("yc", "core"), 2 * count_y), axis=0)
    gram = jnp.sum(spread_all(gram, "gz", count_z), axis=0)
    gram = jnp.sum(spread_all(gram, "xb", narrow), axis=0)
    gram = spread_all(gram, "xa", wide)
    charges, residual = run_finish(gram.reshape(wide, 128), fields)
    return charges.reshape(1, 2, 2, 128), residual.reshape(2, 1, 2, 2, 128)


def solution(mesh):
    count_x, count_y, count_z = mesh.devices.shape
    wide = 4 if count_x % 4 == 0 else 1
    mesh = jax.sharding.Mesh(
        mesh.devices.reshape(wide, count_x // wide, count_y // 2, 2, count_z),
        ("xa", "xb", "yc", "core", "gz"),
    )
    x, y = ("xa", "xb"), ("yc", "core")
    placed = (
        P(x, y, "gz", None, None),
        P(x, y, "gz", None),
        P(x, y, "gz", None),
        P(x, y, "gz", None),
        P(x, y, "gz"),
        P(x, y, "gz", None),
    )
    return jax.shard_map(
        shards,
        mesh=mesh,
        in_specs=placed,
        out_specs=(P(x, y, "gz", None), P(None, x, y, "gz", None)),
        check_vma=False,
    )
```

time: 1100 us -> 195 us (0.18)
  blocking collectives: 809 us -> 48.3 us
  local copies, waits for them, and re-layouts: 63.4 us -> 8.03 us
  other arithmetic: 47.5 us -> 3.97 us
  matrix products: 39.8 us -> 0 us
  waiting for transfers between devices: 50.2 us -> 32 us
  Pallas kernels: 0 us -> 17.2 us
    psum x8 -> x0, blocking collectives: 809 us -> none  [the longest x4 402 us: squares(): return lax.psum(inner(residual, residual), ('gx', 'gy', 'gz'))]
    all_to_all x0 -> x5, blocking collectives: none -> 48.3 us  [spread_all(): return lax.all_to_all(sent, axes, 0, 0)]
    dot_general x12 -> x0, matrix products: 39.8 us -> none  [the longest x4 22.4 us: operate(): jnp.einsum('kabcij,krabcj->krabci', tiles, from_j, precision=lax.Precisio...]
    sub x15 -> x0, other arithmetic: 25.2 us -> none  [the longest x13 24.6 us: pair_tile(): offset[component] + place_j[..., component, None, :]]
    ppermute x27 -> x20, waiting for transfers between devices: 50.2 us -> 27.4 us  [the longest x4 9.93 us: edge_swap(): return lax.ppermute(value, ('yc', 'core'), pairs)]
    mul x39 -> x0, local copies, waits for them, and re-layouts: 17.9 us -> none  [the longest x13 8.96 us: pair_tile(): jnp.where(ratio < 1.0, coulomb, 0.0) * mask_i[..., :, None]]
    pallas_call x0 -> x5, Pallas kernels: none -> 17.2 us  [the longest x1 10.3 us: run_tiles(): pl.pallas_call(tile_kernel, out_shape=(shape((108 * 16, 8, 128)), shape((...]
    ppermute x27 -> x20, starting transfers between devices: 74.8 us -> 78.3 us  [the longest x10 46.3 us: swap(): return lax.ppermute(value, 'core', [(0, 1), (1, 0)])]
  transfers between devices with their start and end apart: 27 -> 21, of which waited for: 25 -> 21; matrix products, arithmetic and copies ran while one was open for 0% -> 0% of each run, Pallas kernels for 0% -> 0%
where the time goes in v1:
time: 195 us; the launch traced here: 192 us
  starting transfers between devices  81.6 us (42%)
  blocking collectives  48.3 us (25%)
  waiting for transfers between devices  32 us (16%)
  Pallas kernels  17.2 us (9%)
  local copies, waits for them, and re-layouts  8.03 us (4%)
  other arithmetic  3.97 us (2%)
    all_to_all x5, blocking collectives, spread_all(): return lax.all_to_all(sent, axes, 0, 0)  48.3 us
    ppermute x10, starting transfers between devices, swap(): return lax.ppermute(value, 'core', [(0, 1), (1, 0)])  46.3 us
    ppermute x4, starting transfers between devices, opposite(): return lax.ppermute(value, axes, pairs)  13.7 us
    ppermute x4, starting transfers between devices, edge_swap(): return lax.ppermute(value, ('yc', 'core'), pairs)  10.7 us
    pallas_call x1, Pallas kernels, run_tiles(): pl.pallas_call(tile_kernel, out_shape=(shape((108 * 16, 8, 128)), shape((...  10.3 us
    ppermute x4, waiting for transfers between devices, edge_swap(): return lax.ppermute(value, ('yc', 'core'), pairs)  9.93 us
    ppermute x10, waiting for transfers between devices, swap(): return lax.ppermute(value, 'core', [(0, 1), (1, 0)])  8.24 us
    ppermute x2, starting transfers between devices, opposite_last(): return lax.ppermute(value, ('core', axis), pairs)  7.56 us
  transfers between devices with their start and end apart: 21, of which 21 were waited for; matrix products, arithmetic and copies ran while one was open for 0% of the time, Pallas kernels for 0%

profile of v1, /device:TPU:1, one launch (start us, length us, event | category | flops | bytes accessed | tf_op | source)
XLA Modules:
  0.0 192.1 jit_solution(11680162830958531328)
XLA Ops:
  4.4 4.6 %collective-permute-start = (f32[1,1,2,8,128]{4,2,3,1,0:T(2,128)S(1)}, f32[1,1,2,8,128]{4,2,3,1,0:T(2,128)S(1)}, u32[]{:S(2)}, u32[]{:S(2)}) collective-permute-start(f32[1,1,2,8,128]{4,2,3,1,0:T(2,128)S(1)} %slice_select_fusion.4), channel_id=1, source_target_pairs={{4,8},{8,4},{12,16},{16,12},{20,24},{24,20},{28,0},{0,28},{5,9},{9... | collective-permute-start | bytes 24584 | tf_op jit(solution)/shard_map/ppermute | solution.py:338
  10.3 9.0 %collective-permute-start.1 = (f32[1,3,2,8,128]{4,2,3,1,0:T(2,128)S(1)}, f32[1,3,2,8,128]{4,2,3,1,0:T(2,128)S(1)}, u32[]{:S(2)}, u32[]{:S(2)}) collective-permute-start(f32[1,3,2,8,128]{4,2,3,1,0:T(2,128)S(1)} %maximum_select_fusion), channel_id=1, source_target_pairs={{0,4},{4,0},{1,5},{5,1},{2,6},{6,2},{3,7},{7,3},{8,12},{12,8},{9,1... | collective-permute-start | bytes 73736 | tf_op jit(solution)/shard_map/ppermute | solution.py:314
  20.2 5.7 %collective-permute-start.2 = (f32[1,6,2,8,128]{4,2,3,1,0:T(2,128)S(1)}, f32[1,6,2,8,128]{4,2,3,1,0:T(2,128)S(1)}, u32[]{:S(2)}, u32[]{:S(2)}) collective-permute-start(f32[1,6,2,8,128]{4,2,3,1,0:T(2,128)S(1)} %pad_maximum_fusion.3), channel_id=1, source_target_pairs={{0,32},{4,484},{32,64},{36,4},{64,96},{68,36},{96,128},{100,68},{1... | collective-permute-start | bytes 147464 | tf_op jit(solution)/shard_map/ppermute | solution.py:322
  27.2 3.4 %collective-permute-start.3 = (f32[1,6,2,8,128]{4,2,3,1,0:T(2,128)S(1)}, f32[1,6,2,8,128]{4,2,3,1,0:T(2,128)S(1)}, u32[]{:S(2)}, u32[]{:S(2)}) collective-permute-start(f32[1,6,2,8,128]{4,2,3,1,0:T(2,128)S(1)} %collective-permute-done.2), channel_id=1, source_target_pairs={{0,4},{4,0},{1,5},{5,1},{2,6},{6,2},{3,7},{7,3},{8,12},{12,8},{9,1... | collective-permute-start | bytes 147464 | tf_op jit(solution)/shard_map/ppermute | solution.py:314
  31.6 4.4 %collective-permute-start.4 = (f32[3,6,1,8,128]{4,2,3,1,0:T(1,128)S(1)}, f32[3,6,1,8,128]{4,2,3,1,0:T(1,128)S(1)}, u32[]{:S(2)}, u32[]{:S(2)}) collective-permute-start(f32[3,6,1,8,128]{4,2,3,1,0:T(1,128)S(1)} %broadcast_select_fusion.2), channel_id=1, source_target_pairs={{0,1},{4,7},{1,2},{5,4},{2,3},{6,5},{3,0},{7,6},{8,9},{12,15},{9,1... | collective-permute-start | bytes 221192 | tf_op jit(solution)/shard_map/ppermute | solution.py:330
  37.4 3.9 %collective-permute-start.5 = (f32[3,6,1,8,128]{4,2,3,1,0:T(1,128)S(1)}, f32[3,6,1,8,128]{4,2,3,1,0:T(1,128)S(1)}, u32[]{:S(2)}, u32[]{:S(2)}) collective-permute-start(f32[3,6,1,8,128]{4,2,3,1,0:T(1,128)S(1)} %collective-permute-done.4), channel_id=1, source_target_pairs={{0,4},{4,0},{1,5},{5,1},{2,6},{6,2},{3,7},{7,3},{8,12},{12,8},{9,1... | collective-permute-start | bytes 221192 | tf_op jit(solution)/shard_map/ppermute | solution.py:314
  43.2 10.3 %tiles.1 = (f32[1728,8,128]{2,1,0:T(8,128)S(1)}, f32[8,128]{1,0:T(8,128)S(1)}, f32[8,128]{1,0:T(8,128)S(1)}, f32[16,128]{1,0:T(8,128)S(1)}) custom-call(f32[48,8,128]{2,1,0:T(8,128)S(1)} %bitcast.58, f32[4,128]{1,0:T(4,128)S(1)} %bitcast.72), custom_call_target="tpu_custom_call" | custom-call | tf_op jit(solution)/shard_map/tiles/pallas_call | solution.py:136
  53.5 2.2 %collective-permute-start.6 = (f32[2,1,1,2,128]{4,3,2,1,0:T(2,128)S(1)}, f32[2,1,1,2,128]{4,3,2,1,0:T(2,128)S(1)}, u32[]{:S(2)}, u32[]{:S(2)}) collective-permute-start(f32[2,1,1,2,128]{4,3,2,1,0:T(2,128)S(1)} %slice_select_fusion.7), channel_id=1, source_target_pairs={{4,8},{8,4},{12,16},{16,12},{20,24},{24,20},{28,0},{0,28},{5,9},{9... | collective-permute-start | bytes 6152 | tf_op jit(solution)/shard_map/ppermute | solution.py:338
  55.8 2.7 %collective-permute-done.6 = f32[2,1,1,2,128]{4,3,2,1,0:T(2,128)S(1)} collective-permute-done((f32[2,1,1,2,128]{4,3,2,1,0:T(2,128)S(1)}, f32[2,1,1,2,128]{4,3,2,1,0:T(2,128)S(1)}, u32[]{:S(2)}, u32[]{:S(2)}) %collective-permute-start.6) | collective-permute-done | bytes 2080 | tf_op jit(solution)/shard_map/ppermute | solution.py:338
  58.4 3.5 %collective-permute-start.7 = (f32[2,1,3,2,128]{4,3,2,1,0:T(2,128)S(1)}, f32[2,1,3,2,128]{4,3,2,1,0:T(2,128)S(1)}, u32[]{:S(2)}, u32[]{:S(2)}) collective-permute-start(f32[2,1,3,2,128]{4,3,2,1,0:T(2,128)S(1)} %maximum_select_fusion.1), channel_id=1, source_target_pairs={{0,4},{4,0},{1,5},{5,1},{2,6},{6,2},{3,7},{7,3},{8,12},{12,8},{9,1... | collective-permute-start | bytes 18440 | tf_op jit(solution)/shard_map/ppermute | solution.py:314
  62.7 3.6 %collective-permute-start.8 = (f32[2,1,6,2,128]{4,3,2,1,0:T(2,128)S(1)}, f32[2,1,6,2,128]{4,3,2,1,0:T(2,128)S(1)}, u32[]{:S(2)}, u32[]{:S(2)}) collective-permute-start(f32[2,1,6,2,128]{4,3,2,1,0:T(2,128)S(1)} %pad_maximum_fusion.9), channel_id=1, source_target_pairs={{0,32},{4,484},{32,64},{36,4},{64,96},{68,36},{96,128},{100,68},{1... | collective-permute-start | bytes 36872 | tf_op jit(solution)/shard_map/ppermute | solution.py:322
  67.2 4.6 %collective-permute-start.9 = (f32[2,1,6,2,128]{4,3,2,1,0:T(2,128)S(1)}, f32[2,1,6,2,128]{4,3,2,1,0:T(2,128)S(1)}, u32[]{:S(2)}, u32[]{:S(2)}) collective-permute-start(f32[2,1,6,2,128]{4,3,2,1,0:T(2,128)S(1)} %collective-permute-done.8), channel_id=1, source_target_pairs={{0,4},{4,0},{1,5},{5,1},{2,6},{6,2},{3,7},{7,3},{8,12},{12,8},{9,1... | collective-permute-start | bytes 36872 | tf_op jit(solution)/shard_map/ppermute | solution.py:314
  72.7 3.2 %collective-permute-start.10 = (f32[2,3,6,1,128]{4,3,2,1,0:T(1,128)S(1)}, f32[2,3,6,1,128]{4,3,2,1,0:T(1,128)S(1)}, u32[]{:S(2)}, u32[]{:S(2)}) collective-permute-start(f32[2,3,6,1,128]{4,3,2,1,0:T(1,128)S(1)} %broadcast_select_fusion.7), channel_id=1, source_target_pairs={{0,1},{4,7},{1,2},{5,4},{2,3},{6,5},{3,0},{7,6},{8,9},{12,15},{9,1... | collective-permute-start | bytes 55304 | tf_op jit(solution)/shard_map/ppermute | solution.py:330
  77.2 4.6 %collective-permute-start.11 = (f32[2,3,6,1,128]{4,3,2,1,0:T(1,128)S(1)}, f32[2,3,6,1,128]{4,3,2,1,0:T(1,128)S(1)}, u32[]{:S(2)}, u32[]{:S(2)}) collective-permute-start(f32[2,3,6,1,128]{4,3,2,1,0:T(1,128)S(1)} %collective-permute-done.10), channel_id=1, source_target_pairs={{0,4},{4,0},{1,5},{5,1},{2,6},{6,2},{3,7},{7,3},{8,12},{12,8},{9,1... | collective-permute-start | bytes 55304 | tf_op jit(solution)/shard_map/ppermute | solution.py:314
  84.7 2.9 %copy-done = f32[1728,8,128]{2,1,0:T(8,128)} copy-done((f32[1728,8,128]{2,1,0:T(8,128)}, f32[1728,8,128]{2,1,0:T(8,128)S(1)}, u32[]{:S(2)}) %copy-start) | copy-done | bytes 7077912
  89.5 3.0 %collective-permute-done.12 = f32[2,1,1,2,128]{4,3,2,1,0:T(2,128)S(1)} collective-permute-done((f32[2,1,1,2,128]{4,3,2,1,0:T(2,128)S(1)}, f32[2,1,1,2,128]{4,3,2,1,0:T(2,128)S(1)}, u32[]{:S(2)}, u32[]{:S(2)}) %collective-permute-start.12) | collective-permute-done | bytes 2080 | tf_op jit(solution)/shard_map/ppermute | solution.py:338
  92.5 3.5 %collective-permute-start.13 = (f32[2,1,3,2,128]{4,3,2,1,0:T(2,128)S(1)}, f32[2,1,3,2,128]{4,3,2,1,0:T(2,128)S(1)}, u32[]{:S(2)}, u32[]{:S(2)}) collective-permute-start(f32[2,1,3,2,128]{4,3,2,1,0:T(2,128)S(1)} %maximum_select_fusion.2), channel_id=1, source_target_pairs={{0,4},{4,0},{1,5},{5,1},{2,6},{6,2},{3,7},{7,3},{8,12},{12,8},{9,1... | collective-permute-start | bytes 18440 | tf_op jit(solution)/shard_map/ppermute | solution.py:314
  96.8 2.4 %collective-permute-start.14 = (f32[2,1,6,2,128]{4,3,2,1,0:T(2,128)S(1)}, f32[2,1,6,2,128]{4,3,2,1,0:T(2,128)S(1)}, u32[]{:S(2)}, u32[]{:S(2)}) collective-permute-start(f32[2,1,6,2,128]{4,3,2,1,0:T(2,128)S(1)} %pad_maximum_fusion.10), channel_id=1, source_target_pairs={{0,32},{4,484},{32,64},{36,4},{64,96},{68,36},{96,128},{100,68},{1... | collective-permute-start | bytes 36872 | tf_op jit(solution)/shard_map/ppermute | solution.py:322
  101.2 4.6 %collective-permute-start.15 = (f32[2,1,6,2,128]{4,3,2,1,0:T(2,128)S(1)}, f32[2,1,6,2,128]{4,3,2,1,0:T(2,128)S(1)}, u32[]{:S(2)}, u32[]{:S(2)}) collective-permute-start(f32[2,1,6,2,128]{4,3,2,1,0:T(2,128)S(1)} %collective-permute-done.14), channel_id=1, source_target_pairs={{0,4},{4,0},{1,5},{5,1},{2,6},{6,2},{3,7},{7,3},{8,12},{12,8},{9,1... | collective-permute-start | bytes 36872 | tf_op jit(solution)/shard_map/ppermute | solution.py:314
  107.4 3.3 %all-to-all-start = ((f32[4,2,3,4,2,128]{5,4,3,2,1,0:T(2,128)}), f32[4,2,3,4,2,128]{5,4,3,2,1,0:T(2,128)S(1)}, u32[]{:S(2)}, u32[]{:S(2)}) async-start(f32[4,2,3,4,2,128]{5,4,3,2,1,0:T(2,128)} %broadcast_in_dim.27), calls=%async_computation | async-start | bytes 196608 | tf_op jit(solution)/shard_map/all_to_all | solution.py:398
  110.7 4.6 %all-to-all-done = f32[4,2,3,4,2,128]{5,4,3,2,1,0:T(2,128)S(1)} async-done(((f32[4,2,3,4,2,128]{5,4,3,2,1,0:T(2,128)}), f32[4,2,3,4,2,128]{5,4,3,2,1,0:T(2,128)S(1)}, u32[]{:S(2)}, u32[]{:S(2)}) %all-to-all-start) | async-done | bytes 98336 | tf_op jit(solution)/shard_map/all_to_all | solution.py:398
  115.4 3.0 %copy-done.1 = f32[1728,8,128]{2,1,0:T(8,128)S(1)} copy-done((f32[1728,8,128]{2,1,0:T(8,128)S(1)}, f32[1728,8,128]{2,1,0:T(8,128)}, u32[]{:S(2)}) %copy-start.1) | copy-done | bytes 7077912
  122.3 3.0 %collective-permute-done.16 = f32[2,1,1,2,128]{4,3,2,1,0:T(2,128)S(1)} collective-permute-done((f32[2,1,1,2,128]{4,3,2,1,0:T(2,128)S(1)}, f32[2,1,1,2,128]{4,3,2,1,0:T(2,128)S(1)}, u32[]{:S(2)}, u32[]{:S(2)}) %collective-permute-start.16) | collective-permute-done | bytes 2080 | tf_op jit(solution)/shard_map/ppermute | solution.py:338
  125.3 4.6 %collective-permute-start.17 = (f32[2,1,3,2,128]{4,3,2,1,0:T(2,128)S(1)}, f32[2,1,3,2,128]{4,3,2,1,0:T(2,128)S(1)}, u32[]{:S(2)}, u32[]{:S(2)}) collective-permute-start(f32[2,1,3,2,128]{4,3,2,1,0:T(2,128)S(1)} %maximum_select_fusion.3), channel_id=1, source_target_pairs={{0,4},{4,0},{1,5},{5,1},{2,6},{6,2},{3,7},{7,3},{8,12},{12,8},{9,1... | collective-permute-start | bytes 18440 | tf_op jit(solution)/shard_map/ppermute | solution.py:314
  132.7 2.5 %collective-permute-done.18 = f32[2,1,6,2,128]{4,3,2,1,0:T(2,128)S(1)} collective-permute-done((f32[2,1,6,2,128]{4,3,2,1,0:T(2,128)S(1)}, f32[2,1,6,2,128]{4,3,2,1,0:T(2,128)S(1)}, u32[]{:S(2)}, u32[]{:S(2)}) %collective-permute-start.18) | collective-permute-done | bytes 12320 | tf_op jit(solution)/shard_map/ppermute | solution.py:322
  135.2 4.6 %collective-permute-start.19 = (f32[2,1,6,2,128]{4,3,2,1,0:T(2,128)S(1)}, f32[2,1,6,2,128]{4,3,2,1,0:T(2,128)S(1)}, u32[]{:S(2)}, u32[]{:S(2)}) collective-permute-start(f32[2,1,6,2,128]{4,3,2,1,0:T(2,128)S(1)} %collective-permute-done.18), channel_id=1, source_target_pairs={{0,4},{4,0},{1,5},{5,1},{2,6},{6,2},{3,7},{7,3},{8,12},{12,8},{9,1... | collective-permute-start | bytes 36872 | tf_op jit(solution)/shard_map/ppermute | solution.py:314
  140.7 7.0 %all_to_all.30 = f32[4,2,3,4,2,128]{5,4,3,2,1,0:T(2,128)S(1)} all-to-all(f32[4,2,3,4,2,128]{5,4,3,2,1,0:T(2,128)S(1)} %broadcast_in_dim.28), channel_id=1, replica_groups=mesh['xa'=4,'xb'=4,'yc'=4,'core'=2,'gz'=4] {'gz'}, dimensions={0} | all-to-all | bytes 196608 | tf_op jit(solution)/shard_map/all_to_all | solution.py:398
  147.8 2.1 %apply3.1 = (f32[8,128]{1,0:T(8,128)S(1)}, f32[1,128]{1,0:T(1,128)S(1)}) custom-call(f32[1728,8,128]{2,1,0:T(8,128)S(1)} %copy-done.1, f32[96,128]{1,0:T(8,128)S(1)} %bitcast.65, f32[16,128]{1,0:T(8,128)S(1)} %get-tuple-element.12.aux_ref, f32[8,128]{1,0:T(8,128)S(1)} %get-tuple-element.13.refs_0_.w0, f32[8,128]{1,0:T(8,128)S(1)} %get-tuple-element.11.refs_1_.w1, ...), custom_call_target="tpu_custom_call" | custom-call | tf_op jit(solution)/shard_map/apply3/pallas_call | solution.py:206
  150.0 8.4 %all_to_all.31 = f32[8,1,128]{2,1,0:T(1,128)S(1)} all-to-all(f32[8,1,128]{2,1,0:T(1,128)S(1)} %broadcast_in_dim.30), channel_id=1, replica_groups=mesh['xa'=4,'xb'=4,'yc'=4,'core'=2,'gz'=4] {'yc','core'}, dimensions={0} | all-to-all | bytes 8192 | tf_op jit(solution)/shard_map/all_to_all | solution.py:398
  158.4 6.4 %all_to_all.32 = f32[4,1,128]{2,1,0:T(1,128)S(1)} all-to-all(f32[4,1,128]{2,1,0:T(1,128)S(1)} %broadcast_in_dim.62), channel_id=1, replica_groups=mesh['xa'=4,'xb'=4,'yc'=4,'core'=2,'gz'=4] {'gz'}, dimensions={0} | all-to-all | bytes 4096 | tf_op jit(solution)/shard_map/all_to_all | solution.py:398
  164.9 6.7 %all_to_all.33 = f32[4,1,128]{2,1,0:T(1,128)S(1)} all-to-all(f32[4,1,128]{2,1,0:T(1,128)S(1)} %broadcast_in_dim.63), channel_id=1, replica_groups=mesh['xa'=4,'xb'=4,'yc'=4,'core'=2,'gz'=4] {'xb'}, dimensions={0} | all-to-all | bytes 4096 | tf_op jit(solution)/shard_map/all_to_all | solution.py:398
  171.6 19.7 %all_to_all.34 = f32[4,1,128]{2,1,0:T(1,128)S(1)} all-to-all(f32[4,1,128]{2,1,0:T(1,128)S(1)} %broadcast_in_dim.64), channel_id=1, replica_groups=mesh['xa'=4,'xb'=4,'yc'=4,'core'=2,'gz'=4] {'xa'}, dimensions={0} | all-to-all | bytes 4096 | tf_op jit(solution)/shard_map/all_to_all | solution.py:398
  (85 shorter events, 32.9 us)
Async XLA Ops:
  4.4 5.9 %collective-permute-start = (f32[1,1,2,8,128]{4,2,3,1,0:T(2,128)S(1)}, f32[1,1,2,8,128]{4,2,3,1,0:T(2,128)S(1)}, u32[]{:S(2)}, u32[]{:S(2)}) collective-permute-start(f32[1,1,2,8,128]{4,2,3,1,0:T(2,128)S(1)} %slice_select_fusion.4), channel_id=1, source_target_pairs={{4,8},{8,4},{12,16},{16,12},{20,24},{24,20},{28,0},{0,28},{5,9},{9... | collective-permute-start | bytes 24584 | tf_op jit(solution)/shard_map/ppermute | solution.py:338
  10.3 9.9 %collective-permute-start.1 = (f32[1,3,2,8,128]{4,2,3,1,0:T(2,128)S(1)}, f32[1,3,2,8,128]{4,2,3,1,0:T(2,128)S(1)}, u32[]{:S(2)}, u32[]{:S(2)}) collective-permute-start(f32[1,3,2,8,128]{4,2,3,1,0:T(2,128)S(1)} %maximum_select_fusion), channel_id=1, source_target_pairs={{0,4},{4,0},{1,5},{5,1},{2,6},{6,2},{3,7},{7,3},{8,12},{12,8},{9,1... | collective-permute-start | bytes 73736 | tf_op jit(solution)/shard_map/ppermute | solution.py:314
  20.2 6.9 %collective-permute-start.2 = (f32[1,6,2,8,128]{4,2,3,1,0:T(2,128)S(1)}, f32[1,6,2,8,128]{4,2,3,1,0:T(2,128)S(1)}, u32[]{:S(2)}, u32[]{:S(2)}) collective-permute-start(f32[1,6,2,8,128]{4,2,3,1,0:T(2,128)S(1)} %pad_maximum_fusion.3), channel_id=1, source_target_pairs={{0,32},{4,484},{32,64},{36,4},{64,96},{68,36},{96,128},{100,68},{1... | collective-permute-start | bytes 147464 | tf_op jit(solution)/shard_map/ppermute | solution.py:322
  27.2 4.3 %collective-permute-start.3 = (f32[1,6,2,8,128]{4,2,3,1,0:T(2,128)S(1)}, f32[1,6,2,8,128]{4,2,3,1,0:T(2,128)S(1)}, u32[]{:S(2)}, u32[]{:S(2)}) collective-permute-start(f32[1,6,2,8,128]{4,2,3,1,0:T(2,128)S(1)} %collective-permute-done.2), channel_id=1, source_target_pairs={{0,4},{4,0},{1,5},{5,1},{2,6},{6,2},{3,7},{7,3},{8,12},{12,8},{9,1... | collective-permute-start | bytes 147464 | tf_op jit(solution)/shard_map/ppermute | solution.py:314
  31.6 5.8 %collective-permute-start.4 = (f32[3,6,1,8,128]{4,2,3,1,0:T(1,128)S(1)}, f32[3,6,1,8,128]{4,2,3,1,0:T(1,128)S(1)}, u32[]{:S(2)}, u32[]{:S(2)}) collective-permute-start(f32[3,6,1,8,128]{4,2,3,1,0:T(1,128)S(1)} %broadcast_select_fusion.2), channel_id=1, source_target_pairs={{0,1},{4,7},{1,2},{5,4},{2,3},{6,5},{3,0},{7,6},{8,9},{12,15},{9,1... | collective-permute-start | bytes 221192 | tf_op jit(solution)/shard_map/ppermute | solution.py:330
  37.4 4.8 %collective-permute-start.5 = (f32[3,6,1,8,128]{4,2,3,1,0:T(1,128)S(1)}, f32[3,6,1,8,128]{4,2,3,1,0:T(1,128)S(1)}, u32[]{:S(2)}, u32[]{:S(2)}) collective-permute-start(f32[3,6,1,8,128]{4,2,3,1,0:T(1,128)S(1)} %collective-permute-done.4), channel_id=1, source_target_pairs={{0,4},{4,0},{1,5},{5,1},{2,6},{6,2},{3,7},{7,3},{8,12},{12,8},{9,1... | collective-permute-start | bytes 221192 | tf_op jit(solution)/shard_map/ppermute | solution.py:314
  42.5 0.7 copy-start.2
  53.5 4.9 %collective-permute-start.6 = (f32[2,1,1,2,128]{4,3,2,1,0:T(2,128)S(1)}, f32[2,1,1,2,128]{4,3,2,1,0:T(2,128)S(1)}, u32[]{:S(2)}, u32[]{:S(2)}) collective-permute-start(f32[2,1,1,2,128]{4,3,2,1,0:T(2,128)S(1)} %slice_select_fusion.7), channel_id=1, source_target_pairs={{4,8},{8,4},{12,16},{16,12},{20,24},{24,20},{28,0},{0,28},{5,9},{9... | collective-permute-start | bytes 6152 | tf_op jit(solution)/shard_map/ppermute | solution.py:338
  58.4 4.3 %collective-permute-start.7 = (f32[2,1,3,2,128]{4,3,2,1,0:T(2,128)S(1)}, f32[2,1,3,2,128]{4,3,2,1,0:T(2,128)S(1)}, u32[]{:S(2)}, u32[]{:S(2)}) collective-permute-start(f32[2,1,3,2,128]{4,3,2,1,0:T(2,128)S(1)} %maximum_select_fusion.1), channel_id=1, source_target_pairs={{0,4},{4,0},{1,5},{5,1},{2,6},{6,2},{3,7},{7,3},{8,12},{12,8},{9,1... | collective-permute-start | bytes 18440 | tf_op jit(solution)/shard_map/ppermute | solution.py:314
  62.7 4.5 %collective-permute-start.8 = (f32[2,1,6,2,128]{4,3,2,1,0:T(2,128)S(1)}, f32[2,1,6,2,128]{4,3,2,1,0:T(2,128)S(1)}, u32[]{:S(2)}, u32[]{:S(2)}) collective-permute-start(f32[2,1,6,2,128]{4,3,2,1,0:T(2,128)S(1)} %pad_maximum_fusion.9), channel_id=1, source_target_pairs={{0,32},{4,484},{32,64},{36,4},{64,96},{68,36},{96,128},{100,68},{1... | collective-permute-start | bytes 36872 | tf_op jit(solution)/shard_map/ppermute | solution.py:322
  67.2 5.4 %collective-permute-start.9 = (f32[2,1,6,2,128]{4,3,2,1,0:T(2,128)S(1)}, f32[2,1,6,2,128]{4,3,2,1,0:T(2,128)S(1)}, u32[]{:S(2)}, u32[]{:S(2)}) collective-permute-start(f32[2,1,6,2,128]{4,3,2,1,0:T(2,128)S(1)} %collective-permute-done.8), channel_id=1, source_target_pairs={{0,4},{4,0},{1,5},{5,1},{2,6},{6,2},{3,7},{7,3},{8,12},{12,8},{9,1... | collective-permute-start | bytes 36872 | tf_op jit(solution)/shard_map/ppermute | solution.py:314
  72.7 4.5 %collective-permute-start.10 = (f32[2,3,6,1,128]{4,3,2,1,0:T(1,128)S(1)}, f32[2,3,6,1,128]{4,3,2,1,0:T(1,128)S(1)}, u32[]{:S(2)}, u32[]{:S(2)}) collective-permute-start(f32[2,3,6,1,128]{4,3,2,1,0:T(1,128)S(1)} %broadcast_select_fusion.7), channel_id=1, source_target_pairs={{0,1},{4,7},{1,2},{5,4},{2,3},{6,5},{3,0},{7,6},{8,9},{12,15},{9,1... | collective-permute-start | bytes 55304 | tf_op jit(solution)/shard_map/ppermute | solution.py:330
  77.2 5.4 %collective-permute-start.11 = (f32[2,3,6,1,128]{4,3,2,1,0:T(1,128)S(1)}, f32[2,3,6,1,128]{4,3,2,1,0:T(1,128)S(1)}, u32[]{:S(2)}, u32[]{:S(2)}) collective-permute-start(f32[2,3,6,1,128]{4,3,2,1,0:T(1,128)S(1)} %collective-permute-done.10), channel_id=1, source_target_pairs={{0,4},{4,0},{1,5},{5,1},{2,6},{6,2},{3,7},{7,3},{8,12},{12,8},{9,1... | collective-permute-start | bytes 55304 | tf_op jit(solution)/shard_map/ppermute | solution.py:314
  84.7 2.9 %copy-start = (f32[1728,8,128]{2,1,0:T(8,128)}, f32[1728,8,128]{2,1,0:T(8,128)S(1)}, u32[]{:S(2)}) copy-start(f32[1728,8,128]{2,1,0:T(8,128)S(1)} %get-tuple-element.10.tiles_ref) | copy-start | bytes 21233668
  87.6 4.9 %collective-permute-start.12 = (f32[2,1,1,2,128]{4,3,2,1,0:T(2,128)S(1)}, f32[2,1,1,2,128]{4,3,2,1,0:T(2,128)S(1)}, u32[]{:S(2)}, u32[]{:S(2)}) collective-permute-start(f32[2,1,1,2,128]{4,3,2,1,0:T(2,128)S(1)} %slice_select_fusion.6), channel_id=1, source_target_pairs={{4,8},{8,4},{12,16},{16,12},{20,24},{24,20},{28,0},{0,28},{5,9},{9... | collective-permute-start | bytes 6152 | tf_op jit(solution)/shard_map/ppermute | solution.py:338
  92.5 4.3 %collective-permute-start.13 = (f32[2,1,3,2,128]{4,3,2,1,0:T(2,128)S(1)}, f32[2,1,3,2,128]{4,3,2,1,0:T(2,128)S(1)}, u32[]{:S(2)}, u32[]{:S(2)}) collective-permute-start(f32[2,1,3,2,128]{4,3,2,1,0:T(2,128)S(1)} %maximum_select_fusion.2), channel_id=1, source_target_pairs={{0,4},{4,0},{1,5},{5,1},{2,6},{6,2},{3,7},{7,3},{8,12},{12,8},{9,1... | collective-permute-start | bytes 18440 | tf_op jit(solution)/shard_map/ppermute | solution.py:314
  96.8 4.4 %collective-permute-start.14 = (f32[2,1,6,2,128]{4,3,2,1,0:T(2,128)S(1)}, f32[2,1,6,2,128]{4,3,2,1,0:T(2,128)S(1)}, u32[]{:S(2)}, u32[]{:S(2)}) collective-permute-start(f32[2,1,6,2,128]{4,3,2,1,0:T(2,128)S(1)} %pad_maximum_fusion.10), channel_id=1, source_target_pairs={{0,32},{4,484},{32,64},{36,4},{64,96},{68,36},{96,128},{100,68},{1... | collective-permute-start | bytes 36872 | tf_op jit(solution)/shard_map/ppermute | solution.py:322
  101.2 5.4 %collective-permute-start.15 = (f32[2,1,6,2,128]{4,3,2,1,0:T(2,128)S(1)}, f32[2,1,6,2,128]{4,3,2,1,0:T(2,128)S(1)}, u32[]{:S(2)}, u32[]{:S(2)}) collective-permute-start(f32[2,1,6,2,128]{4,3,2,1,0:T(2,128)S(1)} %collective-permute-done.14), channel_id=1, source_target_pairs={{0,4},{4,0},{1,5},{5,1},{2,6},{6,2},{3,7},{7,3},{8,12},{12,8},{9,1... | collective-permute-start | bytes 36872 | tf_op jit(solution)/shard_map/ppermute | solution.py:314
  107.4 7.9 %all-to-all-start = ((f32[4,2,3,4,2,128]{5,4,3,2,1,0:T(2,128)}), f32[4,2,3,4,2,128]{5,4,3,2,1,0:T(2,128)S(1)}, u32[]{:S(2)}, u32[]{:S(2)}) async-start(f32[4,2,3,4,2,128]{5,4,3,2,1,0:T(2,128)} %broadcast_in_dim.27), calls=%async_computation | async-start | bytes 196608 | tf_op jit(solution)/shard_map/all_to_all | solution.py:398
  115.4 3.0 %copy-start.1 = (f32[1728,8,128]{2,1,0:T(8,128)S(1)}, f32[1728,8,128]{2,1,0:T(8,128)}, u32[]{:S(2)}) copy-start(f32[1728,8,128]{2,1,0:T(8,128)} %copy-done) | copy-start | bytes 21233668
  120.4 4.9 %collective-permute-start.16 = (f32[2,1,1,2,128]{4,3,2,1,0:T(2,128)S(1)}, f32[2,1,1,2,128]{4,3,2,1,0:T(2,128)S(1)}, u32[]{:S(2)}, u32[]{:S(2)}) collective-permute-start(f32[2,1,1,2,128]{4,3,2,1,0:T(2,128)S(1)} %slice_select_fusion.5), channel_id=1, source_target_pairs={{4,8},{8,4},{12,16},{16,12},{20,24},{24,20},{28,0},{0,28},{5,9},{9... | collective-permute-start | bytes 6152 | tf_op jit(solution)/shard_map/ppermute | solution.py:338
  125.3 5.4 %collective-permute-start.17 = (f32[2,1,3,2,128]{4,3,2,1,0:T(2,128)S(1)}, f32[2,1,3,2,128]{4,3,2,1,0:T(2,128)S(1)}, u32[]{:S(2)}, u32[]{:S(2)}) collective-permute-start(f32[2,1,3,2,128]{4,3,2,1,0:T(2,128)S(1)} %maximum_select_fusion.3), channel_id=1, source_target_pairs={{0,4},{4,0},{1,5},{5,1},{2,6},{6,2},{3,7},{7,3},{8,12},{12,8},{9,1... | collective-permute-start | bytes 18440 | tf_op jit(solution)/shard_map/ppermute | solution.py:314
  130.8 4.4 %collective-permute-start.18 = (f32[2,1,6,2,128]{4,3,2,1,0:T(2,128)S(1)}, f32[2,1,6,2,128]{4,3,2,1,0:T(2,128)S(1)}, u32[]{:S(2)}, u32[]{:S(2)}) collective-permute-start(f32[2,1,6,2,128]{4,3,2,1,0:T(2,128)S(1)} %pad_maximum_fusion.11), channel_id=1, source_target_pairs={{0,32},{4,484},{32,64},{36,4},{64,96},{68,36},{96,128},{100,68},{1... | collective-permute-start | bytes 36872 | tf_op jit(solution)/shard_map/ppermute | solution.py:322
  135.2 5.4 %collective-permute-start.19 = (f32[2,1,6,2,128]{4,3,2,1,0:T(2,128)S(1)}, f32[2,1,6,2,128]{4,3,2,1,0:T(2,128)S(1)}, u32[]{:S(2)}, u32[]{:S(2)}) collective-permute-start(f32[2,1,6,2,128]{4,3,2,1,0:T(2,128)S(1)} %collective-permute-done.18), channel_id=1, source_target_pairs={{0,4},{4,0},{1,5},{5,1},{2,6},{6,2},{3,7},{7,3},{8,12},{12,8},{9,1... | collective-permute-start | bytes 36872 | tf_op jit(solution)/shard_map/ppermute | solution.py:314

commit v2 on v1

v2 whole, which is shorter than its diff:
```python
import functools

import jax
import jax.numpy as jnp
from jax import lax
from jax.experimental import pallas as pl
from jax.experimental.pallas import tpu as pltpu
from jax.sharding import PartitionSpec as P

CODES = {
    (0, 0, 1): 0,
    (0, 1, -1): 1,
    (0, 1, 0): 2,
    (0, 1, 1): 3,
    (1, -1, -1): 4,
    (1, -1, 0): 5,
    (1, -1, 1): 6,
    (1, 0, -1): 7,
    (1, 0, 0): 8,
    (1, 0, 1): 9,
    (1, 1, -1): 10,
    (1, 1, 0): 11,
    (1, 1, 1): 12,
}
SHELL = [(x, y, z) for x in (-1, 0, 1) for y in (-1, 0, 1) for z in (-1, 0, 1)]

SHIFT = (220.0, 110.0, 145.0, 140.0)
SCALE = (60.0, 70.0, 70.0, 70.0)
BACK = (0.0, 0.7, 1.0, 1.0)
PAIRS = [(i, j) for i in range(4) for j in range(i, 5)]
VMEM = pl.BlockSpec(memory_space=pltpu.VMEM)
PARAMS = pltpu.CompilerParams(vmem_limit_bytes=24 * 1024 * 1024)


OWN = [(1 + y) * 4 + 1 + z for y in range(2) for z in range(2)]
SAME = [offset for offset in SHELL if offset[0] == 0]
SIDE = [offset for offset in SHELL if offset[0] != 0]


def spread(row):
    return jnp.broadcast_to(row, (8, 128))


def reduce_rows(total_ref, image_ref):
    for field in range(8):
        block = total_ref[field * 16 : (field + 1) * 16].reshape(128, 128)
        image_ref[field : field + 1, :] = jnp.sum(block.T, axis=0, keepdims=True)


def next_basis(step, image, field, before, mask, hard):
    value = image * mask + hard * field
    value = (value - SHIFT[step] * field) * (1.0 / SCALE[step])
    if BACK[step]:
        value = value - BACK[step] * before
    return value


def pack_kernel(*refs):
    sources, packed_ref, inputs, semaphores = refs[:6], refs[6], refs[7:13], refs[13]
    copies = [
        pltpu.make_async_copy(source, target, semaphores.at[number])
        for number, (source, target) in enumerate(zip(sources, inputs))
    ]
    for copy in copies:
        copy.start()
    for copy in copies:
        copy.wait()
    place_ref, shield_ref, hard_ref, electro_ref, count_ref, list_ref = inputs
    lane = lax.broadcasted_iota(jnp.int32, (1, 128), 1)
    for y in range(2):
        for z in range(2):
            cell = 2 * y + z
            count = jnp.broadcast_to(count_ref[0, y : y + 1, z : z + 1], (1, 128))
            mask = jnp.where(lane < count, 1.0, 0.0)
            flags = jnp.zeros((1, 128), jnp.float32)
            for number in range(13):
                code = jnp.broadcast_to(list_ref[0, y, z : z + 1, number : number + 1], (1, 128))
                flags = jnp.where(lane == code, 1.0, flags)
            for number in range(3):
                packed_ref[cell, number : number + 1] = place_ref[0, y, number, z : z + 1]
            shield = shield_ref[0, y, z : z + 1]
            packed_ref[cell, 3:4] = jnp.exp(-1.5 * jnp.log(shield)) * (1000.0**-0.5)
            packed_ref[cell, 4:5] = -electro_ref[0, y, z : z + 1] * mask
            packed_ref[cell, 5:6] = -mask
            packed_ref[cell, 6:7] = flags
            packed_ref[cell, 7:8] = hard_ref[0, y, z : z + 1]


def run_pack(*inputs):
    return pl.pallas_call(
        pack_kernel,
        out_shape=jax.ShapeDtypeStruct((4, 8, 128), jnp.float32),
        in_specs=[pl.BlockSpec(memory_space=pltpu.HBM)] * 6,
        out_specs=VMEM,
        scratch_shapes=[pltpu.VMEM(value.shape, value.dtype) for value in inputs]
        + [pltpu.SemaphoreType.DMA((6,))],
        compiler_params=pltpu.CompilerParams(vmem_limit_bytes=63 * 1024 * 1024),
        name="pack",
    )(*inputs)


def fill_rows(packed_ref, rows, first, layer):
    for y in range(4):
        for z in range(4):
            cell = y * 4 + z
            block = packed_ref[cell]
            for number, shift in enumerate((float(layer), y - 1.0, z - 1.0)):
                rows[first + cell, number] = spread(block[number : number + 1] + shift)
            for number in range(3, 6):
                rows[first + cell, number] = spread(block[number : number + 1])


def neighbor(offset):
    layer = 1 if offset[0] == 1 else 0
    return layer * 16 + (1 + offset[1]) * 4 + 1 + offset[2]


def fill_away(offsets, own_ref, lower_ref, rows, away):
    for own, cell in enumerate(OWN):
        y, z = own // 2, own % 2
        for number, offset in enumerate(offsets):
            row = rows[neighbor(offset) + y * 4 + z, 0]
            if offset in CODES:
                flag = own_ref[cell, 6:7, CODES[offset] : CODES[offset] + 1]
            elif offset == (0, 0, 0):
                flag = None
            else:
                code = CODES[tuple(-value for value in offset)]
                flag = lower_ref[cell + offset[1] * 4 + offset[2], 6:7, code : code + 1]
            if flag is not None:
                row = row + jnp.broadcast_to((1.0 - flag) * 100.0, (8, 128))
            away[own * len(offsets) + number] = row


def build_tiles(offsets, rows, cols, away, tiles_ref, before, total):
    sub = lax.broadcasted_iota(jnp.int32, (8, 128), 0)
    lane = lax.broadcasted_iota(jnp.int32, (8, 128), 1)
    size = len(offsets)

    def body(index, carry):
        own = index // 16
        chunk = index - own * 16
        base = (own // 2) * 4 + own % 2
        xi, yi, zi, si = [cols[(own * 4 + number) * 16 + chunk] for number in range(4)]
        if before is None:
            sums = [jnp.zeros((8, 128), jnp.float32) for _ in range(2)]
        else:
            sums = [before[(system * 4 + own) * 16 + chunk] for system in range(2)]
        for number, offset in enumerate(offsets):
            cell = base + neighbor(offset)
            dx = away[own * size + number] - xi
            dy = rows[cell, 1] - yi
            dz = rows[cell, 2] - zi
            square = jnp.maximum(dx * dx + dy * dy + dz * dz, 1e-30)
            ratio = square * lax.rsqrt(square)
            fourth = square * square
            taper = 1.44 + fourth * (-50.4 + ratio * (120.96 + ratio * (-100.8 + 28.8 * ratio)))
            cube = square * ratio + rows[cell, 3] * si
            value = taper * jnp.exp2(jnp.log(cube) * (-1.0 / (3.0 * 0.6931471805599453)))
            keep = square < 1.0
            if offset == (0, 0, 0):
                keep = keep & (sub + chunk * 8 != lane)
            value = jnp.where(keep, value, 0.0)
            tiles_ref[(own * size + number) * 16 + chunk] = value
            for system in range(2):
                sums[system] = sums[system] + value * rows[cell, 4 + system]
        for system in range(2):
            total[(system * 4 + own) * 16 + chunk] = sums[system]
        return carry

    lax.fori_loop(0, 64, body, 0)


def same_kernel(own_ref, tiles_ref, cols_ref, total_ref, field_ref, aux_ref, rows, away):
    fill_rows(own_ref, rows, 0, 0)
    for own, cell in enumerate(OWN):
        for number in range(4):
            column = jnp.broadcast_to(rows[cell, number, 0:1, :], (128, 128)).T
            start = (own * 4 + number) * 16
            cols_ref[start : start + 16] = column.reshape(16, 8, 128)
        for system in range(2):
            row = system * 4 + own
            mask = -own_ref[cell, 5:6]
            field_ref[row : row + 1] = own_ref[cell, 4 + system : 5 + system]
            aux_ref[row : row + 1] = mask
            aux_ref[8 + row : 9 + row] = own_ref[cell, 7:8] * mask
    fill_away(SAME, own_ref, own_ref, rows, away)
    build_tiles(SAME, rows, cols_ref, away, tiles_ref, None, total_ref)


def side_kernel(own_ref, lower_ref, upper_ref, cols_ref, before_ref, field_ref, aux_ref, tiles_ref, next_ref, rows, away, total, image):
    fill_rows(lower_ref, rows, 0, -1)
    fill_rows(upper_ref, rows, 16, 1)
    fill_away(SIDE, own_ref, lower_ref, rows, away)
    build_tiles(SIDE, rows, cols_ref, away, tiles_ref, before_ref, total)
    reduce_rows(total, image)
    next_ref[...] = next_basis(0, image[...], field_ref[...], None, aux_ref[0:8], aux_ref[8:16])


SHAPE = functools.partial(jax.ShapeDtypeStruct, dtype=jnp.float32)


def cost(flops):
    return pl.CostEstimate(flops=flops, bytes_accessed=4 * 1024 * 1024, transcendentals=0)


def run_same(own):
    return pl.pallas_call(
        same_kernel,
        out_shape=(
            SHAPE((36 * 16, 8, 128)),
            SHAPE((256, 8, 128)),
            SHAPE((128, 8, 128)),
            SHAPE((8, 128)),
            SHAPE((16, 128)),
        ),
        in_specs=[VMEM],
        out_specs=(VMEM,) * 5,
        scratch_shapes=[
            pltpu.VMEM((16, 6, 8, 128), jnp.float32),
            pltpu.VMEM((36, 8, 128), jnp.float32),
        ],
        compiler_params=PARAMS,
        cost_estimate=cost(40 * 36 * 16384),
        name="tiles_same",
    )(own)


def run_side(*inputs):
    return pl.pallas_call(
        side_kernel,
        out_shape=(SHAPE((72 * 16, 8, 128)), SHAPE((8, 128))),
        in_specs=[VMEM] * 7,
        out_specs=(VMEM,) * 2,
        scratch_shapes=[
            pltpu.VMEM((32, 6, 8, 128), jnp.float32),
            pltpu.VMEM((72, 8, 128), jnp.float32),
            pltpu.VMEM((128, 8, 128), jnp.float32),
            pltpu.VMEM((8, 128), jnp.float32),
        ],
        compiler_params=PARAMS,
        cost_estimate=cost(40 * 72 * 16384),
        name="tiles_side",
    )(*inputs)


def gram_row(fields):
    entries = [fields[i] * fields[j] for i, j in PAIRS] + fields[:4]
    lane = lax.broadcasted_iota(jnp.int32, (1, 128), 1)
    row = jnp.zeros((1, 128), jnp.float32)
    for number, entry in enumerate(entries):
        for system in range(2):
            part = jnp.sum(entry[system * 4 : system * 4 + 4], axis=0, keepdims=True)
            part = jnp.sum(part, axis=1, keepdims=True)
            row = row + jnp.where(lane == 2 * number + system, part, 0.0)
    return row


def fill_fields(halo_ref, rows, first):
    for system in range(2):
        for cell in range(16):
            row = system * 16 + cell
            rows[(first + cell) * 2 + system] = spread(halo_ref[row : row + 1])


def apply_tiles(offsets, tiles_ref, rows, before, total):
    size = len(offsets)

    def body(index, carry):
        own = index // 4
        group = index - own * 4
        base = (own // 2) * 4 + own % 2
        places = [[(system * 4 + own) * 16 + group * 4 + part for part in range(4)] for system in range(2)]
        if before is None:
            sums = [[jnp.zeros((8, 128), jnp.float32) for _ in range(4)] for _ in range(2)]
        else:
            sums = [[before[place] for place in line] for line in places]
        for number, offset in enumerate(offsets):
            cell = base + neighbor(offset)
            right = [rows[cell * 2 + system] for system in range(2)]
            for part in range(4):
                tile = tiles_ref[(own * size + number) * 16 + group * 4 + part]
                for system in range(2):
                    sums[system][part] = sums[system][part] + tile * right[system]
        for system in range(2):
            for part in range(4):
                total[places[system][part]] = sums[system][part]
        return carry

    lax.fori_loop(0, 16, body, 0)


def apply_same_kernel(tiles_ref, halo_ref, total_ref, rows):
    fill_fields(halo_ref, rows, 0)
    apply_tiles(SAME, tiles_ref, rows, None, total_ref)


def apply_side_kernel(step, last, tiles_ref, lower_ref, upper_ref, before_ref, aux_ref, *refs):
    count = step + 1
    fields, next_ref, rest = refs[:count], refs[count], refs[count + 1 :]
    if last:
        gram_ref, rest = rest[0], rest[1:]
    rows, total, image = rest
    fill_fields(lower_ref, rows, 0)
    fill_fields(upper_ref, rows, 16)
    apply_tiles(SIDE, tiles_ref, rows, before_ref, total)
    reduce_rows(total, image)
    values = [field[...] for field in fields]
    new = next_basis(step, image[...], values[-1], values[-2], aux_ref[0:8], aux_ref[8:16])
    next_ref[...] = new
    if last:
        gram_ref[...] = gram_row(values + [new])


def run_apply_same(tiles, halo):
    return pl.pallas_call(
        apply_same_kernel,
        out_shape=SHAPE((128, 8, 128)),
        in_specs=[VMEM] * 2,
        out_specs=VMEM,
        scratch_shapes=[pltpu.VMEM((32, 8, 128), jnp.float32)],
        compiler_params=PARAMS,
        cost_estimate=cost(4 * 36 * 16384),
        name="apply_same",
    )(tiles, halo)


def run_apply_side(step, last, tiles, lower, upper, before, aux, fields):
    outs = (SHAPE((8, 128)), SHAPE((1, 128))) if last else (SHAPE((8, 128)),)
    return pl.pallas_call(
        functools.partial(apply_side_kernel, step, last),
        out_shape=outs,
        in_specs=[VMEM] * (5 + len(fields)),
        out_specs=tuple(VMEM for _ in outs),
        scratch_shapes=[
            pltpu.VMEM((64, 8, 128), jnp.float32),
            pltpu.VMEM((128, 8, 128), jnp.float32),
            pltpu.VMEM((8, 128), jnp.float32),
        ],
        compiler_params=PARAMS,
        cost_estimate=cost(4 * 72 * 16384),
        name=f"apply_side{step}",
    )(tiles, lower, upper, before, aux, *fields)


def combine(coefs, fields):
    value = coefs[0] * fields[0]
    for coef, field in zip(coefs[1:], fields[1:]):
        value = value + coef * field
    return value


def finish_kernel(gram_ref, w0, w1, w2, w3, w4, charges_ref, residual_ref):
    fields = [ref[...] for ref in (w0, w1, w2, w3, w4)]
    summed = spread(jnp.sum(gram_ref[...], axis=0, keepdims=True))
    lane = lax.broadcasted_iota(jnp.int32, (8, 128), 1)
    system = lax.broadcasted_iota(jnp.int32, (8, 128), 0) // 4

    def entry(number):
        picked = jnp.where(lane == 2 * number + system, summed, 0.0)
        return jnp.broadcast_to(jnp.sum(picked, axis=1, keepdims=True), (8, 128))

    gram = {}
    for number, (i, j) in enumerate(PAIRS):
        gram[i, j] = gram[j, i] = entry(number)
    totals = [entry(len(PAIRS) + number) for number in range(4)]

    def dot(left, right):
        result = None
        for i, a in enumerate(left):
            part = None
            for j, b in enumerate(right):
                term = gram[i, j] * b
                part = term if part is None else part + term
            result = a * part if result is None else result + a * part
        return result

    def multiply(vector):
        size = len(vector)
        out = []
        for row in range(size + 1):
            value = None
            if row >= 1:
                value = SCALE[row - 1] * vector[row - 1]
            if row < size:
                term = SHIFT[row] * vector[row]
                value = term if value is None else value + term
            if row + 1 < size:
                value = value + SCALE[row + 1] * BACK[row + 1] * vector[row + 1]
            out.append(value)
        return out

    one = jnp.ones((8, 128), jnp.float32)
    residual = [one]
    direction = [one]
    answer = []
    norm_now = gram[0, 0]
    for step in range(4):
        image = multiply(direction)
        alpha = norm_now / dot(direction, image)
        answer = [
            alpha * d if k >= len(answer) else answer[k] + alpha * d for k, d in enumerate(direction)
        ]
        residual = [
            residual[k] - alpha * value if k < len(residual) else -alpha * value
            for k, value in enumerate(image)
        ]
        if step == 3:
            break
        norm_next = dot(residual, residual)
        ratio = norm_next / norm_now
        direction = [
            value + ratio * direction[k] if k < len(direction) else value
            for k, value in enumerate(residual)
        ]
        norm_now = norm_next
    value = combine(residual, fields)
    solution = combine(answer, fields[:4])
    total = combine(answer, totals)
    charges = solution[0:4] - total[0:4] / total[4:8] * solution[4:8]
    for y in range(2):
        charges_ref[0, y] = charges[2 * y : 2 * y + 2]
        for system in range(2):
            row = system * 4 + 2 * y
            residual_ref[system, 0, y] = value[row : row + 2]


def run_finish(gathered, fields):
    shape = functools.partial(jax.ShapeDtypeStruct, dtype=jnp.float32)
    return pl.pallas_call(
        finish_kernel,
        out_shape=(shape((1, 2, 2, 128)), shape((2, 1, 2, 2, 128))),
        in_specs=[VMEM] * 6,
        out_specs=(VMEM, VMEM),
        compiler_params=PARAMS,
        name="finish",
    )(gathered, *fields)


def shifted(value, axis, steps):
    count = lax.axis_size(axis)
    pairs = [(source, (source + steps) % count) for source in range(count)]
    return lax.ppermute(value, axis, pairs)


def spread_all(value, axes, count):
    sent = jnp.broadcast_to(value[None], (count,) + value.shape)
    return lax.all_to_all(sent, axes, 0, 0)


def around(every, axis, group, cells):
    count = lax.axis_size(axis)
    here = lax.axis_index(axis)

    def part(place):
        return lax.dynamic_index_in_dim(every, place, group, keepdims=False)

    cells = cells - 1
    below = lax.slice_in_dim(part(lax.rem(here + count - 1, count)), 1, 2, axis=cells)
    above = lax.slice_in_dim(part(lax.rem(here + 1, count)), 0, 1, axis=cells)
    return jnp.concatenate([below, part(here), above], axis=cells)


def exchange(value, dim):
    count_y, count_z = lax.axis_size("gy"), lax.axis_size("gz")
    every = spread_all(value, ("gy", "gz"), count_y * count_z)
    every = every.reshape((count_y, count_z) + value.shape)
    block = around(every, "gy", 0, 2 + dim)
    block = around(block, "gz", 0, 2 + dim)
    return block, shifted(block, "gx", 1), shifted(block, "gx", -1)


def shards(frac_positions, shielding, hardness, electroneg, counts, neighbor_list):
    count_x, count_y, count_z = [lax.axis_size(axis) for axis in ("gx", "gy", "gz")]
    places = frac_positions.transpose(0, 1, 3, 2, 4)
    packed = run_pack(places, shielding, hardness, electroneg, counts, neighbor_list)
    layers = exchange(packed.reshape(2, 2, 8, 128), 0)
    own, lower, upper = [layer.reshape(16, 8, 128) for layer in layers]
    tiles_same, cols, total, w0, aux = run_same(own)
    tiles_side, w1 = run_side(own, lower, upper, cols, total, w0, aux)
    fields = [w0, w1]
    for step in (1, 2, 3):
        layers = exchange(fields[-1].reshape(2, 2, 2, 128), 1)
        own, lower, upper = [layer.reshape(32, 128) for layer in layers]
        total = run_apply_same(tiles_same, own)
        outs = run_apply_side(step, step == 3, tiles_side, lower, upper, total, aux, fields)
        fields.append(outs[0])
    gram = outs[1]
    gram = jnp.sum(spread_all(gram, ("gy", "gz"), count_y * count_z), axis=0)
    gram = spread_all(gram, "gx", count_x)
    return run_finish(gram.reshape(count_x, 128), fields)


def solution(mesh):
    placed = (
        P("gx", "gy", "gz", None, None),
        P("gx", "gy", "gz", None),
        P("gx", "gy", "gz", None),
        P("gx", "gy", "gz", None),
        P("gx", "gy", "gz"),
        P("gx", "gy", "gz", None),
    )
    return jax.shard_map(
        shards,
        mesh=mesh,
        in_specs=placed,
        out_specs=(P("gx", "gy", "gz", None), P(None, "gx", "gy", "gz", None)),
        check_vma=False,
    )
```

time: 195 us -> 147 us (0.75)
  starting transfers between devices: 81.6 us -> 38.1 us
  blocking collectives: 48.3 us -> 66.8 us
  waiting for transfers between devices: 32 us -> 17.9 us
  local copies, waits for them, and re-layouts: 8.03 us -> 1.88 us
  other arithmetic: 3.97 us -> 0.14 us
  Pallas kernels: 17.2 us -> 20 us
    ppermute x20 -> x8, starting transfers between devices: 78.3 us -> 27.7 us  [shifted(): return lax.ppermute(value, axis, pairs)]
    ppermute x20 -> x8, waiting for transfers between devices: 27.4 us -> 6.48 us  [shifted(): return lax.ppermute(value, axis, pairs)]
    all_to_all x5, blocking collectives: 48.3 us -> 66.8 us  [spread_all(): return lax.all_to_all(sent, axes, 0, 0)]
    unnamed x7 -> x0, local copies, waits for them, and re-layouts: 7.24 us -> none
    all_to_all x1, starting transfers between devices: 3.3 us -> 10.4 us  [spread_all(): return lax.all_to_all(sent, axes, 0, 0)]
    all_to_all x1, waiting for transfers between devices: 4.6 us -> 11.4 us  [spread_all(): return lax.all_to_all(sent, axes, 0, 0)]
    pallas_call x5 -> x10, Pallas kernels: 17.2 us -> 20 us  [the longest x1 7.15 us: run_side(): pl.pallas_call(side_kernel, out_shape=(SHAPE((72 * 16, 8, 128)), SHAPE((8...]
    unnamed x4 -> x0, other arithmetic: 2.24 us -> none
  transfers between devices with their start and end apart: 21 -> 9, of which waited for: 21 -> 4; matrix products, arithmetic and copies ran while one was open for 0% -> 0% of each run, Pallas kernels for 0% -> 4%
where the time goes in v2:
time: 147 us; the launch traced here: 146 us
  blocking collectives  66.8 us (45%)
  starting transfers between devices  38.1 us (26%)
  Pallas kernels  20 us (14%)
  waiting for transfers between devices  17.9 us (12%)
  local copies, waits for them, and re-layouts  1.88 us (1%)
    all_to_all x5, blocking collectives, spread_all(): return lax.all_to_all(sent, axes, 0, 0)  66.8 us
    ppermute x8, starting transfers between devices, shifted(): return lax.ppermute(value, axis, pairs)  27.7 us
    all_to_all x1, waiting for transfers between devices, spread_all(): return lax.all_to_all(sent, axes, 0, 0)  11.4 us
    all_to_all x1, starting transfers between devices, spread_all(): return lax.all_to_all(sent, axes, 0, 0)  10.4 us
    pallas_call x1, Pallas kernels, run_side(): pl.pallas_call(side_kernel, out_shape=(SHAPE((72 * 16, 8, 128)), SHAPE((8...  7.15 us
    ppermute x8, waiting for transfers between devices, shifted(): return lax.ppermute(value, axis, pairs)  6.48 us
    pallas_call x1, Pallas kernels, run_same(): pl.pallas_call(same_kernel, out_shape=(SHAPE((36 * 16, 8, 128)), SHAPE((2...  4.63 us
    pallas_call x3, Pallas kernels, run_apply_side(): pl.pallas_call(functools.partial(apply_side_kernel, step, last), out_shap...  3.99 us
  transfers between devices with their start and end apart: 9, of which 4 were waited for; matrix products, arithmetic and copies ran while one was open for 0% of the time, Pallas kernels for 4%

profile of v2, /device:TPU:1, one launch (start us, length us, event | category | flops | bytes accessed | tf_op | source)
XLA Modules:
  0.0 146.0 jit_solution(12391120798789079698)
XLA Ops:
  0.6 1.6 %pack.1 = f32[4,8,128]{2,1,0:T(8,128)} custom-call(f32[1,2,3,2,128]{4,3,2,1,0:T(2,128)} %bitcast.96, f32[1,2,2,128]{3,2,1,0:T(2,128)} %refs_1_.1, f32[1,2,2,128]{3,2,1,0:T(2,128)} %refs_2_.1, f32[1,2,2,128]{3,2,1,0:T(2,128)} %refs_3_.1, s32[1,2,2]{2,1,0:T(2,128)} %refs_4_.1, s32[1,2,2,13]{3,2,1,0:T(2,128)} %refs_5_.1), custom_call_target="tpu_custom_call" | custom-call | tf_op jit(solution)/shard_map/pack/pallas_call | solution.py:90
  2.2 1.6 %broadcast_in_dim.43 = f32[32,2,2,8,128]{4,3,2,1,0:T(8,128)} broadcast(f32[2,2,8,128]{3,2,1,0:T(8,128)} %bitcast.94), dimensions={1,2,3,4} | broadcast | bytes 540672 | tf_op jit(solution)/shard_map/broadcast_in_dim | solution.py:447
  3.8 10.4 %all-to-all-start = ((f32[32,2,2,8,128]{4,3,2,1,0:T(8,128)}), f32[32,2,2,8,128]{4,3,2,1,0:T(8,128)S(1)}, u32[]{:S(2)}, u32[]{:S(2)}) async-start(f32[32,2,2,8,128]{4,3,2,1,0:T(8,128)} %broadcast_in_dim.43), calls=%async_computation | async-start | bytes 1048576 | tf_op jit(solution)/shard_map/all_to_all | solution.py:448
  14.3 11.4 %all-to-all-done = f32[32,2,2,8,128]{4,3,2,1,0:T(8,128)S(1)} async-done(((f32[32,2,2,8,128]{4,3,2,1,0:T(8,128)}), f32[32,2,2,8,128]{4,3,2,1,0:T(8,128)S(1)}, u32[]{:S(2)}, u32[]{:S(2)}) %all-to-all-start) | async-done | bytes 524320 | tf_op jit(solution)/shard_map/all_to_all | solution.py:448
  25.8 9.2 %collective-permute-start.1 = (f32[4,4,8,128]{3,2,1,0:T(8,128)S(1)}, f32[4,4,8,128]{3,2,1,0:T(8,128)S(1)}, u32[]{:S(2)}, u32[]{:S(2)}) collective-permute-start(f32[4,4,8,128]{3,2,1,0:T(8,128)S(1)} %pad_maximum_fusion.1), channel_id=1, source_target_pairs={{0,480},{32,0},{64,32},{96,64},{128,96},{160,128},{192,160},{224,1... | collective-permute-start | bytes 196616 | tf_op jit(solution)/shard_map/ppermute | solution.py:443
  35.0 1.9 %collective-permute-start = (f32[4,4,8,128]{3,2,1,0:T(8,128)S(1)}, f32[4,4,8,128]{3,2,1,0:T(8,128)S(1)}, u32[]{:S(2)}, u32[]{:S(2)}) collective-permute-start(f32[4,4,8,128]{3,2,1,0:T(8,128)S(1)} %pad_maximum_fusion.1), channel_id=1, source_target_pairs={{0,32},{32,64},{64,96},{96,128},{128,160},{160,192},{192,224},{224... | collective-permute-start | bytes 196616 | tf_op jit(solution)/shard_map/ppermute | solution.py:443
  37.0 4.6 %tiles_same.1 = (f32[576,8,128]{2,1,0:T(8,128)S(1)}, f32[256,8,128]{2,1,0:T(8,128)S(1)}, f32[128,8,128]{2,1,0:T(8,128)S(1)}, f32[8,128]{1,0:T(8,128)S(1)}, f32[16,128]{1,0:T(8,128)S(1)}) custom-call(f32[16,8,128]{2,1,0:T(8,128)S(1)} %bitcast.72), custom_call_target="tpu_custom_call" | custom-call | flops 23592960 | bytes 4194304 | tf_op jit(solution)/shard_map/tiles_same/pallas_call | solution.py:208
  41.6 0.0 collective-permute-done.1
  41.6 7.2 %tiles_side.1 = (f32[1152,8,128]{2,1,0:T(8,128)S(1)}, f32[8,128]{1,0:T(8,128)S(1)}) custom-call(f32[16,8,128]{2,1,0:T(8,128)S(1)} %bitcast.73, f32[16,8,128]{2,1,0:T(8,128)S(1)} %bitcast.77, f32[16,8,128]{2,1,0:T(8,128)S(1)} %bitcast.76, f32[256,8,128]{2,1,0:T(8,128)S(1)} %get-tuple-element.11.cols_ref, f32[128,8,128]{2,1,0:T(8,128)S(1)} %get-tuple-element.12.before_ref, ...), custom_call_target="tpu_custom_call" | custom-call | flops 47185920 | bytes 4194304 | tf_op jit(solution)/shard_map/tiles_side/pallas_call | solution.py:230
  48.8 12.8 %all_to_all.30 = f32[32,2,2,2,128]{4,3,2,1,0:T(2,128)S(1)} all-to-all(f32[32,2,2,2,128]{4,3,2,1,0:T(2,128)S(1)} %broadcast_in_dim.45), channel_id=1, replica_groups=mesh['gx'=16,'gy'=8,'gz'=4] {'gy','gz'}, dimensions={0} | all-to-all | bytes 262144 | tf_op jit(solution)/shard_map/all_to_all | solution.py:448
  61.8 4.1 %collective-permute-start.3 = (f32[2,4,4,128]{3,2,1,0:T(4,128)S(1)}, f32[2,4,4,128]{3,2,1,0:T(4,128)S(1)}, u32[]{:S(2)}, u32[]{:S(2)}) collective-permute-start(f32[2,4,4,128]{3,2,1,0:T(4,128)S(1)} %pad_maximum_fusion.5), channel_id=1, source_target_pairs={{0,480},{32,0},{64,32},{96,64},{128,96},{160,128},{192,160},{224,1... | collective-permute-start | bytes 49160 | tf_op jit(solution)/shard_map/ppermute | solution.py:443
  65.9 1.9 %collective-permute-start.2 = (f32[2,4,4,128]{3,2,1,0:T(4,128)S(1)}, f32[2,4,4,128]{3,2,1,0:T(4,128)S(1)}, u32[]{:S(2)}, u32[]{:S(2)}) collective-permute-start(f32[2,4,4,128]{3,2,1,0:T(4,128)S(1)} %pad_maximum_fusion.5), channel_id=1, source_target_pairs={{0,32},{32,64},{64,96},{96,128},{128,160},{160,192},{192,224},{224... | collective-permute-start | bytes 49160 | tf_op jit(solution)/shard_map/ppermute | solution.py:443
  67.8 0.6 apply_same.3.before_ref
  68.4 3.1 %collective-permute-done.2 = f32[2,4,4,128]{3,2,1,0:T(4,128)S(1)} collective-permute-done((f32[2,4,4,128]{3,2,1,0:T(4,128)S(1)}, f32[2,4,4,128]{3,2,1,0:T(4,128)S(1)}, u32[]{:S(2)}, u32[]{:S(2)}) %collective-permute-start.2) | collective-permute-done | bytes 16416 | tf_op jit(solution)/shard_map/ppermute | solution.py:443
  71.5 1.3 apply_side1.1.refs_2_.w2
  72.9 12.9 %all_to_all.31 = f32[32,2,2,2,128]{4,3,2,1,0:T(2,128)S(1)} all-to-all(f32[32,2,2,2,128]{4,3,2,1,0:T(2,128)S(1)} %broadcast_in_dim.47), channel_id=1, replica_groups=mesh['gx'=16,'gy'=8,'gz'=4] {'gy','gz'}, dimensions={0} | all-to-all | bytes 262144 | tf_op jit(solution)/shard_map/all_to_all | solution.py:448
  85.9 1.9 %collective-permute-start.5 = (f32[2,4,4,128]{3,2,1,0:T(4,128)S(1)}, f32[2,4,4,128]{3,2,1,0:T(4,128)S(1)}, u32[]{:S(2)}, u32[]{:S(2)}) collective-permute-start(f32[2,4,4,128]{3,2,1,0:T(4,128)S(1)} %pad_maximum_fusion.6), channel_id=1, source_target_pairs={{0,480},{32,0},{64,32},{96,64},{128,96},{160,128},{192,160},{224,1... | collective-permute-start | bytes 49160 | tf_op jit(solution)/shard_map/ppermute | solution.py:443
  87.8 3.4 %collective-permute-start.4 = (f32[2,4,4,128]{3,2,1,0:T(4,128)S(1)}, f32[2,4,4,128]{3,2,1,0:T(4,128)S(1)}, u32[]{:S(2)}, u32[]{:S(2)}) collective-permute-start(f32[2,4,4,128]{3,2,1,0:T(4,128)S(1)} %pad_maximum_fusion.6), channel_id=1, source_target_pairs={{0,32},{32,64},{64,96},{96,128},{128,160},{160,192},{192,224},{224... | collective-permute-start | bytes 49160 | tf_op jit(solution)/shard_map/ppermute | solution.py:443
  91.2 0.6 apply_same.4.before_ref
  91.8 0.0 collective-permute-done.5
  91.8 1.7 %collective-permute-done.4 = f32[2,4,4,128]{3,2,1,0:T(4,128)S(1)} collective-permute-done((f32[2,4,4,128]{3,2,1,0:T(4,128)S(1)}, f32[2,4,4,128]{3,2,1,0:T(4,128)S(1)}, u32[]{:S(2)}, u32[]{:S(2)}) %collective-permute-start.4) | collective-permute-done | bytes 16416 | tf_op jit(solution)/shard_map/ppermute | solution.py:443
  93.5 1.3 apply_side2.1.refs_3_.w3
  94.9 12.6 %all_to_all.32 = f32[32,2,2,2,128]{4,3,2,1,0:T(2,128)S(1)} all-to-all(f32[32,2,2,2,128]{4,3,2,1,0:T(2,128)S(1)} %broadcast_in_dim.49), channel_id=1, replica_groups=mesh['gx'=16,'gy'=8,'gz'=4] {'gy','gz'}, dimensions={0} | all-to-all | bytes 262144 | tf_op jit(solution)/shard_map/all_to_all | solution.py:448
  107.6 1.9 %collective-permute-start.7 = (f32[2,4,4,128]{3,2,1,0:T(4,128)S(1)}, f32[2,4,4,128]{3,2,1,0:T(4,128)S(1)}, u32[]{:S(2)}, u32[]{:S(2)}) collective-permute-start(f32[2,4,4,128]{3,2,1,0:T(4,128)S(1)} %pad_maximum_fusion.7), channel_id=1, source_target_pairs={{0,480},{32,0},{64,32},{96,64},{128,96},{160,128},{192,160},{224,1... | collective-permute-start | bytes 49160 | tf_op jit(solution)/shard_map/ppermute | solution.py:443
  109.5 3.4 %collective-permute-start.6 = (f32[2,4,4,128]{3,2,1,0:T(4,128)S(1)}, f32[2,4,4,128]{3,2,1,0:T(4,128)S(1)}, u32[]{:S(2)}, u32[]{:S(2)}) collective-permute-start(f32[2,4,4,128]{3,2,1,0:T(4,128)S(1)} %pad_maximum_fusion.7), channel_id=1, source_target_pairs={{0,32},{32,64},{64,96},{96,128},{128,160},{160,192},{192,224},{224... | collective-permute-start | bytes 49160 | tf_op jit(solution)/shard_map/ppermute | solution.py:443
  112.9 0.6 apply_same.5.before_ref
  113.5 0.0 collective-permute-done.7
  113.5 1.7 %collective-permute-done.6 = f32[2,4,4,128]{3,2,1,0:T(4,128)S(1)} collective-permute-done((f32[2,4,4,128]{3,2,1,0:T(4,128)S(1)}, f32[2,4,4,128]{3,2,1,0:T(4,128)S(1)}, u32[]{:S(2)}, u32[]{:S(2)}) %collective-permute-start.6) | collective-permute-done | bytes 16416 | tf_op jit(solution)/shard_map/ppermute | solution.py:443
  115.2 1.4 apply_side3.1
  116.6 11.9 %all_to_all.33 = f32[32,1,128]{2,1,0:T(1,128)S(1)} all-to-all(f32[32,1,128]{2,1,0:T(1,128)S(1)} %broadcast_in_dim.51), channel_id=1, replica_groups=mesh['gx'=16,'gy'=8,'gz'=4] {'gy','gz'}, dimensions={0} | all-to-all | bytes 32768 | tf_op jit(solution)/shard_map/all_to_all | solution.py:448
  128.6 16.6 %all_to_all.34 = f32[16,1,128]{2,1,0:T(1,128)S(1)} all-to-all(f32[16,1,128]{2,1,0:T(1,128)S(1)} %broadcast_in_dim.52), channel_id=1, replica_groups=mesh['gx'=16,'gy'=8,'gz'=4] {'gx'}, dimensions={0} | all-to-all | bytes 16384 | tf_op jit(solution)/shard_map/all_to_all | solution.py:448
  145.2 0.8 finish.1
  (40 shorter events, 0.4 us)
Async XLA Ops:
  3.8 21.9 %all-to-all-start = ((f32[32,2,2,8,128]{4,3,2,1,0:T(8,128)}), f32[32,2,2,8,128]{4,3,2,1,0:T(8,128)S(1)}, u32[]{:S(2)}, u32[]{:S(2)}) async-start(f32[32,2,2,8,128]{4,3,2,1,0:T(8,128)} %broadcast_in_dim.43), calls=%async_computation | async-start | bytes 1048576 | tf_op jit(solution)/shard_map/all_to_all | solution.py:448
  25.8 15.8 %collective-permute-start.1 = (f32[4,4,8,128]{3,2,1,0:T(8,128)S(1)}, f32[4,4,8,128]{3,2,1,0:T(8,128)S(1)}, u32[]{:S(2)}, u32[]{:S(2)}) collective-permute-start(f32[4,4,8,128]{3,2,1,0:T(8,128)S(1)} %pad_maximum_fusion.1), channel_id=1, source_target_pairs={{0,480},{32,0},{64,32},{96,64},{128,96},{160,128},{192,160},{224,1... | collective-permute-start | bytes 196616 | tf_op jit(solution)/shard_map/ppermute | solution.py:443
  35.0 6.6 %collective-permute-start = (f32[4,4,8,128]{3,2,1,0:T(8,128)S(1)}, f32[4,4,8,128]{3,2,1,0:T(8,128)S(1)}, u32[]{:S(2)}, u32[]{:S(2)}) collective-permute-start(f32[4,4,8,128]{3,2,1,0:T(8,128)S(1)} %pad_maximum_fusion.1), channel_id=1, source_target_pairs={{0,32},{32,64},{64,96},{96,128},{128,160},{160,192},{192,224},{224... | collective-permute-start | bytes 196616 | tf_op jit(solution)/shard_map/ppermute | solution.py:443
  61.8 6.7 %collective-permute-start.3 = (f32[2,4,4,128]{3,2,1,0:T(4,128)S(1)}, f32[2,4,4,128]{3,2,1,0:T(4,128)S(1)}, u32[]{:S(2)}, u32[]{:S(2)}) collective-permute-start(f32[2,4,4,128]{3,2,1,0:T(4,128)S(1)} %pad_maximum_fusion.5), channel_id=1, source_target_pairs={{0,480},{32,0},{64,32},{96,64},{128,96},{160,128},{192,160},{224,1... | collective-permute-start | bytes 49160 | tf_op jit(solution)/shard_map/ppermute | solution.py:443
  65.9 5.7 %collective-permute-start.2 = (f32[2,4,4,128]{3,2,1,0:T(4,128)S(1)}, f32[2,4,4,128]{3,2,1,0:T(4,128)S(1)}, u32[]{:S(2)}, u32[]{:S(2)}) collective-permute-start(f32[2,4,4,128]{3,2,1,0:T(4,128)S(1)} %pad_maximum_fusion.5), channel_id=1, source_target_pairs={{0,32},{32,64},{64,96},{96,128},{128,160},{160,192},{192,224},{224... | collective-permute-start | bytes 49160 | tf_op jit(solution)/shard_map/ppermute | solution.py:443
  85.9 5.9 %collective-permute-start.5 = (f32[2,4,4,128]{3,2,1,0:T(4,128)S(1)}, f32[2,4,4,128]{3,2,1,0:T(4,128)S(1)}, u32[]{:S(2)}, u32[]{:S(2)}) collective-permute-start(f32[2,4,4,128]{3,2,1,0:T(4,128)S(1)} %pad_maximum_fusion.6), channel_id=1, source_target_pairs={{0,480},{32,0},{64,32},{96,64},{128,96},{160,128},{192,160},{224,1... | collective-permute-start | bytes 49160 | tf_op jit(solution)/shard_map/ppermute | solution.py:443
  87.8 5.7 %collective-permute-start.4 = (f32[2,4,4,128]{3,2,1,0:T(4,128)S(1)}, f32[2,4,4,128]{3,2,1,0:T(4,128)S(1)}, u32[]{:S(2)}, u32[]{:S(2)}) collective-permute-start(f32[2,4,4,128]{3,2,1,0:T(4,128)S(1)} %pad_maximum_fusion.6), channel_id=1, source_target_pairs={{0,32},{32,64},{64,96},{96,128},{128,160},{160,192},{192,224},{224... | collective-permute-start | bytes 49160 | tf_op jit(solution)/shard_map/ppermute | solution.py:443
  107.6 5.9 %collective-permute-start.7 = (f32[2,4,4,128]{3,2,1,0:T(4,128)S(1)}, f32[2,4,4,128]{3,2,1,0:T(4,128)S(1)}, u32[]{:S(2)}, u32[]{:S(2)}) collective-permute-start(f32[2,4,4,128]{3,2,1,0:T(4,128)S(1)} %pad_maximum_fusion.7), channel_id=1, source_target_pairs={{0,480},{32,0},{64,32},{96,64},{128,96},{160,128},{192,160},{224,1... | collective-permute-start | bytes 49160 | tf_op jit(solution)/shard_map/ppermute | solution.py:443
  109.5 5.7 %collective-permute-start.6 = (f32[2,4,4,128]{3,2,1,0:T(4,128)S(1)}, f32[2,4,4,128]{3,2,1,0:T(4,128)S(1)}, u32[]{:S(2)}, u32[]{:S(2)}) collective-permute-start(f32[2,4,4,128]{3,2,1,0:T(4,128)S(1)} %pad_maximum_fusion.7), channel_id=1, source_target_pairs={{0,32},{32,64},{64,96},{96,128},{128,160},{160,192},{192,224},{224... | collective-permute-start | bytes 49160 | tf_op jit(solution)/shard_map/ppermute | solution.py:443

commit v3 on v2

v3 whole, which is shorter than its diff:
```python
import functools

import jax
import jax.numpy as jnp
from jax import lax
from jax.experimental import pallas as pl
from jax.experimental.pallas import tpu as pltpu
from jax.sharding import PartitionSpec as P

CODES = {
    (0, 0, 1): 0,
    (0, 1, -1): 1,
    (0, 1, 0): 2,
    (0, 1, 1): 3,
    (1, -1, -1): 4,
    (1, -1, 0): 5,
    (1, -1, 1): 6,
    (1, 0, -1): 7,
    (1, 0, 0): 8,
    (1, 0, 1): 9,
    (1, 1, -1): 10,
    (1, 1, 0): 11,
    (1, 1, 1): 12,
}
SHELL = [(x, y, z) for x in (-1, 0, 1) for y in (-1, 0, 1) for z in (-1, 0, 1)]

SHIFT = (220.0, 110.0, 145.0, 140.0)
SCALE = (60.0, 70.0, 70.0, 70.0)
BACK = (0.0, 0.7, 1.0, 1.0)
PAIRS = [(i, j) for i in range(4) for j in range(i, 5)]
VMEM = pl.BlockSpec(memory_space=pltpu.VMEM)
SMEM = pl.BlockSpec(memory_space=pltpu.SMEM)
PARAMS = pltpu.CompilerParams(vmem_limit_bytes=24 * 1024 * 1024)


CHIP = [(1 + y) * 4 + 1 + z for y in range(4) for z in range(2)]
PLANE = [(y, z) for y in (-1, 0, 1) for z in (-1, 0, 1)]


def spread(row):
    return jnp.broadcast_to(row, (8, 128))


def reduce_rows(total_ref, image_ref):
    for field in range(image_ref.shape[0]):
        block = total_ref[field * 16 : (field + 1) * 16].reshape(128, 128)
        image_ref[field : field + 1, :] = jnp.sum(block.T, axis=0, keepdims=True)


def next_basis(step, image, field, before, mask, hard):
    value = image * mask + hard * field
    value = (value - SHIFT[step] * field) * (1.0 / SCALE[step])
    if BACK[step]:
        value = value - BACK[step] * before
    return value


def pack_kernel(*refs):
    sources, packed_ref, inputs, semaphores = refs[:6], refs[6], refs[7:13], refs[13]
    copies = [
        pltpu.make_async_copy(source, target, semaphores.at[number])
        for number, (source, target) in enumerate(zip(sources, inputs))
    ]
    for copy in copies:
        copy.start()
    for copy in copies:
        copy.wait()
    place_ref, shield_ref, hard_ref, electro_ref, count_ref, list_ref = inputs
    lane = lax.broadcasted_iota(jnp.int32, (1, 128), 1)
    for y in range(2):
        for z in range(2):
            cell = 2 * y + z
            count = jnp.broadcast_to(count_ref[0, y : y + 1, z : z + 1], (1, 128))
            mask = jnp.where(lane < count, 1.0, 0.0)
            flags = jnp.zeros((1, 128), jnp.float32)
            for number in range(13):
                code = jnp.broadcast_to(list_ref[0, y, z : z + 1, number : number + 1], (1, 128))
                flags = jnp.where(lane == code, 1.0, flags)
            rows = []
            for number in range(3):
                rows.append(place_ref[0, y, number, z : z + 1])
            shield = shield_ref[0, y, z : z + 1]
            rows.append(jnp.exp(-1.5 * jnp.log(shield)) * (1000.0**-0.5))
            rows.append(-electro_ref[0, y, z : z + 1] * mask)
            rows.append(-mask)
            rows.append(flags)
            rows.append(hard_ref[0, y, z : z + 1])
            block = jnp.concatenate(rows, axis=0)
            for copy in range(packed_ref.shape[0]):
                packed_ref[copy, cell] = block


def run_pack(count, *inputs):
    return pl.pallas_call(
        pack_kernel,
        out_shape=jax.ShapeDtypeStruct((count, 4, 8, 128), jnp.float32),
        in_specs=[pl.BlockSpec(memory_space=pltpu.HBM)] * 6,
        out_specs=VMEM,
        scratch_shapes=[pltpu.VMEM(value.shape, value.dtype) for value in inputs]
        + [pltpu.SemaphoreType.DMA((6,))],
        compiler_params=pltpu.CompilerParams(vmem_limit_bytes=63 * 1024 * 1024),
        name="pack",
    )(*inputs)


def fill_rows(packed_ref, rows, layer):
    for y in range(6):
        for z in range(4):
            cell = y * 4 + z
            block = packed_ref[cell]
            for number, shift in enumerate((layer, y - 1.0, z - 1.0)):
                rows[cell, number] = spread(block[number : number + 1] + shift)
            for number in range(3, 6):
                rows[cell, number] = spread(block[number : number + 1])


def move_away(flag):
    return jnp.broadcast_to((1.0 - flag) * 100.0, (8, 128))


def build_tiles(same, size, base_of, cols, away, rows, tiles_ref, start_of, total):
    sub = lax.broadcasted_iota(jnp.int32, (8, 128), 0)
    lane = lax.broadcasted_iota(jnp.int32, (8, 128), 1)

    def body(index, carry):
        cell = index // 16
        chunk = index - cell * 16
        chip, base = base_of(cell)
        xi, yi, zi, si = [cols[(chip * 4 + number) * 16 + chunk] for number in range(4)]
        sums = [start_of(system, cell, chunk) for system in range(2)]
        for number, (dy, dz) in enumerate(PLANE):
            other = base + dy * 4 + dz
            dx = away[cell * 9 + number] - xi
            dy = rows[other, 1] - yi
            dz = rows[other, 2] - zi
            square = jnp.maximum(dx * dx + dy * dy + dz * dz, 1e-30)
            ratio = square * lax.rsqrt(square)
            fourth = square * square
            taper = 1.44 + fourth * (-50.4 + ratio * (120.96 + ratio * (-100.8 + 28.8 * ratio)))
            cube = square * ratio + rows[other, 3] * si
            value = taper * jnp.exp2(jnp.log(cube) * (-1.0 / (3.0 * 0.6931471805599453)))
            keep = square < 1.0
            if same and number == 4:
                keep = keep & (sub + chunk * 8 != lane)
            value = jnp.where(keep, value, 0.0)
            tiles_ref[(cell * 9 + number) * 16 + chunk] = value
            for system in range(2):
                sums[system] = sums[system] + value * rows[other, 4 + system]
        for system in range(2):
            total[(system * size + cell) * 16 + chunk] = sums[system]
        return carry

    lax.fori_loop(0, size * 16, body, 0)


def own_base(core):
    def place(own):
        chip = core * 4 + own
        return chip, (1 + chip // 2) * 4 + 1 + chip % 2

    return place


def chip_base(cell):
    return cell, (1 + cell // 2) * 4 + 1 + cell % 2


def nothing(system, cell, chunk):
    return jnp.zeros((8, 128), jnp.float32)


def partly(before, core):
    def start(system, cell, chunk):
        mine = jnp.where(cell // 4 == core, 1.0, 0.0)
        return before[(system * 4 + cell % 4) * 16 + chunk] * mine

    return start


def same_kernel(place_ref, region_ref, tiles_ref, cols_ref, total_ref, field_ref, aux_ref, rows, away):
    core = place_ref[0]
    fill_rows(region_ref, rows, 0.0)
    for chip, cell in enumerate(CHIP):
        for number in range(4):
            column = jnp.broadcast_to(rows[cell, number, 0:1, :], (128, 128)).T
            start = (chip * 4 + number) * 16
            cols_ref[start : start + 16] = column.reshape(16, 8, 128)
    for cell in range(24):
        mask = -region_ref[cell, 5:6]
        for system in range(2):
            row = system * 24 + cell
            field_ref[row : row + 1] = region_ref[cell, 4 + system : 5 + system]
            aux_ref[row : row + 1] = mask
            aux_ref[48 + row : 49 + row] = region_ref[cell, 7:8] * mask
    for own in range(4):
        _, base = own_base(core)(own)
        for number, (dy, dz) in enumerate(PLANE):
            other = base + dy * 4 + dz
            row = rows[other, 0]
            if (0, dy, dz) in CODES:
                code = CODES[0, dy, dz]
                row = row + move_away(region_ref[base, 6:7, code : code + 1])
            elif (dy, dz) != (0, 0):
                code = CODES[0, -dy, -dz]
                row = row + move_away(region_ref[other, 6:7, code : code + 1])
            away[own * 9 + number] = row
    build_tiles(True, 4, own_base(core), cols_ref, away, rows, tiles_ref, nothing, total_ref)


def side_kernel(place_ref, region_ref, side_ref, cols_ref, before_ref, tiles_ref, image_ref, rows, away, total):
    core = place_ref[0]
    upper = jnp.where(core == 1, 1.0, 0.0)
    fill_rows(side_ref, rows, 2.0 * upper - 1.0)
    for chip, cell in enumerate(CHIP):
        for number, (dy, dz) in enumerate(PLANE):
            other = cell + dy * 4 + dz
            code, back = CODES[1, dy, dz], CODES[1, -dy, -dz]
            flag = upper * region_ref[cell, 6:7, code : code + 1]
            flag = flag + (1.0 - upper) * side_ref[other, 6:7, back : back + 1]
            away[chip * 9 + number] = rows[other, 0] + move_away(flag)
    start = partly(before_ref, core)
    build_tiles(False, 8, chip_base, cols_ref, away, rows, tiles_ref, start, total)
    reduce_rows(total, image_ref)


SHAPE = functools.partial(jax.ShapeDtypeStruct, dtype=jnp.float32)


def cost(flops):
    return pl.CostEstimate(flops=flops, bytes_accessed=4 * 1024 * 1024, transcendentals=0)


def run_same(place, region):
    return pl.pallas_call(
        same_kernel,
        out_shape=(
            SHAPE((36 * 16, 8, 128)),
            SHAPE((512, 8, 128)),
            SHAPE((128, 8, 128)),
            SHAPE((48, 128)),
            SHAPE((96, 128)),
        ),
        in_specs=[SMEM, VMEM],
        out_specs=(VMEM,) * 5,
        scratch_shapes=[
            pltpu.VMEM((24, 6, 8, 128), jnp.float32),
            pltpu.VMEM((36, 8, 128), jnp.float32),
        ],
        compiler_params=PARAMS,
        cost_estimate=cost(40 * 36 * 16384),
        name="tiles_same",
    )(place, region)


def run_side(*inputs):
    return pl.pallas_call(
        side_kernel,
        out_shape=(SHAPE((72 * 16, 8, 128)), SHAPE((16, 128))),
        in_specs=[SMEM] + [VMEM] * 4,
        out_specs=(VMEM,) * 2,
        scratch_shapes=[
            pltpu.VMEM((24, 6, 8, 128), jnp.float32),
            pltpu.VMEM((72, 8, 128), jnp.float32),
            pltpu.VMEM((256, 8, 128), jnp.float32),
        ],
        compiler_params=PARAMS,
        cost_estimate=cost(40 * 72 * 16384),
        name="tiles_side",
    )(*inputs)


def gram_row(fields, last):
    lane = lax.broadcasted_iota(jnp.int32, (1, 128), 1)
    row = jnp.zeros((1, 128), jnp.float32)
    for system in range(2):
        mine = [0.5 * field for field in fields[system]]
        entries = [
            fields[system][i] * last[system] if j == 4 else mine[i] * fields[system][j] for i, j in PAIRS
        ] + mine
        for number, entry in enumerate(entries):
            part = jnp.sum(jnp.sum(entry, axis=0, keepdims=True), axis=1, keepdims=True)
            row = row + jnp.where(lane == 2 * number + system, part, 0.0)
    return row


def fill_fields(field_ref, rows):
    for system in range(2):
        for cell in range(24):
            row = system * 24 + cell
            rows[cell * 2 + system] = spread(field_ref[row : row + 1])


def apply_tiles(size, base_of, tiles_ref, rows, start_of, total):
    def body(index, carry):
        cell = index // 4
        group = index - cell * 4
        _, base = base_of(cell)
        chunks = [group * 4 + part for part in range(4)]
        sums = [[start_of(system, cell, chunk) for chunk in chunks] for system in range(2)]
        for number, (dy, dz) in enumerate(PLANE):
            other = base + dy * 4 + dz
            right = [rows[other * 2 + system] for system in range(2)]
            for part, chunk in enumerate(chunks):
                tile = tiles_ref[(cell * 9 + number) * 16 + chunk]
                for system in range(2):
                    sums[system][part] = sums[system][part] + tile * right[system]
        for system in range(2):
            for part, chunk in enumerate(chunks):
                total[(system * size + cell) * 16 + chunk] = sums[system][part]
        return carry

    lax.fori_loop(0, size * 4, body, 0)


def update_kernel(step, place_ref, every_ref, aux_ref, *refs):
    fields, next_ref, image = refs[: step + 1], refs[step + 1], refs[step + 2]
    chips, line, chip_y, chip_z = place_ref[1], place_ref[2], place_ref[3], place_ref[4]
    ys = [(lax.rem(chip_y + chips - 1, chips), 3)]
    ys += [(chip_y, inner) for inner in range(4)] + [(lax.rem(chip_y + 1, chips), 0)]
    zs = [(lax.rem(chip_z + line - 1, line), 1), (chip_z, 0), (chip_z, 1), (lax.rem(chip_z + 1, line), 0)]
    for y, (place_y, inner_y) in enumerate(ys):
        for z, (place_z, inner_z) in enumerate(zs):
            device = 2 * place_y * line + place_z
            for system in range(2):
                source = system * 8 + inner_y * 2 + inner_z
                row = system * 24 + y * 4 + z
                both = every_ref[device, source : source + 1] + every_ref[device + line, source : source + 1]
                image[row : row + 1] = both
    before = fields[step - 1][...] if step else None
    next_ref[...] = next_basis(step, image[...], fields[step][...], before, aux_ref[0:48], aux_ref[48:96])


def run_update(step, place, every, aux, fields):
    return pl.pallas_call(
        functools.partial(update_kernel, step),
        out_shape=SHAPE((48, 128)),
        in_specs=[SMEM] + [VMEM] * (2 + len(fields)),
        out_specs=VMEM,
        scratch_shapes=[pltpu.VMEM((48, 128), jnp.float32)],
        compiler_params=PARAMS,
        name=f"update{step}",
    )(place, every, aux, *fields)


def apply_same_kernel(place_ref, tiles_ref, field_ref, total_ref, rows):
    fill_fields(field_ref, rows)
    apply_tiles(4, own_base(place_ref[0]), tiles_ref, rows, nothing, total_ref)


def apply_side_kernel(last, place_ref, tiles_ref, side_ref, before_ref, *refs):
    core = place_ref[0]
    if last:
        aux_ref, fields, image_ref, (rows, total) = refs[0], refs[1:5], refs[5], refs[6:]
        partial = image_ref.at[8:24]
    else:
        image_ref, rows, total = refs
        partial = image_ref
    fill_fields(side_ref, rows)
    apply_tiles(8, chip_base, tiles_ref, rows, partly(before_ref, core), total)
    reduce_rows(total, partial)
    if last:

        def chip(ref, system, first):
            parts = [ref[first + system * 24 + cell : first + system * 24 + cell + 2] for cell in (5, 9, 13, 17)]
            return jnp.concatenate(parts, axis=0)

        mine = [[chip(field, system, 0) for field in fields] for system in range(2)]
        images = []
        for system in range(2):
            diagonal = 0.5 * (chip(aux_ref, system, 48) - SHIFT[3])
            image = partial[system * 8 : system * 8 + 8] + diagonal * mine[system][3]
            images.append(image * (1.0 / SCALE[3]) - 0.5 * BACK[3] * mine[system][2])
        image_ref[0:8] = jnp.broadcast_to(gram_row(mine, images), (8, 128))


def run_apply_same(place, tiles, field):
    return pl.pallas_call(
        apply_same_kernel,
        out_shape=SHAPE((128, 8, 128)),
        in_specs=[SMEM] + [VMEM] * 2,
        out_specs=VMEM,
        scratch_shapes=[pltpu.VMEM((48, 8, 128), jnp.float32)],
        compiler_params=PARAMS,
        cost_estimate=cost(4 * 36 * 16384),
        name="apply_same",
    )(place, tiles, field)


def run_apply_side(last, place, tiles, side, before, *more):
    return pl.pallas_call(
        functools.partial(apply_side_kernel, last),
        out_shape=SHAPE((24 if last else 16, 128)),
        in_specs=[SMEM] + [VMEM] * (3 + len(more)),
        out_specs=VMEM,
        scratch_shapes=[
            pltpu.VMEM((48, 8, 128), jnp.float32),
            pltpu.VMEM((256, 8, 128), jnp.float32),
        ],
        compiler_params=PARAMS,
        cost_estimate=cost(4 * 72 * 16384),
        name="apply_last" if last else "apply_side",
    )(place, tiles, side, before, *more)


def combine(coefs, fields):
    value = coefs[0] * fields[0]
    for coef, field in zip(coefs[1:], fields[1:]):
        value = value + coef * field
    return value


def finish_kernel(place_ref, gram_ref, every_ref, aux_ref, *refs):
    regions, (charges_ref, residual_ref, own, image) = refs[:4], refs[4:]
    core, line, chip_y, chip_z = place_ref[0], place_ref[2], place_ref[3], place_ref[4]
    device = 2 * chip_y * line + chip_z
    for system in range(2):
        for cell in range(4):
            row = system * 4 + cell
            place = system * 24 + (1 + 2 * core + cell // 2) * 4 + 1 + cell % 2
            source = 8 + system * 8 + 4 * core + cell
            both = every_ref[device, pl.ds(source, 1)] + every_ref[device + line, pl.ds(source, 1)]
            image[row : row + 1] = both
            for number, region in enumerate(regions):
                own[number, row : row + 1] = region[pl.ds(place, 1)]
            own[4, row : row + 1] = aux_ref[pl.ds(place, 1)]
            own[5, row : row + 1] = aux_ref[pl.ds(48 + place, 1)]
    fields = [own[number] for number in range(4)]
    fields.append(next_basis(3, image[...], fields[3], fields[2], own[4], own[5]))
    summed = spread(jnp.sum(gram_ref[...], axis=0, keepdims=True))
    lane = lax.broadcasted_iota(jnp.int32, (8, 128), 1)
    system = lax.broadcasted_iota(jnp.int32, (8, 128), 0) // 4

    def entry(number):
        picked = jnp.where(lane == 2 * number + system, summed, 0.0)
        return jnp.broadcast_to(jnp.sum(picked, axis=1, keepdims=True), (8, 128))

    gram = {}
    for number, (i, j) in enumerate(PAIRS):
        gram[i, j] = gram[j, i] = entry(number)
    totals = [entry(len(PAIRS) + number) for number in range(4)]

    def dot(left, right):
        result = None
        for i, a in enumerate(left):
            part = None
            for j, b in enumerate(right):
                term = gram[i, j] * b
                part = term if part is None else part + term
            result = a * part if result is None else result + a * part
        return result

    def multiply(vector):
        size = len(vector)
        out = []
        for row in range(size + 1):
            value = None
            if row >= 1:
                value = SCALE[row - 1] * vector[row - 1]
            if row < size:
                term = SHIFT[row] * vector[row]
                value = term if value is None else value + term
            if row + 1 < size:
                value = value + SCALE[row + 1] * BACK[row + 1] * vector[row + 1]
            out.append(value)
        return out

    one = jnp.ones((8, 128), jnp.float32)
    residual = [one]
    direction = [one]
    answer = []
    norm_now = gram[0, 0]
    for step in range(4):
        image = multiply(direction)
        alpha = norm_now / dot(direction, image)
        answer = [
            alpha * d if k >= len(answer) else answer[k] + alpha * d for k, d in enumerate(direction)
        ]
        residual = [
            residual[k] - alpha * value if k < len(residual) else -alpha * value
            for k, value in enumerate(image)
        ]
        if step == 3:
            break
        norm_next = dot(residual, residual)
        ratio = norm_next / norm_now
        direction = [
            value + ratio * direction[k] if k < len(direction) else value
            for k, value in enumerate(residual)
        ]
        norm_now = norm_next
    value = combine(residual, fields)
    solution = combine(answer, fields[:4])
    total = combine(answer, totals)
    charges = solution[0:4] - total[0:4] / total[4:8] * solution[4:8]
    for y in range(2):
        charges_ref[0, y] = charges[2 * y : 2 * y + 2]
        for system in range(2):
            row = system * 4 + 2 * y
            residual_ref[system, 0, y] = value[row : row + 2]


def run_finish(place, gram, every, aux, fields):
    return pl.pallas_call(
        finish_kernel,
        out_shape=(SHAPE((1, 2, 2, 128)), SHAPE((2, 1, 2, 2, 128))),
        in_specs=[SMEM] + [VMEM] * 7,
        out_specs=(VMEM, VMEM),
        scratch_shapes=[pltpu.VMEM((6, 8, 128), jnp.float32), pltpu.VMEM((8, 128), jnp.float32)],
        compiler_params=PARAMS,
        name="finish",
    )(place, gram, every, aux, *fields)


def opposite(value):
    count_x, count_y = lax.axis_size("gx"), lax.axis_size("gy")
    pairs = []
    for x in range(count_x):
        for y in range(count_y):
            target = (x + 1) % count_x if y % 2 == 0 else (x - 1) % count_x
            pairs.append((x * count_y + y, target * count_y + y))
    return lax.ppermute(value, ("gx", "gy"), pairs)


def spread_all(value, axes, count):
    sent = jnp.broadcast_to(value[None], (count,) + value.shape)
    return lax.all_to_all(sent, axes, 0, 0)


def region_of(every, chips, line, chip_y, chip_z):
    def part(place, axis):
        return lax.dynamic_index_in_dim(every, place, axis, keepdims=False)

    every = every.reshape((chips, 2, line) + every.shape[2:])
    every = jnp.moveaxis(every, 2, 1).reshape((chips, line, 4) + every.shape[4:])
    below = part(lax.rem(chip_y + chips - 1, chips), 0)[:, 3:4]
    above = part(lax.rem(chip_y + 1, chips), 0)[:, 0:1]
    every = jnp.concatenate([below, part(chip_y, 0), above], axis=1)
    below = part(lax.rem(chip_z + line - 1, line), 0)[:, 1:2]
    above = part(lax.rem(chip_z + 1, line), 0)[:, 0:1]
    return jnp.concatenate([below, part(chip_z, 0), above], axis=1)


def shards(frac_positions, shielding, hardness, electroneg, counts, neighbor_list):
    count_x, count_y, count_z = [lax.axis_size(axis) for axis in ("gx", "gy", "gz")]
    chips, plane = count_y // 2, count_y * count_z
    chip_y, core = lax.axis_index("gy") // 2, lax.rem(lax.axis_index("gy"), 2)
    chip_z = lax.axis_index("gz")
    place = jnp.stack([core, jnp.int32(chips), jnp.int32(count_z), chip_y, chip_z])

    places = frac_positions.transpose(0, 1, 3, 2, 4)
    packed = run_pack(plane, places, shielding, hardness, electroneg, counts, neighbor_list)
    every = lax.all_to_all(packed, ("gy", "gz"), 0, 0)
    every = every.reshape(count_y, count_z, 2, 2, 8, 128)
    region = region_of(every, chips, count_z, chip_y, chip_z).reshape(24, 8, 128)
    side = opposite(region)
    tiles_same, cols, total, field, aux = run_same(place, region)
    tiles_side, image = run_side(place, region, side, cols, total)
    fields = [field]
    for step in range(3):
        every = spread_all(image, ("gy", "gz"), plane)
        fields.append(run_update(step, place, every, aux, fields))
        side = opposite(fields[-1])
        total = run_apply_same(place, tiles_same, fields[-1])
        more = [aux] + fields if step == 2 else []
        image = run_apply_side(step == 2, place, tiles_side, side, total, *more)
    every = spread_all(image, ("gy", "gz"), plane)
    gram = spread_all(jnp.sum(every[:, 0:1], axis=0), "gx", count_x)
    return run_finish(place, gram.reshape(count_x, 128), every, aux, fields)


def solution(mesh):
    placed = (
        P("gx", "gy", "gz", None, None),
        P("gx", "gy", "gz", None),
        P("gx", "gy", "gz", None),
        P("gx", "gy", "gz", None),
        P("gx", "gy", "gz"),
        P("gx", "gy", "gz", None),
    )
    return jax.shard_map(
        shards,
        mesh=mesh,
        in_specs=placed,
        out_specs=(P("gx", "gy", "gz", None), P(None, "gx", "gy", "gz", None)),
        check_vma=False,
    )
```

time: 147 us -> 152 us (1.034)
  starting transfers between devices: 38.1 us -> 26.2 us
  Pallas kernels: 20 us -> 31.3 us
  blocking collectives: 66.8 us -> 77.6 us
  waiting for transfers between devices: 17.9 us -> 14.9 us
  local copies, waits for them, and re-layouts: 1.88 us -> 0.2 us
    ppermute x8 -> x4, starting transfers between devices: 27.7 us -> 15.7 us  [opposite(): return lax.ppermute(value, ('gx', 'gy'), pairs)]
    all_to_all x5, blocking collectives: 66.8 us -> 77.6 us  [spread_all(): return lax.all_to_all(sent, axes, 0, 0)]
    pallas_call x7 -> x10, Pallas kernels: 18.1 us -> 27.7 us  [the longest x1 9.82 us: run_side(): pl.pallas_call(side_kernel, out_shape=(SHAPE((72 * 16, 8, 128)), SHAPE((1...]
    ppermute x8 -> x4, waiting for transfers between devices: 6.48 us -> 3.48 us  [opposite(): return lax.ppermute(value, ('gx', 'gy'), pairs)]
    pallas_call x3, Pallas kernels: 1.9 us -> 3.67 us  [run_apply_same(): pl.pallas_call(apply_same_kernel, out_shape=SHAPE((128, 8, 128)), in_spec...]
    broadcast_in_dim x6 -> x5, local copies, waits for them, and re-layouts: 1.72 us -> 0.09 us  [spread_all(): sent = jnp.broadcast_to(value[None], (count,) + value.shape)]
  transfers between devices with their start and end apart: 9 -> 5, of which waited for: 4 -> 4; matrix products, arithmetic and copies ran while one was open for 0% -> 0% of each run, Pallas kernels for 4% -> 6%
where the time goes in v3:
time: 152 us; the launch traced here: 151 us
  blocking collectives  77.6 us (51%)
  Pallas kernels  31.3 us (21%)
  starting transfers between devices  26.2 us (17%)
  waiting for transfers between devices  14.9 us (10%)
    all_to_all x5, blocking collectives, spread_all(): return lax.all_to_all(sent, axes, 0, 0)  77.6 us
    ppermute x4, starting transfers between devices, opposite(): return lax.ppermute(value, ('gx', 'gy'), pairs)  15.7 us
    all_to_all x1, waiting for transfers between devices, shards(): every = lax.all_to_all(packed, ('gy', 'gz'), 0, 0)  11.4 us
    all_to_all x1, starting transfers between devices, shards(): every = lax.all_to_all(packed, ('gy', 'gz'), 0, 0)  10.5 us
    pallas_call x1, Pallas kernels, run_side(): pl.pallas_call(side_kernel, out_shape=(SHAPE((72 * 16, 8, 128)), SHAPE((1...  9.82 us
    pallas_call x3, Pallas kernels, run_apply_side(): pl.pallas_call(functools.partial(apply_side_kernel, last), out_shape=SHAP...  7.39 us
    pallas_call x1, Pallas kernels, run_same(): pl.pallas_call(same_kernel, out_shape=(SHAPE((36 * 16, 8, 128)), SHAPE((5...  5.53 us
    pallas_call x3, Pallas kernels, run_apply_same(): pl.pallas_call(apply_same_kernel, out_shape=SHAPE((128, 8, 128)), in_spec...  3.67 us
  transfers between devices with their start and end apart: 5, of which 4 were waited for; matrix products, arithmetic and copies ran while one was open for 0% of the time, Pallas kernels for 6%

profile of v3, /device:TPU:1, one launch (start us, length us, event | category | flops | bytes accessed | tf_op | source)
XLA Modules:
  0.0 151.3 jit_solution(16573402271442304314)
XLA Ops:
  0.6 1.8 %pack.1 = f32[32,4,8,128]{3,2,1,0:T(8,128)} custom-call(f32[1,2,3,2,128]{4,3,2,1,0:T(2,128)} %bitcast.28, f32[1,2,2,128]{3,2,1,0:T(2,128)} %refs_1_.1, f32[1,2,2,128]{3,2,1,0:T(2,128)} %refs_2_.1, f32[1,2,2,128]{3,2,1,0:T(2,128)} %refs_3_.1, s32[1,2,2]{2,1,0:T(2,128)} %refs_4_.1, s32[1,2,2,13]{3,2,1,0:T(2,128)} %refs_5_.1), custom_call_target="tpu_custom_call" | custom-call | tf_op jit(solution)/shard_map/pack/pallas_call | solution.py:94
  2.4 10.5 %all-to-all-start = ((f32[32,4,8,128]{3,2,1,0:T(8,128)}), f32[32,4,8,128]{3,2,1,0:T(8,128)S(1)}, u32[]{:S(2)}, u32[]{:S(2)}) async-start(f32[32,4,8,128]{3,2,1,0:T(8,128)} %pack.1), calls=%async_computation | async-start | bytes 1048576 | tf_op jit(solution)/shard_map/all_to_all | solution.py:552
  13.0 11.4 %all-to-all-done = f32[32,4,8,128]{3,2,1,0:T(8,128)S(1)} async-done(((f32[32,4,8,128]{3,2,1,0:T(8,128)}), f32[32,4,8,128]{3,2,1,0:T(8,128)S(1)}, u32[]{:S(2)}, u32[]{:S(2)}) %all-to-all-start) | async-done | bytes 524320 | tf_op jit(solution)/shard_map/all_to_all | solution.py:552
  24.6 9.2 %collective-permute-start = (f32[24,8,128]{2,1,0:T(8,128)S(1)}, f32[24,8,128]{2,1,0:T(8,128)S(1)}, u32[]{:S(2)}, u32[]{:S(2)}) collective-permute-start(f32[24,8,128]{2,1,0:T(8,128)S(1)} %bitcast.22), channel_id=1, source_target_pairs={{0,32},{4,484},{8,40},{12,492},{16,48},{20,500},{24,56},{28,508},{... | collective-permute-start | bytes 294920 | tf_op jit(solution)/shard_map/ppermute | solution.py:521
  33.8 0.1 pad_add_fusion.place_ref
  33.9 5.5 %tiles_same.1 = (f32[576,8,128]{2,1,0:T(8,128)S(1)}, f32[512,8,128]{2,1,0:T(8,128)S(1)}, f32[128,8,128]{2,1,0:T(8,128)S(1)}, f32[48,128]{1,0:T(8,128)S(1)}, f32[96,128]{1,0:T(8,128)S(1)}) custom-call(s32[5]{0:T(128)S(1)} %pad_add_fusion.place_ref, f32[24,8,128]{2,1,0:T(8,128)S(1)} %bitcast.23), custom_call_target="tpu_custom_call" | custom-call | flops 23592960 | bytes 4194304 | tf_op jit(solution)/shard_map/tiles_same/pallas_call | solution.py:234
  39.4 0.0 collective-permute-done.side_ref
  39.4 9.8 %tiles_side.1 = (f32[1152,8,128]{2,1,0:T(8,128)S(1)}, f32[16,128]{1,0:T(8,128)S(1)}) custom-call(s32[5]{0:T(128)S(1)} %pad_add_fusion.place_ref, f32[24,8,128]{2,1,0:T(8,128)S(1)} %bitcast.24, f32[24,8,128]{2,1,0:T(8,128)S(1)} %collective-permute-done.side_ref, f32[512,8,128]{2,1,0:T(8,128)S(1)} %get-tuple-element.9.cols_ref, ...), custom_call_target="tpu_custom_call" | custom-call | flops 47185920 | bytes 4194304 | tf_op jit(solution)/shard_map/tiles_side/pallas_call | solution.py:256
  49.3 12.3 %all_to_all.30.every_ref = f32[32,16,128]{2,1,0:T(8,128)S(1)} all-to-all(f32[32,16,128]{2,1,0:T(8,128)S(1)} %broadcast_in_dim.10), channel_id=1, replica_groups=mesh['gx'=16,'gy'=8,'gz'=4] {'gy','gz'}, dimensions={0} | all-to-all | bytes 524288 | tf_op jit(solution)/shard_map/all_to_all | solution.py:526
  61.5 0.6 update0.1.field_ref.refs_1_.refs_2_
  62.1 2.7 %collective-permute-start.1 = (f32[48,128]{1,0:T(8,128)S(1)}, f32[48,128]{1,0:T(8,128)S(1)}, u32[]{:S(2)}, u32[]{:S(2)}) collective-permute-start(f32[48,128]{1,0:T(8,128)S(1)} %update0.1.field_ref.refs_1_.refs_2_), channel_id=1, source_target_pairs={{0,32},{4,484},{8,40},{12,492},{16,48},{20,500},{24,56},{28,508},{... | collective-permute-start | bytes 73736 | tf_op jit(solution)/shard_map/ppermute | solution.py:521
  64.8 1.2 apply_same.3.before_ref
  66.1 0.6 collective-permute-done.1.side_ref
  66.7 2.4 %apply_side.2 = f32[16,128]{1,0:T(8,128)S(1)} custom-call(s32[5]{0:T(128)S(1)} %pad_add_fusion.place_ref, f32[1152,8,128]{2,1,0:T(8,128)S(1)} %get-tuple-element.11.tiles_ref, f32[48,128]{1,0:T(8,128)S(1)} %collective-permute-done.1.side_ref, f32[128,8,128]{2,1,0:T(8,128)S(1)} %apply_same.3.before_ref), custom_call_target="tpu_custom_call" | custom-call | flops 4718592 | bytes 4194304 | tf_op jit(solution)/shard_map/apply_side/pallas_call | solution.py:390
  69.2 15.2 %all_to_all.31.every_ref = f32[32,16,128]{2,1,0:T(8,128)S(1)} all-to-all(f32[32,16,128]{2,1,0:T(8,128)S(1)} %broadcast_in_dim.11), channel_id=1, replica_groups=mesh['gx'=16,'gy'=8,'gz'=4] {'gy','gz'}, dimensions={0} | all-to-all | bytes 524288 | tf_op jit(solution)/shard_map/all_to_all | solution.py:526
  84.3 0.6 update1.1.field_ref.refs_2_.refs_3_
  84.9 1.9 %collective-permute-start.2 = (f32[48,128]{1,0:T(8,128)S(1)}, f32[48,128]{1,0:T(8,128)S(1)}, u32[]{:S(2)}, u32[]{:S(2)}) collective-permute-start(f32[48,128]{1,0:T(8,128)S(1)} %update1.1.field_ref.refs_2_.refs_3_), channel_id=1, source_target_pairs={{0,32},{4,484},{8,40},{12,492},{16,48},{20,500},{24,56},{28,508},{... | collective-permute-start | bytes 73736 | tf_op jit(solution)/shard_map/ppermute | solution.py:521
  86.9 1.2 apply_same.4.before_ref
  88.1 1.4 collective-permute-done.2.side_ref
  89.5 2.4 %apply_side.3 = f32[16,128]{1,0:T(8,128)S(1)} custom-call(s32[5]{0:T(128)S(1)} %pad_add_fusion.place_ref, f32[1152,8,128]{2,1,0:T(8,128)S(1)} %get-tuple-element.11.tiles_ref, f32[48,128]{1,0:T(8,128)S(1)} %collective-permute-done.2.side_ref, f32[128,8,128]{2,1,0:T(8,128)S(1)} %apply_same.4.before_ref), custom_call_target="tpu_custom_call" | custom-call | flops 4718592 | bytes 4194304 | tf_op jit(solution)/shard_map/apply_side/pallas_call | solution.py:390
  92.0 15.2 %all_to_all.32.every_ref = f32[32,16,128]{2,1,0:T(8,128)S(1)} all-to-all(f32[32,16,128]{2,1,0:T(8,128)S(1)} %broadcast_in_dim.12), channel_id=1, replica_groups=mesh['gx'=16,'gy'=8,'gz'=4] {'gy','gz'}, dimensions={0} | all-to-all | bytes 524288 | tf_op jit(solution)/shard_map/all_to_all | solution.py:526
  107.2 0.6 update2.1.field_ref.refs_4_.refs_3_
  107.8 1.9 %collective-permute-start.3 = (f32[48,128]{1,0:T(8,128)S(1)}, f32[48,128]{1,0:T(8,128)S(1)}, u32[]{:S(2)}, u32[]{:S(2)}) collective-permute-start(f32[48,128]{1,0:T(8,128)S(1)} %update2.1.field_ref.refs_4_.refs_3_), channel_id=1, source_target_pairs={{0,32},{4,484},{8,40},{12,492},{16,48},{20,500},{24,56},{28,508},{... | collective-permute-start | bytes 73736 | tf_op jit(solution)/shard_map/ppermute | solution.py:521
  109.7 1.2 apply_same.5.before_ref
  110.9 1.4 collective-permute-done.3.side_ref
  112.3 2.5 %apply_last.1 = f32[24,128]{1,0:T(8,128)S(1)} custom-call(s32[5]{0:T(128)S(1)} %pad_add_fusion.place_ref, f32[1152,8,128]{2,1,0:T(8,128)S(1)} %get-tuple-element.11.tiles_ref, f32[48,128]{1,0:T(8,128)S(1)} %collective-permute-done.3.side_ref, f32[128,8,128]{2,1,0:T(8,128)S(1)} %apply_same.5.before_ref, f32[96,128]{1,0:T(8,128)S(1)} %get-tuple-element.13.aux_ref.refs_0_, ...), custom_call_target="tpu_custom_call" | custom-call | flops 4718592 | bytes 4194304 | tf_op jit(solution)/shard_map/apply_last/pallas_call | solution.py:390
  114.9 16.4 %all_to_all.33.every_ref = f32[32,24,128]{2,1,0:T(8,128)S(1)} all-to-all(f32[32,24,128]{2,1,0:T(8,128)S(1)} %broadcast_in_dim.13), channel_id=1, replica_groups=mesh['gx'=16,'gy'=8,'gz'=4] {'gy','gz'}, dimensions={0} | all-to-all | bytes 786432 | tf_op jit(solution)/shard_map/all_to_all | solution.py:526
  131.4 18.6 %all_to_all.34 = f32[16,1,128]{2,1,0:T(1,128)S(1)} all-to-all(f32[16,1,128]{2,1,0:T(1,128)S(1)} %broadcast_in_dim.14), channel_id=1, replica_groups=mesh['gx'=16,'gy'=8,'gz'=4] {'gx'}, dimensions={0} | all-to-all | bytes 16384 | tf_op jit(solution)/shard_map/all_to_all | solution.py:526
  150.0 1.3 finish.1
  (16 shorter events, 0.3 us)
Async XLA Ops:
  2.4 21.9 %all-to-all-start = ((f32[32,4,8,128]{3,2,1,0:T(8,128)}), f32[32,4,8,128]{3,2,1,0:T(8,128)S(1)}, u32[]{:S(2)}, u32[]{:S(2)}) async-start(f32[32,4,8,128]{3,2,1,0:T(8,128)} %pack.1), calls=%async_computation | async-start | bytes 1048576 | tf_op jit(solution)/shard_map/all_to_all | solution.py:552
  24.6 14.8 %collective-permute-start = (f32[24,8,128]{2,1,0:T(8,128)S(1)}, f32[24,8,128]{2,1,0:T(8,128)S(1)}, u32[]{:S(2)}, u32[]{:S(2)}) collective-permute-start(f32[24,8,128]{2,1,0:T(8,128)S(1)} %bitcast.22), channel_id=1, source_target_pairs={{0,32},{4,484},{8,40},{12,492},{16,48},{20,500},{24,56},{28,508},{... | collective-permute-start | bytes 294920 | tf_op jit(solution)/shard_map/ppermute | solution.py:521
  62.1 4.6 %collective-permute-start.1 = (f32[48,128]{1,0:T(8,128)S(1)}, f32[48,128]{1,0:T(8,128)S(1)}, u32[]{:S(2)}, u32[]{:S(2)}) collective-permute-start(f32[48,128]{1,0:T(8,128)S(1)} %update0.1.field_ref.refs_1_.refs_2_), channel_id=1, source_target_pairs={{0,32},{4,484},{8,40},{12,492},{16,48},{20,500},{24,56},{28,508},{... | collective-permute-start | bytes 73736 | tf_op jit(solution)/shard_map/ppermute | solution.py:521
  84.9 4.6 %collective-permute-start.2 = (f32[48,128]{1,0:T(8,128)S(1)}, f32[48,128]{1,0:T(8,128)S(1)}, u32[]{:S(2)}, u32[]{:S(2)}) collective-permute-start(f32[48,128]{1,0:T(8,128)S(1)} %update1.1.field_ref.refs_2_.refs_3_), channel_id=1, source_target_pairs={{0,32},{4,484},{8,40},{12,492},{16,48},{20,500},{24,56},{28,508},{... | collective-permute-start | bytes 73736 | tf_op jit(solution)/shard_map/ppermute | solution.py:521
  107.8 4.6 %collective-permute-start.3 = (f32[48,128]{1,0:T(8,128)S(1)}, f32[48,128]{1,0:T(8,128)S(1)}, u32[]{:S(2)}, u32[]{:S(2)}) collective-permute-start(f32[48,128]{1,0:T(8,128)S(1)} %update2.1.field_ref.refs_4_.refs_3_), channel_id=1, source_target_pairs={{0,32},{4,484},{8,40},{12,492},{16,48},{20,500},{24,56},{28,508},{... | collective-permute-start | bytes 73736 | tf_op jit(solution)/shard_map/ppermute | solution.py:521

commit v4 on v2

--- a/solution.py
+++ b/solution.py
@@ -29,6 +29,7 @@
 BACK = (0.0, 0.7, 1.0, 1.0)
 PAIRS = [(i, j) for i in range(4) for j in range(i, 5)]
 VMEM = pl.BlockSpec(memory_space=pltpu.VMEM)
+SMEM = pl.BlockSpec(memory_space=pltpu.SMEM)
 PARAMS = pltpu.CompilerParams(vmem_limit_bytes=24 * 1024 * 1024)
 
 
@@ -55,7 +56,7 @@
     return value
 
 
-def pack_kernel(*refs):
+def pack_kernel(order_ref, *refs):
     sources, packed_ref, inputs, semaphores = refs[:6], refs[6], refs[7:13], refs[13]
     copies = [
         pltpu.make_async_copy(source, target, semaphores.at[number])
@@ -76,27 +77,31 @@
             for number in range(13):
                 code = jnp.broadcast_to(list_ref[0, y, z : z + 1, number : number + 1], (1, 128))
                 flags = jnp.where(lane == code, 1.0, flags)
+            rows = []
             for number in range(3):
-                packed_ref[cell, number : number + 1] = place_ref[0, y, number, z : z + 1]
+                rows.append(place_ref[0, y, number, z : z + 1])
             shield = shield_ref[0, y, z : z + 1]
-            packed_ref[cell, 3:4] = jnp.exp(-1.5 * jnp.log(shield)) * (1000.0**-0.5)
-            packed_ref[cell, 4:5] = -electro_ref[0, y, z : z + 1] * mask
-            packed_ref[cell, 5:6] = -mask
-            packed_ref[cell, 6:7] = flags
-            packed_ref[cell, 7:8] = hard_ref[0, y, z : z + 1]
-
-
-def run_pack(*inputs):
+            rows.append(jnp.exp(-1.5 * jnp.log(shield)) * (1000.0**-0.5))
+            rows.append(-electro_ref[0, y, z : z + 1] * mask)
+            rows.append(-mask)
+            rows.append(flags)
+            rows.append(hard_ref[0, y, z : z + 1])
+            block = jnp.concatenate(rows, axis=0)
+            for copy in range(packed_ref.shape[0]):
+                packed_ref[copy, cell] = block
+
+
+def run_pack(count, order, *inputs):
     return pl.pallas_call(
         pack_kernel,
-        out_shape=jax.ShapeDtypeStruct((4, 8, 128), jnp.float32),
-        in_specs=[pl.BlockSpec(memory_space=pltpu.HBM)] * 6,
+        out_shape=jax.ShapeDtypeStruct((count, 4, 8, 128), jnp.float32),
+        in_specs=[SMEM] + [pl.BlockSpec(memory_space=pltpu.HBM)] * 6,
         out_specs=VMEM,
         scratch_shapes=[pltpu.VMEM(value.shape, value.dtype) for value in inputs]
         + [pltpu.SemaphoreType.DMA((6,))],
         compiler_params=pltpu.CompilerParams(vmem_limit_bytes=63 * 1024 * 1024),
         name="pack",
-    )(*inputs)
+    )(order, *inputs)
 
 
 def fill_rows(packed_ref, rows, first, layer):
@@ -137,10 +142,7 @@
     lane = lax.broadcasted_iota(jnp.int32, (8, 128), 1)
     size = len(offsets)
 
-    def body(index, carry):
-        own = index // 16
-        chunk = index - own * 16
-        base = (own // 2) * 4 + own % 2
+    def body(own, base, chunk):
         xi, yi, zi, si = [cols[(own * 4 + number) * 16 + chunk] for number in range(4)]
         if before is None:
             sums = [jnp.zeros((8, 128), jnp.float32) for _ in range(2)]
@@ -166,9 +168,16 @@
                 sums[system] = sums[system] + value * rows[cell, 4 + system]
         for system in range(2):
             total[(system * 4 + own) * 16 + chunk] = sums[system]
-        return carry
-
-    lax.fori_loop(0, 64, body, 0)
+
+    for own in range(4):
+        base = (own // 2) * 4 + own % 2
+
+        def step(index, carry, own=own, base=base):
+            for part in range(2):
+                body(own, base, index * 2 + part)
+            return carry
+
+        lax.fori_loop(0, 8, step, 0)
 
 
 def same_kernel(own_ref, tiles_ref, cols_ref, total_ref, field_ref, aux_ref, rows, away):
@@ -266,28 +275,26 @@
 def apply_tiles(offsets, tiles_ref, rows, before, total):
     size = len(offsets)
 
-    def body(index, carry):
-        own = index // 4
-        group = index - own * 4
+    for own in range(4):
         base = (own // 2) * 4 + own % 2
-        places = [[(system * 4 + own) * 16 + group * 4 + part for part in range(4)] for system in range(2)]
-        if before is None:
-            sums = [[jnp.zeros((8, 128), jnp.float32) for _ in range(4)] for _ in range(2)]
-        else:
-            sums = [[before[place] for place in line] for line in places]
-        for number, offset in enumerate(offsets):
-            cell = base + neighbor(offset)
-            right = [rows[cell * 2 + system] for system in range(2)]
-            for part in range(4):
-                tile = tiles_ref[(own * size + number) * 16 + group * 4 + part]
-                for system in range(2):
-                    sums[system][part] = sums[system][part] + tile * right[system]
-        for system in range(2):
-            for part in range(4):
-                total[places[system][part]] = sums[system][part]
-        return carry
-
-    lax.fori_loop(0, 16, body, 0)
+        for group in range(4):
+            places = [[(system * 4 + own) * 16 + group * 4 + part for part in range(4)] for system in range(2)]
+            if before is None:
+                sums = [[None] * 4 for _ in range(2)]
+            else:
+                sums = [[before[place] for place in line] for line in places]
+            for number, offset in enumerate(offsets):
+                cell = base + neighbor(offset)
+                right = [rows[cell * 2 + system] for system in range(2)]
+                for part in range(4):
+                    tile = tiles_ref[(own * size + number) * 16 + group * 4 + part]
+                    for system in range(2):
+                        term = tile * right[system]
+                        held = sums[system][part]
+                        sums[system][part] = term if held is None else held + term
+            for system in range(2):
+                for part in range(4):
+                    total[places[system][part]] = sums[system][part]
 
 
 def apply_same_kernel(tiles_ref, halo_ref, total_ref, rows):
@@ -448,39 +455,48 @@
     return lax.all_to_all(sent, axes, 0, 0)
 
 
-def around(every, axis, group, cells):
-    count = lax.axis_size(axis)
-    here = lax.axis_index(axis)
-
+def wrapped(axis):
+    here, count = lax.axis_index(axis), lax.axis_size(axis)
+    below = jnp.where(here == 0, count - 1, here - 1)
+    above = jnp.where(here == count - 1, 0, here + 1)
+    return [value.astype(jnp.uint32) for value in (below, here, above)]
+
+
+def around(every, places, cells):
     def part(place):
-        return lax.dynamic_index_in_dim(every, place, group, keepdims=False)
-
+        start = [place] + [jnp.uint32(0)] * (every.ndim - 1)
+        return lax.dynamic_slice(every, start, (1,) + every.shape[1:])[0]
+
+    below, here, above = [part(place) for place in places]
     cells = cells - 1
-    below = lax.slice_in_dim(part(lax.rem(here + count - 1, count)), 1, 2, axis=cells)
-    above = lax.slice_in_dim(part(lax.rem(here + 1, count)), 0, 1, axis=cells)
-    return jnp.concatenate([below, part(here), above], axis=cells)
-
-
-def exchange(value, dim):
-    count_y, count_z = lax.axis_size("gy"), lax.axis_size("gz")
-    every = spread_all(value, ("gy", "gz"), count_y * count_z)
-    every = every.reshape((count_y, count_z) + value.shape)
-    block = around(every, "gy", 0, 2 + dim)
-    block = around(block, "gz", 0, 2 + dim)
+    below = lax.slice_in_dim(below, 1, 2, axis=cells)
+    above = lax.slice_in_dim(above, 0, 1, axis=cells)
+    return jnp.concatenate([below, here, above], axis=cells)
+
+
+def exchange(sent, dim, places):
+    every = lax.all_to_all(sent, ("gy", "gz"), 0, 0)
+    every = every.reshape((lax.axis_size("gy"), lax.axis_size("gz")) + sent.shape[1:])
+    block = around(every, places[0:3], 2 + dim)
+    block = around(block, places[3:6], 2 + dim)
     return block, shifted(block, "gx", 1), shifted(block, "gx", -1)
 
 
 def shards(frac_positions, shielding, hardness, electroneg, counts, neighbor_list):
     count_x, count_y, count_z = [lax.axis_size(axis) for axis in ("gx", "gy", "gz")]
     places = frac_positions.transpose(0, 1, 3, 2, 4)
-    packed = run_pack(places, shielding, hardness, electroneg, counts, neighbor_list)
-    layers = exchange(packed.reshape(2, 2, 8, 128), 0)
+    count = count_y * count_z
+    indices = lax.optimization_barrier(wrapped("gy") + wrapped("gz"))
+    order = sum(indices[1:], indices[0]).astype(jnp.int32).reshape(1)
+    packed = run_pack(count, order, places, shielding, hardness, electroneg, counts, neighbor_list)
+    layers = exchange(packed.reshape(count, 2, 2, 8, 128), 0, indices)
     own, lower, upper = [layer.reshape(16, 8, 128) for layer in layers]
     tiles_same, cols, total, w0, aux = run_same(own)
     tiles_side, w1 = run_side(own, lower, upper, cols, total, w0, aux)
     fields = [w0, w1]
     for step in (1, 2, 3):
-        layers = exchange(fields[-1].reshape(2, 2, 2, 128), 1)
+        sent = jnp.broadcast_to(fields[-1].reshape(1, 2, 2, 2, 128), (count, 2, 2, 2, 128))
+        layers = exchange(sent, 1, indices)
         own, lower, upper = [layer.reshape(32, 128) for layer in layers]
         total = run_apply_same(tiles_same, own)
         outs = run_apply_side(step, step == 3, tiles_side, lower, upper, total, aux, fields)

time: 147 us -> 142 us (0.966)
  blocking collectives: 66.8 us -> 89.1 us
  starting transfers between devices: 38.1 us -> 27 us
  waiting for transfers between devices: 17.9 us -> 7.84 us
  Pallas kernels: 20 us -> 16.2 us
  local copies, waits for them, and re-layouts: 1.88 us -> 0.29 us
    all_to_all x0 -> x4, blocking collectives: none -> 60.6 us  [exchange(): every = lax.all_to_all(sent, ('gy', 'gz'), 0, 0)]
    all_to_all x5 -> x2, blocking collectives: 66.8 us -> 28.5 us  [spread_all(): return lax.all_to_all(sent, axes, 0, 0)]
    all_to_all x1 -> x0, waiting for transfers between devices: 11.4 us -> none  [spread_all(): return lax.all_to_all(sent, axes, 0, 0)]
    all_to_all x1 -> x0, starting transfers between devices: 10.4 us -> none  [spread_all(): return lax.all_to_all(sent, axes, 0, 0)]
    broadcast_in_dim x6 -> x2, local copies, waits for them, and re-layouts: 1.72 us -> 0.02 us  [spread_all(): sent = jnp.broadcast_to(value[None], (count,) + value.shape)]
  transfers between devices with their start and end apart: 9 -> 8, of which waited for: 4 -> 4; matrix products, arithmetic and copies ran while one was open for 0% -> 0% of each run, Pallas kernels for 4% -> 3%
where the time goes in v4:
time: 142 us
  blocking collectives  89.1 us (63%)
  starting transfers between devices  27 us (19%)
  Pallas kernels  16.2 us (11%)
  waiting for transfers between devices  7.84 us (6%)
    all_to_all x4, blocking collectives, exchange(): every = lax.all_to_all(sent, ('gy', 'gz'), 0, 0)  60.6 us
    all_to_all x2, blocking collectives, spread_all(): return lax.all_to_all(sent, axes, 0, 0)  28.5 us
    ppermute x8, starting transfers between devices, shifted(): return lax.ppermute(value, axis, pairs)  27 us
    ppermute x8, waiting for transfers between devices, shifted(): return lax.ppermute(value, axis, pairs)  7.84 us
    pallas_call x1, Pallas kernels, run_side(): pl.pallas_call(side_kernel, out_shape=(SHAPE((72 * 16, 8, 128)), SHAPE((8...  6.15 us
    pallas_call x1, Pallas kernels, run_same(): pl.pallas_call(same_kernel, out_shape=(SHAPE((36 * 16, 8, 128)), SHAPE((2...  3.54 us
    pallas_call x3, Pallas kernels, run_apply_side(): pl.pallas_call(functools.partial(apply_side_kernel, step, last), out_shap...  3.01 us
  transfers between devices with their start and end apart: 8, of which 4 were waited for; matrix products, arithmetic and copies ran while one was open for 0% of the time, Pallas kernels for 3%

profile of v4, /device:TPU:1, one launch (start us, length us, event | category | flops | bytes accessed | tf_op | source)
XLA Modules:
  0.0 141.6 jit_solution(6457508950854117442)
XLA Ops:
  0.7 1.8 %pack.1 = f32[32,4,8,128]{3,2,1,0:T(8,128)} custom-call(s32[1]{0:T(128)} %bitcast.order_ref, f32[1,2,3,2,128]{4,3,2,1,0:T(2,128)} %bitcast.97, f32[1,2,2,128]{3,2,1,0:T(2,128)} %refs_1_.1, f32[1,2,2,128]{3,2,1,0:T(2,128)} %refs_2_.1, f32[1,2,2,128]{3,2,1,0:T(2,128)} %refs_3_.1, s32[1,2,2]{2,1,0:T(2,128)} %refs_4_.1, s32[1,2,2,13]{3,2,1,0:T(2,128)} %refs_5_.1), custom_call_target="tpu_custom_call" | custom-call | tf_op jit(solution)/shard_map/pack/pallas_call | solution.py:95
  2.5 21.9 %all_to_all.30 = f32[32,2,2,8,128]{4,3,2,1,0:T(8,128)S(1)} all-to-all(f32[32,2,2,8,128]{4,3,2,1,0:T(8,128)} %bitcast.91), channel_id=1, replica_groups=mesh['gx'=16,'gy'=8,'gz'=4] {'gy','gz'}, dimensions={0} | all-to-all | bytes 1048576 | tf_op jit(solution)/shard_map/all_to_all | solution.py:478
  24.5 9.2 %collective-permute-start.1 = (f32[4,4,8,128]{3,2,1,0:T(8,128)S(1)}, f32[4,4,8,128]{3,2,1,0:T(8,128)S(1)}, u32[]{:S(2)}, u32[]{:S(2)}) collective-permute-start(f32[4,4,8,128]{3,2,1,0:T(8,128)S(1)} %pad_maximum_fusion.1), channel_id=1, source_target_pairs={{0,480},{32,0},{64,32},{96,64},{128,96},{160,128},{192,160},{224,1... | collective-permute-start | bytes 196616 | tf_op jit(solution)/shard_map/ppermute | solution.py:450
  33.7 1.9 %collective-permute-start = (f32[4,4,8,128]{3,2,1,0:T(8,128)S(1)}, f32[4,4,8,128]{3,2,1,0:T(8,128)S(1)}, u32[]{:S(2)}, u32[]{:S(2)}) collective-permute-start(f32[4,4,8,128]{3,2,1,0:T(8,128)S(1)} %pad_maximum_fusion.1), channel_id=1, source_target_pairs={{0,32},{32,64},{64,96},{96,128},{128,160},{160,192},{192,224},{224... | collective-permute-start | bytes 196616 | tf_op jit(solution)/shard_map/ppermute | solution.py:450
  35.6 3.5 %tiles_same.1 = (f32[576,8,128]{2,1,0:T(8,128)S(1)}, f32[256,8,128]{2,1,0:T(8,128)S(1)}, f32[128,8,128]{2,1,0:T(8,128)S(1)}, f32[8,128]{1,0:T(8,128)S(1)}, f32[16,128]{1,0:T(8,128)S(1)}) custom-call(f32[16,8,128]{2,1,0:T(8,128)S(1)} %bitcast.73), custom_call_target="tpu_custom_call" | custom-call | flops 23592960 | bytes 4194304 | tf_op jit(solution)/shard_map/tiles_same/pallas_call | solution.py:217
  39.2 0.0 collective-permute-done.1
  39.2 0.7 collective-permute-done
  39.9 6.1 %tiles_side.1 = (f32[1152,8,128]{2,1,0:T(8,128)S(1)}, f32[8,128]{1,0:T(8,128)S(1)}) custom-call(f32[16,8,128]{2,1,0:T(8,128)S(1)} %bitcast.74, f32[16,8,128]{2,1,0:T(8,128)S(1)} %bitcast.78, f32[16,8,128]{2,1,0:T(8,128)S(1)} %bitcast.77, f32[256,8,128]{2,1,0:T(8,128)S(1)} %get-tuple-element.23.cols_ref, f32[128,8,128]{2,1,0:T(8,128)S(1)} %get-tuple-element.24.before_ref, ...), custom_call_target="tpu_custom_call" | custom-call | flops 47185920 | bytes 4194304 | tf_op jit(solution)/shard_map/tiles_side/pallas_call | solution.py:239
  46.1 13.2 %all_to_all.31 = f32[32,2,2,2,128]{4,3,2,1,0:T(2,128)S(1)} all-to-all(f32[32,2,2,2,128]{4,3,2,1,0:T(2,128)S(1)} %broadcast_in_dim.36), channel_id=1, replica_groups=mesh['gx'=16,'gy'=8,'gz'=4] {'gy','gz'}, dimensions={0} | all-to-all | bytes 262144 | tf_op jit(solution)/shard_map/all_to_all | solution.py:478
  59.5 3.0 %collective-permute-start.3 = (f32[2,4,4,128]{3,2,1,0:T(4,128)S(1)}, f32[2,4,4,128]{3,2,1,0:T(4,128)S(1)}, u32[]{:S(2)}, u32[]{:S(2)}) collective-permute-start(f32[2,4,4,128]{3,2,1,0:T(4,128)S(1)} %pad_maximum_fusion.5), channel_id=1, source_target_pairs={{0,480},{32,0},{64,32},{96,64},{128,96},{160,128},{192,160},{224,1... | collective-permute-start | bytes 49160 | tf_op jit(solution)/shard_map/ppermute | solution.py:450
  62.4 2.3 %collective-permute-start.2 = (f32[2,4,4,128]{3,2,1,0:T(4,128)S(1)}, f32[2,4,4,128]{3,2,1,0:T(4,128)S(1)}, u32[]{:S(2)}, u32[]{:S(2)}) collective-permute-start(f32[2,4,4,128]{3,2,1,0:T(4,128)S(1)} %pad_maximum_fusion.5), channel_id=1, source_target_pairs={{0,32},{32,64},{64,96},{96,128},{128,160},{160,192},{192,224},{224... | collective-permute-start | bytes 49160 | tf_op jit(solution)/shard_map/ppermute | solution.py:450
  64.8 0.3 apply_same.3.before_ref
  65.1 0.0 collective-permute-done.3
  65.1 3.1 %collective-permute-done.2 = f32[2,4,4,128]{3,2,1,0:T(4,128)S(1)} collective-permute-done((f32[2,4,4,128]{3,2,1,0:T(4,128)S(1)}, f32[2,4,4,128]{3,2,1,0:T(4,128)S(1)}, u32[]{:S(2)}, u32[]{:S(2)}) %collective-permute-start.2) | collective-permute-done | bytes 16416 | tf_op jit(solution)/shard_map/ppermute | solution.py:450
  68.1 0.9 apply_side1.1.refs_2_.w2
  69.1 12.9 %all_to_all.32 = f32[32,2,2,2,128]{4,3,2,1,0:T(2,128)S(1)} all-to-all(f32[32,2,2,2,128]{4,3,2,1,0:T(2,128)S(1)} %broadcast_in_dim.38), channel_id=1, replica_groups=mesh['gx'=16,'gy'=8,'gz'=4] {'gy','gz'}, dimensions={0} | all-to-all | bytes 262144 | tf_op jit(solution)/shard_map/all_to_all | solution.py:478
  82.1 1.9 %collective-permute-start.5 = (f32[2,4,4,128]{3,2,1,0:T(4,128)S(1)}, f32[2,4,4,128]{3,2,1,0:T(4,128)S(1)}, u32[]{:S(2)}, u32[]{:S(2)}) collective-permute-start(f32[2,4,4,128]{3,2,1,0:T(4,128)S(1)} %pad_maximum_fusion.6), channel_id=1, source_target_pairs={{0,480},{32,0},{64,32},{96,64},{128,96},{160,128},{192,160},{224,1... | collective-permute-start | bytes 49160 | tf_op jit(solution)/shard_map/ppermute | solution.py:450
  84.1 3.4 %collective-permute-start.4 = (f32[2,4,4,128]{3,2,1,0:T(4,128)S(1)}, f32[2,4,4,128]{3,2,1,0:T(4,128)S(1)}, u32[]{:S(2)}, u32[]{:S(2)}) collective-permute-start(f32[2,4,4,128]{3,2,1,0:T(4,128)S(1)} %pad_maximum_fusion.6), channel_id=1, source_target_pairs={{0,32},{32,64},{64,96},{96,128},{128,160},{160,192},{192,224},{224... | collective-permute-start | bytes 49160 | tf_op jit(solution)/shard_map/ppermute | solution.py:450
  87.4 0.3 apply_same.4.before_ref
  87.7 0.0 collective-permute-done.5
  87.7 2.0 %collective-permute-done.4 = f32[2,4,4,128]{3,2,1,0:T(4,128)S(1)} collective-permute-done((f32[2,4,4,128]{3,2,1,0:T(4,128)S(1)}, f32[2,4,4,128]{3,2,1,0:T(4,128)S(1)}, u32[]{:S(2)}, u32[]{:S(2)}) %collective-permute-start.4) | collective-permute-done | bytes 16416 | tf_op jit(solution)/shard_map/ppermute | solution.py:450
  89.7 1.0 apply_side2.1.refs_3_.w3
  90.8 12.6 %all_to_all.33 = f32[32,2,2,2,128]{4,3,2,1,0:T(2,128)S(1)} all-to-all(f32[32,2,2,2,128]{4,3,2,1,0:T(2,128)S(1)} %broadcast_in_dim.40), channel_id=1, replica_groups=mesh['gx'=16,'gy'=8,'gz'=4] {'gy','gz'}, dimensions={0} | all-to-all | bytes 262144 | tf_op jit(solution)/shard_map/all_to_all | solution.py:478
  103.5 1.9 %collective-permute-start.7 = (f32[2,4,4,128]{3,2,1,0:T(4,128)S(1)}, f32[2,4,4,128]{3,2,1,0:T(4,128)S(1)}, u32[]{:S(2)}, u32[]{:S(2)}) collective-permute-start(f32[2,4,4,128]{3,2,1,0:T(4,128)S(1)} %pad_maximum_fusion.7), channel_id=1, source_target_pairs={{0,480},{32,0},{64,32},{96,64},{128,96},{160,128},{192,160},{224,1... | collective-permute-start | bytes 49160 | tf_op jit(solution)/shard_map/ppermute | solution.py:450
  105.4 3.4 %collective-permute-start.6 = (f32[2,4,4,128]{3,2,1,0:T(4,128)S(1)}, f32[2,4,4,128]{3,2,1,0:T(4,128)S(1)}, u32[]{:S(2)}, u32[]{:S(2)}) collective-permute-start(f32[2,4,4,128]{3,2,1,0:T(4,128)S(1)} %pad_maximum_fusion.7), channel_id=1, source_target_pairs={{0,32},{32,64},{64,96},{96,128},{128,160},{160,192},{192,224},{224... | collective-permute-start | bytes 49160 | tf_op jit(solution)/shard_map/ppermute | solution.py:450
  108.8 0.3 apply_same.5.before_ref
  109.1 0.0 collective-permute-done.7
  109.1 2.0 %collective-permute-done.6 = f32[2,4,4,128]{3,2,1,0:T(4,128)S(1)} collective-permute-done((f32[2,4,4,128]{3,2,1,0:T(4,128)S(1)}, f32[2,4,4,128]{3,2,1,0:T(4,128)S(1)}, u32[]{:S(2)}, u32[]{:S(2)}) %collective-permute-start.6) | collective-permute-done | bytes 16416 | tf_op jit(solution)/shard_map/ppermute | solution.py:450
  111.1 1.1 apply_side3.1
  112.2 11.9 %all_to_all.34 = f32[32,1,128]{2,1,0:T(1,128)S(1)} all-to-all(f32[32,1,128]{2,1,0:T(1,128)S(1)} %broadcast_in_dim.42), channel_id=1, replica_groups=mesh['gx'=16,'gy'=8,'gz'=4] {'gy','gz'}, dimensions={0} | all-to-all | bytes 32768 | tf_op jit(solution)/shard_map/all_to_all | solution.py:455
  124.2 16.6 %all_to_all.35 = f32[16,1,128]{2,1,0:T(1,128)S(1)} all-to-all(f32[16,1,128]{2,1,0:T(1,128)S(1)} %broadcast_in_dim.43), channel_id=1, replica_groups=mesh['gx'=16,'gy'=8,'gz'=4] {'gx'}, dimensions={0} | all-to-all | bytes 16384 | tf_op jit(solution)/shard_map/all_to_all | solution.py:455
  140.8 0.8 finish.1
  (38 shorter events, 0.4 us)
Async XLA Ops:
  24.5 14.7 %collective-permute-start.1 = (f32[4,4,8,128]{3,2,1,0:T(8,128)S(1)}, f32[4,4,8,128]{3,2,1,0:T(8,128)S(1)}, u32[]{:S(2)}, u32[]{:S(2)}) collective-permute-start(f32[4,4,8,128]{3,2,1,0:T(8,128)S(1)} %pad_maximum_fusion.1), channel_id=1, source_target_pairs={{0,480},{32,0},{64,32},{96,64},{128,96},{160,128},{192,160},{224,1... | collective-permute-start | bytes 196616 | tf_op jit(solution)/shard_map/ppermute | solution.py:450
  33.7 6.2 %collective-permute-start = (f32[4,4,8,128]{3,2,1,0:T(8,128)S(1)}, f32[4,4,8,128]{3,2,1,0:T(8,128)S(1)}, u32[]{:S(2)}, u32[]{:S(2)}) collective-permute-start(f32[4,4,8,128]{3,2,1,0:T(8,128)S(1)} %pad_maximum_fusion.1), channel_id=1, source_target_pairs={{0,32},{32,64},{64,96},{96,128},{128,160},{160,192},{192,224},{224... | collective-permute-start | bytes 196616 | tf_op jit(solution)/shard_map/ppermute | solution.py:450
  59.5 5.6 %collective-permute-start.3 = (f32[2,4,4,128]{3,2,1,0:T(4,128)S(1)}, f32[2,4,4,128]{3,2,1,0:T(4,128)S(1)}, u32[]{:S(2)}, u32[]{:S(2)}) collective-permute-start(f32[2,4,4,128]{3,2,1,0:T(4,128)S(1)} %pad_maximum_fusion.5), channel_id=1, source_target_pairs={{0,480},{32,0},{64,32},{96,64},{128,96},{160,128},{192,160},{224,1... | collective-permute-start | bytes 49160 | tf_op jit(solution)/shard_map/ppermute | solution.py:450
  62.4 5.7 %collective-permute-start.2 = (f32[2,4,4,128]{3,2,1,0:T(4,128)S(1)}, f32[2,4,4,128]{3,2,1,0:T(4,128)S(1)}, u32[]{:S(2)}, u32[]{:S(2)}) collective-permute-start(f32[2,4,4,128]{3,2,1,0:T(4,128)S(1)} %pad_maximum_fusion.5), channel_id=1, source_target_pairs={{0,32},{32,64},{64,96},{96,128},{128,160},{160,192},{192,224},{224... | collective-permute-start | bytes 49160 | tf_op jit(solution)/shard_map/ppermute | solution.py:450
  82.1 5.6 %collective-permute-start.5 = (f32[2,4,4,128]{3,2,1,0:T(4,128)S(1)}, f32[2,4,4,128]{3,2,1,0:T(4,128)S(1)}, u32[]{:S(2)}, u32[]{:S(2)}) collective-permute-start(f32[2,4,4,128]{3,2,1,0:T(4,128)S(1)} %pad_maximum_fusion.6), channel_id=1, source_target_pairs={{0,480},{32,0},{64,32},{96,64},{128,96},{160,128},{192,160},{224,1... | collective-permute-start | bytes 49160 | tf_op jit(solution)/shard_map/ppermute | solution.py:450
  84.1 5.7 %collective-permute-start.4 = (f32[2,4,4,128]{3,2,1,0:T(4,128)S(1)}, f32[2,4,4,128]{3,2,1,0:T(4,128)S(1)}, u32[]{:S(2)}, u32[]{:S(2)}) collective-permute-start(f32[2,4,4,128]{3,2,1,0:T(4,128)S(1)} %pad_maximum_fusion.6), channel_id=1, source_target_pairs={{0,32},{32,64},{64,96},{96,128},{128,160},{160,192},{192,224},{224... | collective-permute-start | bytes 49160 | tf_op jit(solution)/shard_map/ppermute | solution.py:450
  103.5 5.6 %collective-permute-start.7 = (f32[2,4,4,128]{3,2,1,0:T(4,128)S(1)}, f32[2,4,4,128]{3,2,1,0:T(4,128)S(1)}, u32[]{:S(2)}, u32[]{:S(2)}) collective-permute-start(f32[2,4,4,128]{3,2,1,0:T(4,128)S(1)} %pad_maximum_fusion.7), channel_id=1, source_target_pairs={{0,480},{32,0},{64,32},{96,64},{128,96},{160,128},{192,160},{224,1... | collective-permute-start | bytes 49160 | tf_op jit(solution)/shard_map/ppermute | solution.py:450
  105.4 5.7 %collective-permute-start.6 = (f32[2,4,4,128]{3,2,1,0:T(4,128)S(1)}, f32[2,4,4,128]{3,2,1,0:T(4,128)S(1)}, u32[]{:S(2)}, u32[]{:S(2)}) collective-permute-start(f32[2,4,4,128]{3,2,1,0:T(4,128)S(1)} %pad_maximum_fusion.7), channel_id=1, source_target_pairs={{0,32},{32,64},{64,96},{96,128},{128,160},{160,192},{192,224},{224... | collective-permute-start | bytes 49160 | tf_op jit(solution)/shard_map/ppermute | solution.py:450

commit v5 on v4

--- a/solution.py
+++ b/solution.py
@@ -87,14 +87,13 @@
             rows.append(flags)
             rows.append(hard_ref[0, y, z : z + 1])
             block = jnp.concatenate(rows, axis=0)
-            for copy in range(packed_ref.shape[0]):
-                packed_ref[copy, cell] = block
-
-
-def run_pack(count, order, *inputs):
+            packed_ref[cell] = block
+
+
+def run_pack(order, *inputs):
     return pl.pallas_call(
         pack_kernel,
-        out_shape=jax.ShapeDtypeStruct((count, 4, 8, 128), jnp.float32),
+        out_shape=jax.ShapeDtypeStruct((4, 8, 128), jnp.float32),
         in_specs=[SMEM] + [pl.BlockSpec(memory_space=pltpu.HBM)] * 6,
         out_specs=VMEM,
         scratch_shapes=[pltpu.VMEM(value.shape, value.dtype) for value in inputs]
@@ -124,7 +123,8 @@
     for own, cell in enumerate(OWN):
         y, z = own // 2, own % 2
         for number, offset in enumerate(offsets):
-            row = rows[neighbor(offset) + y * 4 + z, 0]
+            place = neighbor(offset) + y * 4 + z
+            row = rows[place, 0] + (1.0 + rows[place, 5]) * 100.0
             if offset in CODES:
                 flag = own_ref[cell, 6:7, CODES[offset] : CODES[offset] + 1]
             elif offset == (0, 0, 0):
@@ -164,8 +164,8 @@
                 keep = keep & (sub + chunk * 8 != lane)
             value = jnp.where(keep, value, 0.0)
             tiles_ref[(own * size + number) * 16 + chunk] = value
-            for system in range(2):
-                sums[system] = sums[system] + value * rows[cell, 4 + system]
+            sums[0] = sums[0] + value * rows[cell, 4]
+            sums[1] = sums[1] - value
         for system in range(2):
             total[(system * 4 + own) * 16 + chunk] = sums[system]
 
@@ -482,14 +482,22 @@
     return block, shifted(block, "gx", 1), shifted(block, "gx", -1)
 
 
+def exchange_cells(value, places):
+    below = shifted(value[1:2], "gy", 1)
+    above = shifted(value[0:1], "gy", -1)
+    value = jnp.concatenate([below, value, above], axis=0)
+    block = around(spread_all(value, "gz", lax.axis_size("gz")), places[3:6], 2)
+    return block, shifted(block, "gx", 1), shifted(block, "gx", -1)
+
+
 def shards(frac_positions, shielding, hardness, electroneg, counts, neighbor_list):
     count_x, count_y, count_z = [lax.axis_size(axis) for axis in ("gx", "gy", "gz")]
     places = frac_positions.transpose(0, 1, 3, 2, 4)
     count = count_y * count_z
     indices = lax.optimization_barrier(wrapped("gy") + wrapped("gz"))
     order = sum(indices[1:], indices[0]).astype(jnp.int32).reshape(1)
-    packed = run_pack(count, order, places, shielding, hardness, electroneg, counts, neighbor_list)
-    layers = exchange(packed.reshape(count, 2, 2, 8, 128), 0, indices)
+    packed = run_pack(order, places, shielding, hardness, electroneg, counts, neighbor_list)
+    layers = exchange_cells(packed.reshape(2, 2, 8, 128), indices)
     own, lower, upper = [layer.reshape(16, 8, 128) for layer in layers]
     tiles_same, cols, total, w0, aux = run_same(own)
     tiles_side, w1 = run_side(own, lower, upper, cols, total, w0, aux)

time: 142 us -> 140 us (0.986)
  blocking collectives: 89.1 us -> 76.2 us
  starting transfers between devices: 27 us -> 35.3 us
    all_to_all x4 -> x3, blocking collectives: 60.6 us -> 40.4 us  [exchange(): every = lax.all_to_all(sent, ('gy', 'gz'), 0, 0)]
    ppermute x8 -> x10, starting transfers between devices: 27 us -> 35.3 us  [shifted(): return lax.ppermute(value, axis, pairs)]
    all_to_all x2 -> x3, blocking collectives: 28.5 us -> 35.8 us  [spread_all(): return lax.all_to_all(sent, axes, 0, 0)]
    ppermute x8 -> x10, waiting for transfers between devices: 7.84 us -> 8.65 us  [shifted(): return lax.ppermute(value, axis, pairs)]
  transfers between devices with their start and end apart: 8 -> 10, of which waited for: 4 -> 6; matrix products, arithmetic and copies ran while one was open for 0% -> 0% of each run, Pallas kernels for 3% -> 3%
where the time goes in v5:
time: 140 us; the launch traced here: 139 us
  blocking collectives  76.2 us (54%)
  starting transfers between devices  35.3 us (25%)
  Pallas kernels  16 us (11%)
  waiting for transfers between devices  8.65 us (6%)
    all_to_all x3, blocking collectives, exchange(): every = lax.all_to_all(sent, ('gy', 'gz'), 0, 0)  40.4 us
    all_to_all x3, blocking collectives, spread_all(): return lax.all_to_all(sent, axes, 0, 0)  35.8 us
    ppermute x10, starting transfers between devices, shifted(): return lax.ppermute(value, axis, pairs)  35.3 us
    ppermute x10, waiting for transfers between devices, shifted(): return lax.ppermute(value, axis, pairs)  8.65 us
    pallas_call x1, Pallas kernels, run_side(): pl.pallas_call(side_kernel, out_shape=(SHAPE((72 * 16, 8, 128)), SHAPE((8...  6.07 us
    pallas_call x1, Pallas kernels, run_same(): pl.pallas_call(same_kernel, out_shape=(SHAPE((36 * 16, 8, 128)), SHAPE((2...  3.56 us
    pallas_call x3, Pallas kernels, run_apply_side(): pl.pallas_call(functools.partial(apply_side_kernel, step, last), out_shap...  3.04 us
  transfers between devices with their start and end apart: 10, of which 6 were waited for; matrix products, arithmetic and copies ran while one was open for 0% of the time, Pallas kernels for 3%

profile of v5, /device:TPU:1, one launch (start us, length us, event | category | flops | bytes accessed | tf_op | source)
XLA Modules:
  0.0 138.9 jit_solution(12899941171595068890)
XLA Ops:
  0.7 1.6 %pack.1 = f32[4,8,128]{2,1,0:T(8,128)} custom-call(s32[1]{0:T(128)} %bitcast.order_ref, f32[1,2,3,2,128]{4,3,2,1,0:T(2,128)} %bitcast.93, f32[1,2,2,128]{3,2,1,0:T(2,128)} %refs_1_.1, f32[1,2,2,128]{3,2,1,0:T(2,128)} %refs_2_.1, f32[1,2,2,128]{3,2,1,0:T(2,128)} %refs_3_.1, s32[1,2,2]{2,1,0:T(2,128)} %refs_4_.1, s32[1,2,2,13]{3,2,1,0:T(2,128)} %refs_5_.1), custom_call_target="tpu_custom_call" | custom-call | tf_op jit(solution)/shard_map/pack/pallas_call | solution.py:94
  2.3 0.7 slice_bitcast_fusion.1
  3.0 2.7 %collective-permute-start = (f32[1,2,8,128]{3,2,1,0:T(8,128)S(1)}, f32[1,2,8,128]{3,2,1,0:T(8,128)S(1)}, u32[]{:S(2)}, u32[]{:S(2)}) collective-permute-start(f32[1,2,8,128]{3,2,1,0:T(8,128)S(1)} %get-tuple-element.53), channel_id=1, source_target_pairs={{0,4},{4,8},{8,12},{12,16},{16,20},{20,24},{24,28},{28,0},{1,5},{5... | collective-permute-start | bytes 24584 | tf_op jit(solution)/shard_map/ppermute | solution.py:450
  5.7 4.2 %collective-permute-start.1 = (f32[1,2,8,128]{3,2,1,0:T(8,128)S(1)}, f32[1,2,8,128]{3,2,1,0:T(8,128)S(1)}, u32[]{:S(2)}, u32[]{:S(2)}) collective-permute-start(f32[1,2,8,128]{3,2,1,0:T(8,128)S(1)} %get-tuple-element.54), channel_id=1, source_target_pairs={{0,28},{4,0},{8,4},{12,8},{16,12},{20,16},{24,20},{28,24},{1,29},{... | collective-permute-start | bytes 24584 | tf_op jit(solution)/shard_map/ppermute | solution.py:450
  9.9 0.7 collective-permute-done
  10.7 0.7 pad_maximum_fusion.1
  11.4 7.2 %all_to_all.30 = f32[4,4,2,8,128]{4,3,2,1,0:T(8,128)S(1)} all-to-all(f32[4,4,2,8,128]{4,3,2,1,0:T(8,128)S(1)} %broadcast_in_dim.20), channel_id=1, replica_groups=mesh['gx'=16,'gy'=8,'gz'=4] {'gz'}, dimensions={0} | all-to-all | bytes 262144 | tf_op jit(solution)/shard_map/all_to_all | solution.py:455
  18.7 10.6 %collective-permute-start.3 = (f32[4,4,8,128]{3,2,1,0:T(8,128)S(1)}, f32[4,4,8,128]{3,2,1,0:T(8,128)S(1)}, u32[]{:S(2)}, u32[]{:S(2)}) collective-permute-start(f32[4,4,8,128]{3,2,1,0:T(8,128)S(1)} %pad_maximum_fusion), channel_id=1, source_target_pairs={{0,480},{32,0},{64,32},{96,64},{128,96},{160,128},{192,160},{224,1... | collective-permute-start | bytes 196616 | tf_op jit(solution)/shard_map/ppermute | solution.py:450
  29.3 1.9 %collective-permute-start.2 = (f32[4,4,8,128]{3,2,1,0:T(8,128)S(1)}, f32[4,4,8,128]{3,2,1,0:T(8,128)S(1)}, u32[]{:S(2)}, u32[]{:S(2)}) collective-permute-start(f32[4,4,8,128]{3,2,1,0:T(8,128)S(1)} %pad_maximum_fusion), channel_id=1, source_target_pairs={{0,32},{32,64},{64,96},{96,128},{128,160},{160,192},{192,224},{224... | collective-permute-start | bytes 196616 | tf_op jit(solution)/shard_map/ppermute | solution.py:450
  31.2 3.6 %tiles_same.1 = (f32[576,8,128]{2,1,0:T(8,128)S(1)}, f32[256,8,128]{2,1,0:T(8,128)S(1)}, f32[128,8,128]{2,1,0:T(8,128)S(1)}, f32[8,128]{1,0:T(8,128)S(1)}, f32[16,128]{1,0:T(8,128)S(1)}) custom-call(f32[16,8,128]{2,1,0:T(8,128)S(1)} %bitcast.70), custom_call_target="tpu_custom_call" | custom-call | flops 23592960 | bytes 4194304 | tf_op jit(solution)/shard_map/tiles_same/pallas_call | solution.py:217
  34.8 0.7 collective-permute-done.2
  35.5 6.1 %tiles_side.1 = (f32[1152,8,128]{2,1,0:T(8,128)S(1)}, f32[8,128]{1,0:T(8,128)S(1)}) custom-call(f32[16,8,128]{2,1,0:T(8,128)S(1)} %bitcast.71, f32[16,8,128]{2,1,0:T(8,128)S(1)} %bitcast.75, f32[16,8,128]{2,1,0:T(8,128)S(1)} %bitcast.74, f32[256,8,128]{2,1,0:T(8,128)S(1)} %get-tuple-element.23.cols_ref, f32[128,8,128]{2,1,0:T(8,128)S(1)} %get-tuple-element.24.before_ref, ...), custom_call_target="tpu_custom_call" | custom-call | flops 47185920 | bytes 4194304 | tf_op jit(solution)/shard_map/tiles_side/pallas_call | solution.py:239
  41.6 14.9 %all_to_all.31 = f32[32,2,2,2,128]{4,3,2,1,0:T(2,128)S(1)} all-to-all(f32[32,2,2,2,128]{4,3,2,1,0:T(2,128)S(1)} %broadcast_in_dim.43), channel_id=1, replica_groups=mesh['gx'=16,'gy'=8,'gz'=4] {'gy','gz'}, dimensions={0} | all-to-all | bytes 262144 | tf_op jit(solution)/shard_map/all_to_all | solution.py:478
  56.7 3.0 %collective-permute-start.5 = (f32[2,4,4,128]{3,2,1,0:T(4,128)S(1)}, f32[2,4,4,128]{3,2,1,0:T(4,128)S(1)}, u32[]{:S(2)}, u32[]{:S(2)}) collective-permute-start(f32[2,4,4,128]{3,2,1,0:T(4,128)S(1)} %pad_maximum_fusion.5), channel_id=1, source_target_pairs={{0,480},{32,0},{64,32},{96,64},{128,96},{160,128},{192,160},{224,1... | collective-permute-start | bytes 49160 | tf_op jit(solution)/shard_map/ppermute | solution.py:450
  59.7 2.3 %collective-permute-start.4 = (f32[2,4,4,128]{3,2,1,0:T(4,128)S(1)}, f32[2,4,4,128]{3,2,1,0:T(4,128)S(1)}, u32[]{:S(2)}, u32[]{:S(2)}) collective-permute-start(f32[2,4,4,128]{3,2,1,0:T(4,128)S(1)} %pad_maximum_fusion.5), channel_id=1, source_target_pairs={{0,32},{32,64},{64,96},{96,128},{128,160},{160,192},{192,224},{224... | collective-permute-start | bytes 49160 | tf_op jit(solution)/shard_map/ppermute | solution.py:450
  62.0 0.3 apply_same.3.before_ref
  62.3 3.1 %collective-permute-done.4 = f32[2,4,4,128]{3,2,1,0:T(4,128)S(1)} collective-permute-done((f32[2,4,4,128]{3,2,1,0:T(4,128)S(1)}, f32[2,4,4,128]{3,2,1,0:T(4,128)S(1)}, u32[]{:S(2)}, u32[]{:S(2)}) %collective-permute-start.4) | collective-permute-done | bytes 16416 | tf_op jit(solution)/shard_map/ppermute | solution.py:450
  65.4 1.0 apply_side1.1.refs_2_.w2
  66.4 12.9 %all_to_all.32 = f32[32,2,2,2,128]{4,3,2,1,0:T(2,128)S(1)} all-to-all(f32[32,2,2,2,128]{4,3,2,1,0:T(2,128)S(1)} %broadcast_in_dim.45), channel_id=1, replica_groups=mesh['gx'=16,'gy'=8,'gz'=4] {'gy','gz'}, dimensions={0} | all-to-all | bytes 262144 | tf_op jit(solution)/shard_map/all_to_all | solution.py:478
  79.4 1.9 %collective-permute-start.7 = (f32[2,4,4,128]{3,2,1,0:T(4,128)S(1)}, f32[2,4,4,128]{3,2,1,0:T(4,128)S(1)}, u32[]{:S(2)}, u32[]{:S(2)}) collective-permute-start(f32[2,4,4,128]{3,2,1,0:T(4,128)S(1)} %pad_maximum_fusion.6), channel_id=1, source_target_pairs={{0,480},{32,0},{64,32},{96,64},{128,96},{160,128},{192,160},{224,1... | collective-permute-start | bytes 49160 | tf_op jit(solution)/shard_map/ppermute | solution.py:450
  81.4 3.4 %collective-permute-start.6 = (f32[2,4,4,128]{3,2,1,0:T(4,128)S(1)}, f32[2,4,4,128]{3,2,1,0:T(4,128)S(1)}, u32[]{:S(2)}, u32[]{:S(2)}) collective-permute-start(f32[2,4,4,128]{3,2,1,0:T(4,128)S(1)} %pad_maximum_fusion.6), channel_id=1, source_target_pairs={{0,32},{32,64},{64,96},{96,128},{128,160},{160,192},{192,224},{224... | collective-permute-start | bytes 49160 | tf_op jit(solution)/shard_map/ppermute | solution.py:450
  84.7 0.3 apply_same.4.before_ref
  85.0 2.0 %collective-permute-done.6 = f32[2,4,4,128]{3,2,1,0:T(4,128)S(1)} collective-permute-done((f32[2,4,4,128]{3,2,1,0:T(4,128)S(1)}, f32[2,4,4,128]{3,2,1,0:T(4,128)S(1)}, u32[]{:S(2)}, u32[]{:S(2)}) %collective-permute-start.6) | collective-permute-done | bytes 16416 | tf_op jit(solution)/shard_map/ppermute | solution.py:450
  87.1 1.0 apply_side2.1.refs_3_.w3
  88.1 12.6 %all_to_all.33 = f32[32,2,2,2,128]{4,3,2,1,0:T(2,128)S(1)} all-to-all(f32[32,2,2,2,128]{4,3,2,1,0:T(2,128)S(1)} %broadcast_in_dim.47), channel_id=1, replica_groups=mesh['gx'=16,'gy'=8,'gz'=4] {'gy','gz'}, dimensions={0} | all-to-all | bytes 262144 | tf_op jit(solution)/shard_map/all_to_all | solution.py:478
  100.8 1.9 %collective-permute-start.9 = (f32[2,4,4,128]{3,2,1,0:T(4,128)S(1)}, f32[2,4,4,128]{3,2,1,0:T(4,128)S(1)}, u32[]{:S(2)}, u32[]{:S(2)}) collective-permute-start(f32[2,4,4,128]{3,2,1,0:T(4,128)S(1)} %pad_maximum_fusion.7), channel_id=1, source_target_pairs={{0,480},{32,0},{64,32},{96,64},{128,96},{160,128},{192,160},{224,1... | collective-permute-start | bytes 49160 | tf_op jit(solution)/shard_map/ppermute | solution.py:450
  102.7 3.4 %collective-permute-start.8 = (f32[2,4,4,128]{3,2,1,0:T(4,128)S(1)}, f32[2,4,4,128]{3,2,1,0:T(4,128)S(1)}, u32[]{:S(2)}, u32[]{:S(2)}) collective-permute-start(f32[2,4,4,128]{3,2,1,0:T(4,128)S(1)} %pad_maximum_fusion.7), channel_id=1, source_target_pairs={{0,32},{32,64},{64,96},{96,128},{128,160},{160,192},{192,224},{224... | collective-permute-start | bytes 49160 | tf_op jit(solution)/shard_map/ppermute | solution.py:450
  106.4 2.0 %collective-permute-done.8 = f32[2,4,4,128]{3,2,1,0:T(4,128)S(1)} collective-permute-done((f32[2,4,4,128]{3,2,1,0:T(4,128)S(1)}, f32[2,4,4,128]{3,2,1,0:T(4,128)S(1)}, u32[]{:S(2)}, u32[]{:S(2)}) %collective-permute-start.8) | collective-permute-done | bytes 16416 | tf_op jit(solution)/shard_map/ppermute | solution.py:450
  108.4 1.1 apply_side3.1
  109.5 11.9 %all_to_all.34 = f32[32,1,128]{2,1,0:T(1,128)S(1)} all-to-all(f32[32,1,128]{2,1,0:T(1,128)S(1)} %broadcast_in_dim.49), channel_id=1, replica_groups=mesh['gx'=16,'gy'=8,'gz'=4] {'gy','gz'}, dimensions={0} | all-to-all | bytes 32768 | tf_op jit(solution)/shard_map/all_to_all | solution.py:455
  121.5 16.6 %all_to_all.35 = f32[16,1,128]{2,1,0:T(1,128)S(1)} all-to-all(f32[16,1,128]{2,1,0:T(1,128)S(1)} %broadcast_in_dim.50), channel_id=1, replica_groups=mesh['gx'=16,'gy'=8,'gz'=4] {'gx'}, dimensions={0} | all-to-all | bytes 16384 | tf_op jit(solution)/shard_map/all_to_all | solution.py:455
  138.1 0.8 finish.1
  (41 shorter events, 0.9 us)
Async XLA Ops:
  3.0 7.5 %collective-permute-start = (f32[1,2,8,128]{3,2,1,0:T(8,128)S(1)}, f32[1,2,8,128]{3,2,1,0:T(8,128)S(1)}, u32[]{:S(2)}, u32[]{:S(2)}) collective-permute-start(f32[1,2,8,128]{3,2,1,0:T(8,128)S(1)} %get-tuple-element.53), channel_id=1, source_target_pairs={{0,4},{4,8},{8,12},{12,16},{16,20},{20,24},{24,28},{28,0},{1,5},{5... | collective-permute-start | bytes 24584 | tf_op jit(solution)/shard_map/ppermute | solution.py:450
  5.7 5.0 %collective-permute-start.1 = (f32[1,2,8,128]{3,2,1,0:T(8,128)S(1)}, f32[1,2,8,128]{3,2,1,0:T(8,128)S(1)}, u32[]{:S(2)}, u32[]{:S(2)}) collective-permute-start(f32[1,2,8,128]{3,2,1,0:T(8,128)S(1)} %get-tuple-element.54), channel_id=1, source_target_pairs={{0,28},{4,0},{8,4},{12,8},{16,12},{20,16},{24,20},{28,24},{1,29},{... | collective-permute-start | bytes 24584 | tf_op jit(solution)/shard_map/ppermute | solution.py:450
  18.7 16.1 %collective-permute-start.3 = (f32[4,4,8,128]{3,2,1,0:T(8,128)S(1)}, f32[4,4,8,128]{3,2,1,0:T(8,128)S(1)}, u32[]{:S(2)}, u32[]{:S(2)}) collective-permute-start(f32[4,4,8,128]{3,2,1,0:T(8,128)S(1)} %pad_maximum_fusion), channel_id=1, source_target_pairs={{0,480},{32,0},{64,32},{96,64},{128,96},{160,128},{192,160},{224,1... | collective-permute-start | bytes 196616 | tf_op jit(solution)/shard_map/ppermute | solution.py:450
  29.3 6.2 %collective-permute-start.2 = (f32[4,4,8,128]{3,2,1,0:T(8,128)S(1)}, f32[4,4,8,128]{3,2,1,0:T(8,128)S(1)}, u32[]{:S(2)}, u32[]{:S(2)}) collective-permute-start(f32[4,4,8,128]{3,2,1,0:T(8,128)S(1)} %pad_maximum_fusion), channel_id=1, source_target_pairs={{0,32},{32,64},{64,96},{96,128},{128,160},{160,192},{192,224},{224... | collective-permute-start | bytes 196616 | tf_op jit(solution)/shard_map/ppermute | solution.py:450
  56.7 5.6 %collective-permute-start.5 = (f32[2,4,4,128]{3,2,1,0:T(4,128)S(1)}, f32[2,4,4,128]{3,2,1,0:T(4,128)S(1)}, u32[]{:S(2)}, u32[]{:S(2)}) collective-permute-start(f32[2,4,4,128]{3,2,1,0:T(4,128)S(1)} %pad_maximum_fusion.5), channel_id=1, source_target_pairs={{0,480},{32,0},{64,32},{96,64},{128,96},{160,128},{192,160},{224,1... | collective-permute-start | bytes 49160 | tf_op jit(solution)/shard_map/ppermute | solution.py:450
  59.7 5.7 %collective-permute-start.4 = (f32[2,4,4,128]{3,2,1,0:T(4,128)S(1)}, f32[2,4,4,128]{3,2,1,0:T(4,128)S(1)}, u32[]{:S(2)}, u32[]{:S(2)}) collective-permute-start(f32[2,4,4,128]{3,2,1,0:T(4,128)S(1)} %pad_maximum_fusion.5), channel_id=1, source_target_pairs={{0,32},{32,64},{64,96},{96,128},{128,160},{160,192},{192,224},{224... | collective-permute-start | bytes 49160 | tf_op jit(solution)/shard_map/ppermute | solution.py:450
  79.4 5.6 %collective-permute-start.7 = (f32[2,4,4,128]{3,2,1,0:T(4,128)S(1)}, f32[2,4,4,128]{3,2,1,0:T(4,128)S(1)}, u32[]{:S(2)}, u32[]{:S(2)}) collective-permute-start(f32[2,4,4,128]{3,2,1,0:T(4,128)S(1)} %pad_maximum_fusion.6), channel_id=1, source_target_pairs={{0,480},{32,0},{64,32},{96,64},{128,96},{160,128},{192,160},{224,1... | collective-permute-start | bytes 49160 | tf_op jit(solution)/shard_map/ppermute | solution.py:450
  81.4 5.7 %collective-permute-start.6 = (f32[2,4,4,128]{3,2,1,0:T(4,128)S(1)}, f32[2,4,4,128]{3,2,1,0:T(4,128)S(1)}, u32[]{:S(2)}, u32[]{:S(2)}) collective-permute-start(f32[2,4,4,128]{3,2,1,0:T(4,128)S(1)} %pad_maximum_fusion.6), channel_id=1, source_target_pairs={{0,32},{32,64},{64,96},{96,128},{128,160},{160,192},{192,224},{224... | collective-permute-start | bytes 49160 | tf_op jit(solution)/shard_map/ppermute | solution.py:450
  100.8 5.6 %collective-permute-start.9 = (f32[2,4,4,128]{3,2,1,0:T(4,128)S(1)}, f32[2,4,4,128]{3,2,1,0:T(4,128)S(1)}, u32[]{:S(2)}, u32[]{:S(2)}) collective-permute-start(f32[2,4,4,128]{3,2,1,0:T(4,128)S(1)} %pad_maximum_fusion.7), channel_id=1, source_target_pairs={{0,480},{32,0},{64,32},{96,64},{128,96},{160,128},{192,160},{224,1... | collective-permute-start | bytes 49160 | tf_op jit(solution)/shard_map/ppermute | solution.py:450
  102.7 5.7 %collective-permute-start.8 = (f32[2,4,4,128]{3,2,1,0:T(4,128)S(1)}, f32[2,4,4,128]{3,2,1,0:T(4,128)S(1)}, u32[]{:S(2)}, u32[]{:S(2)}) collective-permute-start(f32[2,4,4,128]{3,2,1,0:T(4,128)S(1)} %pad_maximum_fusion.7), channel_id=1, source_target_pairs={{0,32},{32,64},{64,96},{96,128},{128,160},{160,192},{192,224},{224... | collective-permute-start | bytes 49160 | tf_op jit(solution)/shard_map/ppermute | solution.py:450

commit v6 on v5

--- a/solution.py
+++ b/solution.py
@@ -49,7 +49,7 @@
 
 
 def next_basis(step, image, field, before, mask, hard):
-    value = image * mask + hard * field
+    value = jnp.where(mask > 0.0, image, 0.0) + hard * field
     value = (value - SHIFT[step] * field) * (1.0 / SCALE[step])
     if BACK[step]:
         value = value - BACK[step] * before
@@ -93,12 +93,12 @@
 def run_pack(order, *inputs):
     return pl.pallas_call(
         pack_kernel,
-        out_shape=jax.ShapeDtypeStruct((4, 8, 128), jnp.float32),
+        out_shape=pltpu.VMEM((4, 8, 128), jnp.float32),
         in_specs=[SMEM] + [pl.BlockSpec(memory_space=pltpu.HBM)] * 6,
         out_specs=VMEM,
         scratch_shapes=[pltpu.VMEM(value.shape, value.dtype) for value in inputs]
         + [pltpu.SemaphoreType.DMA((6,))],
-        compiler_params=pltpu.CompilerParams(vmem_limit_bytes=63 * 1024 * 1024),
+        compiler_params=pltpu.CompilerParams(vmem_limit_bytes=60 * 1024 * 1024),
         name="pack",
     )(order, *inputs)
 
@@ -137,7 +137,7 @@
             away[own * len(offsets) + number] = row
 
 
-def build_tiles(offsets, rows, cols, away, tiles_ref, before, total):
+def build_tiles(offsets, own_ref, rows, cols, away, tiles_ref, before, total):
     sub = lax.broadcasted_iota(jnp.int32, (8, 128), 0)
     lane = lax.broadcasted_iota(jnp.int32, (8, 128), 1)
     size = len(offsets)
@@ -177,7 +177,8 @@
                 body(own, base, index * 2 + part)
             return carry
 
-        lax.fori_loop(0, 8, step, 0)
+        count = jnp.sum(-own_ref[OWN[own], 5:6]).astype(jnp.int32)
+        lax.fori_loop(0, lax.shift_right_logical(count + 15, 4), step, 0)
 
 
 def same_kernel(own_ref, tiles_ref, cols_ref, total_ref, field_ref, aux_ref, rows, away):
@@ -194,14 +195,14 @@
             aux_ref[row : row + 1] = mask
             aux_ref[8 + row : 9 + row] = own_ref[cell, 7:8] * mask
     fill_away(SAME, own_ref, own_ref, rows, away)
-    build_tiles(SAME, rows, cols_ref, away, tiles_ref, None, total_ref)
+    build_tiles(SAME, own_ref, rows, cols_ref, away, tiles_ref, None, total_ref)
 
 
 def side_kernel(own_ref, lower_ref, upper_ref, cols_ref, before_ref, field_ref, aux_ref, tiles_ref, next_ref, rows, away, total, image):
     fill_rows(lower_ref, rows, 0, -1)
     fill_rows(upper_ref, rows, 16, 1)
     fill_away(SIDE, own_ref, lower_ref, rows, away)
-    build_tiles(SIDE, rows, cols_ref, away, tiles_ref, before_ref, total)
+    build_tiles(SIDE, own_ref, rows, cols_ref, away, tiles_ref, before_ref, total)
     reduce_rows(total, image)
     next_ref[...] = next_basis(0, image[...], field_ref[...], None, aux_ref[0:8], aux_ref[8:16])
 

time: 140 us -> 137 us (0.979)
  no operation moved by 1% of the time
where the time goes in v6:
time: 137 us
  blocking collectives  76.8 us (56%)
  starting transfers between devices  35.3 us (26%)
  Pallas kernels  14.7 us (11%)
  waiting for transfers between devices  8.51 us (6%)
    all_to_all x3, blocking collectives, exchange(): every = lax.all_to_all(sent, ('gy', 'gz'), 0, 0)  40.8 us
    all_to_all x3, blocking collectives, spread_all(): return lax.all_to_all(sent, axes, 0, 0)  36 us
    ppermute x10, starting transfers between devices, shifted(): return lax.ppermute(value, axis, pairs)  35.3 us
    ppermute x10, waiting for transfers between devices, shifted(): return lax.ppermute(value, axis, pairs)  8.51 us
    pallas_call x1, Pallas kernels, run_side(): pl.pallas_call(side_kernel, out_shape=(SHAPE((72 * 16, 8, 128)), SHAPE((8...  5.57 us
    pallas_call x1, Pallas kernels, run_same(): pl.pallas_call(same_kernel, out_shape=(SHAPE((36 * 16, 8, 128)), SHAPE((2...  3.44 us
    pallas_call x3, Pallas kernels, run_apply_side(): pl.pallas_call(functools.partial(apply_side_kernel, step, last), out_shap...  3.01 us
  transfers between devices with their start and end apart: 10, of which 6 were waited for; matrix products, arithmetic and copies ran while one was open for 0% of the time, Pallas kernels for 3%

profile of v6, /device:TPU:1, one launch (start us, length us, event | category | flops | bytes accessed | tf_op | source)
XLA Modules:
  0.0 136.7 jit_solution(10007309423663739029)
XLA Ops:
  0.7 1.0 pack.1
  1.7 2.7 %collective-permute-start = (f32[1,2,8,128]{3,2,1,0:T(8,128)S(1)}, f32[1,2,8,128]{3,2,1,0:T(8,128)S(1)}, u32[]{:S(2)}, u32[]{:S(2)}) collective-permute-start(f32[1,2,8,128]{3,2,1,0:T(8,128)S(1)} %get-tuple-element.53), channel_id=1, source_target_pairs={{0,4},{4,8},{8,12},{12,16},{16,20},{20,24},{24,28},{28,0},{1,5},{5... | collective-permute-start | bytes 24584 | tf_op jit(solution)/shard_map/ppermute | solution.py:451
  4.4 4.2 %collective-permute-start.1 = (f32[1,2,8,128]{3,2,1,0:T(8,128)S(1)}, f32[1,2,8,128]{3,2,1,0:T(8,128)S(1)}, u32[]{:S(2)}, u32[]{:S(2)}) collective-permute-start(f32[1,2,8,128]{3,2,1,0:T(8,128)S(1)} %get-tuple-element.54), channel_id=1, source_target_pairs={{0,28},{4,0},{8,4},{12,8},{16,12},{20,16},{24,20},{28,24},{1,29},{... | collective-permute-start | bytes 24584 | tf_op jit(solution)/shard_map/ppermute | solution.py:451
  8.6 0.6 collective-permute-done
  9.2 0.2 collective-permute-done.1
  9.4 7.2 %all_to_all.30 = f32[4,4,2,8,128]{4,3,2,1,0:T(8,128)S(1)} all-to-all(f32[4,4,2,8,128]{4,3,2,1,0:T(8,128)S(1)} %broadcast_in_dim.20), channel_id=1, replica_groups=mesh['gx'=16,'gy'=8,'gz'=4] {'gz'}, dimensions={0} | all-to-all | bytes 262144 | tf_op jit(solution)/shard_map/all_to_all | solution.py:456
  16.7 10.6 %collective-permute-start.3 = (f32[4,4,8,128]{3,2,1,0:T(8,128)S(1)}, f32[4,4,8,128]{3,2,1,0:T(8,128)S(1)}, u32[]{:S(2)}, u32[]{:S(2)}) collective-permute-start(f32[4,4,8,128]{3,2,1,0:T(8,128)S(1)} %pad_maximum_fusion), channel_id=1, source_target_pairs={{0,480},{32,0},{64,32},{96,64},{128,96},{160,128},{192,160},{224,1... | collective-permute-start | bytes 196616 | tf_op jit(solution)/shard_map/ppermute | solution.py:451
  27.3 1.9 %collective-permute-start.2 = (f32[4,4,8,128]{3,2,1,0:T(8,128)S(1)}, f32[4,4,8,128]{3,2,1,0:T(8,128)S(1)}, u32[]{:S(2)}, u32[]{:S(2)}) collective-permute-start(f32[4,4,8,128]{3,2,1,0:T(8,128)S(1)} %pad_maximum_fusion), channel_id=1, source_target_pairs={{0,32},{32,64},{64,96},{96,128},{128,160},{160,192},{192,224},{224... | collective-permute-start | bytes 196616 | tf_op jit(solution)/shard_map/ppermute | solution.py:451
  29.2 3.4 %tiles_same.1 = (f32[576,8,128]{2,1,0:T(8,128)S(1)}, f32[256,8,128]{2,1,0:T(8,128)S(1)}, f32[128,8,128]{2,1,0:T(8,128)S(1)}, f32[8,128]{1,0:T(8,128)S(1)}, f32[16,128]{1,0:T(8,128)S(1)}) custom-call(f32[16,8,128]{2,1,0:T(8,128)S(1)} %bitcast.70), custom_call_target="tpu_custom_call" | custom-call | flops 23592960 | bytes 4194304 | tf_op jit(solution)/shard_map/tiles_same/pallas_call | solution.py:218
  32.7 0.8 collective-permute-done.2
  33.5 5.6 %tiles_side.1 = (f32[1152,8,128]{2,1,0:T(8,128)S(1)}, f32[8,128]{1,0:T(8,128)S(1)}) custom-call(f32[16,8,128]{2,1,0:T(8,128)S(1)} %bitcast.71, f32[16,8,128]{2,1,0:T(8,128)S(1)} %bitcast.76, f32[16,8,128]{2,1,0:T(8,128)S(1)} %bitcast.75, f32[256,8,128]{2,1,0:T(8,128)S(1)} %get-tuple-element.23.cols_ref, f32[128,8,128]{2,1,0:T(8,128)S(1)} %get-tuple-element.24.before_ref, ...), custom_call_target="tpu_custom_call" | custom-call | flops 47185920 | bytes 4194304 | tf_op jit(solution)/shard_map/tiles_side/pallas_call | solution.py:240
  39.1 15.3 %all_to_all.31 = f32[32,2,2,2,128]{4,3,2,1,0:T(2,128)S(1)} all-to-all(f32[32,2,2,2,128]{4,3,2,1,0:T(2,128)S(1)} %broadcast_in_dim.43), channel_id=1, replica_groups=mesh['gx'=16,'gy'=8,'gz'=4] {'gy','gz'}, dimensions={0} | all-to-all | bytes 262144 | tf_op jit(solution)/shard_map/all_to_all | solution.py:479
  54.6 2.7 %collective-permute-start.5 = (f32[2,4,4,128]{3,2,1,0:T(4,128)S(1)}, f32[2,4,4,128]{3,2,1,0:T(4,128)S(1)}, u32[]{:S(2)}, u32[]{:S(2)}) collective-permute-start(f32[2,4,4,128]{3,2,1,0:T(4,128)S(1)} %pad_maximum_fusion.5), channel_id=1, source_target_pairs={{0,480},{32,0},{64,32},{96,64},{128,96},{160,128},{192,160},{224,1... | collective-permute-start | bytes 49160 | tf_op jit(solution)/shard_map/ppermute | solution.py:451
  57.3 2.6 %collective-permute-start.4 = (f32[2,4,4,128]{3,2,1,0:T(4,128)S(1)}, f32[2,4,4,128]{3,2,1,0:T(4,128)S(1)}, u32[]{:S(2)}, u32[]{:S(2)}) collective-permute-start(f32[2,4,4,128]{3,2,1,0:T(4,128)S(1)} %pad_maximum_fusion.5), channel_id=1, source_target_pairs={{0,32},{32,64},{64,96},{96,128},{128,160},{160,192},{192,224},{224... | collective-permute-start | bytes 49160 | tf_op jit(solution)/shard_map/ppermute | solution.py:451
  59.9 0.3 apply_same.3.before_ref
  60.2 2.8 %collective-permute-done.4 = f32[2,4,4,128]{3,2,1,0:T(4,128)S(1)} collective-permute-done((f32[2,4,4,128]{3,2,1,0:T(4,128)S(1)}, f32[2,4,4,128]{3,2,1,0:T(4,128)S(1)}, u32[]{:S(2)}, u32[]{:S(2)}) %collective-permute-start.4) | collective-permute-done | bytes 16416 | tf_op jit(solution)/shard_map/ppermute | solution.py:451
  63.0 0.9 apply_side1.1.refs_2_.w2
  64.0 12.9 %all_to_all.32 = f32[32,2,2,2,128]{4,3,2,1,0:T(2,128)S(1)} all-to-all(f32[32,2,2,2,128]{4,3,2,1,0:T(2,128)S(1)} %broadcast_in_dim.45), channel_id=1, replica_groups=mesh['gx'=16,'gy'=8,'gz'=4] {'gy','gz'}, dimensions={0} | all-to-all | bytes 262144 | tf_op jit(solution)/shard_map/all_to_all | solution.py:479
  77.0 1.9 %collective-permute-start.7 = (f32[2,4,4,128]{3,2,1,0:T(4,128)S(1)}, f32[2,4,4,128]{3,2,1,0:T(4,128)S(1)}, u32[]{:S(2)}, u32[]{:S(2)}) collective-permute-start(f32[2,4,4,128]{3,2,1,0:T(4,128)S(1)} %pad_maximum_fusion.6), channel_id=1, source_target_pairs={{0,480},{32,0},{64,32},{96,64},{128,96},{160,128},{192,160},{224,1... | collective-permute-start | bytes 49160 | tf_op jit(solution)/shard_map/ppermute | solution.py:451
  78.9 3.4 %collective-permute-start.6 = (f32[2,4,4,128]{3,2,1,0:T(4,128)S(1)}, f32[2,4,4,128]{3,2,1,0:T(4,128)S(1)}, u32[]{:S(2)}, u32[]{:S(2)}) collective-permute-start(f32[2,4,4,128]{3,2,1,0:T(4,128)S(1)} %pad_maximum_fusion.6), channel_id=1, source_target_pairs={{0,32},{32,64},{64,96},{96,128},{128,160},{160,192},{192,224},{224... | collective-permute-start | bytes 49160 | tf_op jit(solution)/shard_map/ppermute | solution.py:451
  82.3 0.3 apply_same.4.before_ref
  82.6 2.0 %collective-permute-done.6 = f32[2,4,4,128]{3,2,1,0:T(4,128)S(1)} collective-permute-done((f32[2,4,4,128]{3,2,1,0:T(4,128)S(1)}, f32[2,4,4,128]{3,2,1,0:T(4,128)S(1)}, u32[]{:S(2)}, u32[]{:S(2)}) %collective-permute-start.6) | collective-permute-done | bytes 16416 | tf_op jit(solution)/shard_map/ppermute | solution.py:451
  84.6 1.0 apply_side2.1.refs_3_.w3
  85.6 12.6 %all_to_all.33 = f32[32,2,2,2,128]{4,3,2,1,0:T(2,128)S(1)} all-to-all(f32[32,2,2,2,128]{4,3,2,1,0:T(2,128)S(1)} %broadcast_in_dim.47), channel_id=1, replica_groups=mesh['gx'=16,'gy'=8,'gz'=4] {'gy','gz'}, dimensions={0} | all-to-all | bytes 262144 | tf_op jit(solution)/shard_map/all_to_all | solution.py:479
  98.4 1.9 %collective-permute-start.9 = (f32[2,4,4,128]{3,2,1,0:T(4,128)S(1)}, f32[2,4,4,128]{3,2,1,0:T(4,128)S(1)}, u32[]{:S(2)}, u32[]{:S(2)}) collective-permute-start(f32[2,4,4,128]{3,2,1,0:T(4,128)S(1)} %pad_maximum_fusion.7), channel_id=1, source_target_pairs={{0,480},{32,0},{64,32},{96,64},{128,96},{160,128},{192,160},{224,1... | collective-permute-start | bytes 49160 | tf_op jit(solution)/shard_map/ppermute | solution.py:451
  100.3 3.4 %collective-permute-start.8 = (f32[2,4,4,128]{3,2,1,0:T(4,128)S(1)}, f32[2,4,4,128]{3,2,1,0:T(4,128)S(1)}, u32[]{:S(2)}, u32[]{:S(2)}) collective-permute-start(f32[2,4,4,128]{3,2,1,0:T(4,128)S(1)} %pad_maximum_fusion.7), channel_id=1, source_target_pairs={{0,32},{32,64},{64,96},{96,128},{128,160},{160,192},{192,224},{224... | collective-permute-start | bytes 49160 | tf_op jit(solution)/shard_map/ppermute | solution.py:451
  103.7 0.3 apply_same.5.before_ref
  104.0 2.0 %collective-permute-done.8 = f32[2,4,4,128]{3,2,1,0:T(4,128)S(1)} collective-permute-done((f32[2,4,4,128]{3,2,1,0:T(4,128)S(1)}, f32[2,4,4,128]{3,2,1,0:T(4,128)S(1)}, u32[]{:S(2)}, u32[]{:S(2)}) %collective-permute-start.8) | collective-permute-done | bytes 16416 | tf_op jit(solution)/shard_map/ppermute | solution.py:451
  106.0 1.1 apply_side3.1
  107.1 11.9 %all_to_all.34 = f32[32,1,128]{2,1,0:T(1,128)S(1)} all-to-all(f32[32,1,128]{2,1,0:T(1,128)S(1)} %broadcast_in_dim.49), channel_id=1, replica_groups=mesh['gx'=16,'gy'=8,'gz'=4] {'gy','gz'}, dimensions={0} | all-to-all | bytes 32768 | tf_op jit(solution)/shard_map/all_to_all | solution.py:456
  119.0 16.9 %all_to_all.35 = f32[16,1,128]{2,1,0:T(1,128)S(1)} all-to-all(f32[16,1,128]{2,1,0:T(1,128)S(1)} %broadcast_in_dim.50), channel_id=1, replica_groups=mesh['gx'=16,'gy'=8,'gz'=4] {'gx'}, dimensions={0} | all-to-all | bytes 16384 | tf_op jit(solution)/shard_map/all_to_all | solution.py:456
  135.9 0.8 finish.1
  (41 shorter events, 0.4 us)
Async XLA Ops:
  1.7 7.6 %collective-permute-start = (f32[1,2,8,128]{3,2,1,0:T(8,128)S(1)}, f32[1,2,8,128]{3,2,1,0:T(8,128)S(1)}, u32[]{:S(2)}, u32[]{:S(2)}) collective-permute-start(f32[1,2,8,128]{3,2,1,0:T(8,128)S(1)} %get-tuple-element.53), channel_id=1, source_target_pairs={{0,4},{4,8},{8,12},{12,16},{16,20},{20,24},{24,28},{28,0},{1,5},{5... | collective-permute-start | bytes 24584 | tf_op jit(solution)/shard_map/ppermute | solution.py:451
  4.4 5.0 %collective-permute-start.1 = (f32[1,2,8,128]{3,2,1,0:T(8,128)S(1)}, f32[1,2,8,128]{3,2,1,0:T(8,128)S(1)}, u32[]{:S(2)}, u32[]{:S(2)}) collective-permute-start(f32[1,2,8,128]{3,2,1,0:T(8,128)S(1)} %get-tuple-element.54), channel_id=1, source_target_pairs={{0,28},{4,0},{8,4},{12,8},{16,12},{20,16},{24,20},{28,24},{1,29},{... | collective-permute-start | bytes 24584 | tf_op jit(solution)/shard_map/ppermute | solution.py:451
  16.7 16.0 %collective-permute-start.3 = (f32[4,4,8,128]{3,2,1,0:T(8,128)S(1)}, f32[4,4,8,128]{3,2,1,0:T(8,128)S(1)}, u32[]{:S(2)}, u32[]{:S(2)}) collective-permute-start(f32[4,4,8,128]{3,2,1,0:T(8,128)S(1)} %pad_maximum_fusion), channel_id=1, source_target_pairs={{0,480},{32,0},{64,32},{96,64},{128,96},{160,128},{192,160},{224,1... | collective-permute-start | bytes 196616 | tf_op jit(solution)/shard_map/ppermute | solution.py:451
  27.3 6.2 %collective-permute-start.2 = (f32[4,4,8,128]{3,2,1,0:T(8,128)S(1)}, f32[4,4,8,128]{3,2,1,0:T(8,128)S(1)}, u32[]{:S(2)}, u32[]{:S(2)}) collective-permute-start(f32[4,4,8,128]{3,2,1,0:T(8,128)S(1)} %pad_maximum_fusion), channel_id=1, source_target_pairs={{0,32},{32,64},{64,96},{96,128},{128,160},{160,192},{192,224},{224... | collective-permute-start | bytes 196616 | tf_op jit(solution)/shard_map/ppermute | solution.py:451
  54.6 5.6 %collective-permute-start.5 = (f32[2,4,4,128]{3,2,1,0:T(4,128)S(1)}, f32[2,4,4,128]{3,2,1,0:T(4,128)S(1)}, u32[]{:S(2)}, u32[]{:S(2)}) collective-permute-start(f32[2,4,4,128]{3,2,1,0:T(4,128)S(1)} %pad_maximum_fusion.5), channel_id=1, source_target_pairs={{0,480},{32,0},{64,32},{96,64},{128,96},{160,128},{192,160},{224,1... | collective-permute-start | bytes 49160 | tf_op jit(solution)/shard_map/ppermute | solution.py:451
  57.3 5.7 %collective-permute-start.4 = (f32[2,4,4,128]{3,2,1,0:T(4,128)S(1)}, f32[2,4,4,128]{3,2,1,0:T(4,128)S(1)}, u32[]{:S(2)}, u32[]{:S(2)}) collective-permute-start(f32[2,4,4,128]{3,2,1,0:T(4,128)S(1)} %pad_maximum_fusion.5), channel_id=1, source_target_pairs={{0,32},{32,64},{64,96},{96,128},{128,160},{160,192},{192,224},{224... | collective-permute-start | bytes 49160 | tf_op jit(solution)/shard_map/ppermute | solution.py:451
  77.0 5.6 %collective-permute-start.7 = (f32[2,4,4,128]{3,2,1,0:T(4,128)S(1)}, f32[2,4,4,128]{3,2,1,0:T(4,128)S(1)}, u32[]{:S(2)}, u32[]{:S(2)}) collective-permute-start(f32[2,4,4,128]{3,2,1,0:T(4,128)S(1)} %pad_maximum_fusion.6), channel_id=1, source_target_pairs={{0,480},{32,0},{64,32},{96,64},{128,96},{160,128},{192,160},{224,1... | collective-permute-start | bytes 49160 | tf_op jit(solution)/shard_map/ppermute | solution.py:451
  78.9 5.7 %collective-permute-start.6 = (f32[2,4,4,128]{3,2,1,0:T(4,128)S(1)}, f32[2,4,4,128]{3,2,1,0:T(4,128)S(1)}, u32[]{:S(2)}, u32[]{:S(2)}) collective-permute-start(f32[2,4,4,128]{3,2,1,0:T(4,128)S(1)} %pad_maximum_fusion.6), channel_id=1, source_target_pairs={{0,32},{32,64},{64,96},{96,128},{128,160},{160,192},{192,224},{224... | collective-permute-start | bytes 49160 | tf_op jit(solution)/shard_map/ppermute | solution.py:451
  98.4 5.6 %collective-permute-start.9 = (f32[2,4,4,128]{3,2,1,0:T(4,128)S(1)}, f32[2,4,4,128]{3,2,1,0:T(4,128)S(1)}, u32[]{:S(2)}, u32[]{:S(2)}) collective-permute-start(f32[2,4,4,128]{3,2,1,0:T(4,128)S(1)} %pad_maximum_fusion.7), channel_id=1, source_target_pairs={{0,480},{32,0},{64,32},{96,64},{128,96},{160,128},{192,160},{224,1... | collective-permute-start | bytes 49160 | tf_op jit(solution)/shard_map/ppermute | solution.py:451
  100.3 5.7 %collective-permute-start.8 = (f32[2,4,4,128]{3,2,1,0:T(4,128)S(1)}, f32[2,4,4,128]{3,2,1,0:T(4,128)S(1)}, u32[]{:S(2)}, u32[]{:S(2)}) collective-permute-start(f32[2,4,4,128]{3,2,1,0:T(4,128)S(1)} %pad_maximum_fusion.7), channel_id=1, source_target_pairs={{0,32},{32,64},{64,96},{96,128},{128,160},{160,192},{192,224},{224... | collective-permute-start | bytes 49160 | tf_op jit(solution)/shard_map/ppermute | solution.py:451

commit v7 on v6

--- a/solution.py
+++ b/solution.py
@@ -27,7 +27,7 @@
 SHIFT = (220.0, 110.0, 145.0, 140.0)
 SCALE = (60.0, 70.0, 70.0, 70.0)
 BACK = (0.0, 0.7, 1.0, 1.0)
-PAIRS = [(i, j) for i in range(4) for j in range(i, 5)]
+PAIRS = [(i, j) for i in range(4) for j in range(i, 4)]
 VMEM = pl.BlockSpec(memory_space=pltpu.VMEM)
 SMEM = pl.BlockSpec(memory_space=pltpu.SMEM)
 PARAMS = pltpu.CompilerParams(vmem_limit_bytes=24 * 1024 * 1024)
@@ -36,6 +36,7 @@
 OWN = [(1 + y) * 4 + 1 + z for y in range(2) for z in range(2)]
 SAME = [offset for offset in SHELL if offset[0] == 0]
 SIDE = [offset for offset in SHELL if offset[0] != 0]
+LOWER, UPPER = SIDE[:9], SIDE[9:]
 
 
 def spread(row):
@@ -254,8 +255,8 @@
     )(*inputs)
 
 
-def gram_row(fields):
-    entries = [fields[i] * fields[j] for i, j in PAIRS] + fields[:4]
+def gram_row(fields, image):
+    entries = [fields[i] * fields[j] for i, j in PAIRS] + [fields[3] * image] + fields
     lane = lax.broadcasted_iota(jnp.int32, (1, 128), 1)
     row = jnp.zeros((1, 128), jnp.float32)
     for number, entry in enumerate(entries):
@@ -273,8 +274,7 @@
             rows[(first + cell) * 2 + system] = spread(halo_ref[row : row + 1])
 
 
-def apply_tiles(offsets, tiles_ref, rows, before, total):
-    size = len(offsets)
+def apply_tiles(offsets, size, first, tiles_ref, rows, before, total):
 
     for own in range(4):
         base = (own // 2) * 4 + own % 2
@@ -288,7 +288,7 @@
                 cell = base + neighbor(offset)
                 right = [rows[cell * 2 + system] for system in range(2)]
                 for part in range(4):
-                    tile = tiles_ref[(own * size + number) * 16 + group * 4 + part]
+                    tile = tiles_ref[(own * size + first + number) * 16 + group * 4 + part]
                     for system in range(2):
                         term = tile * right[system]
                         held = sums[system][part]
@@ -300,24 +300,30 @@
 
 def apply_same_kernel(tiles_ref, halo_ref, total_ref, rows):
     fill_fields(halo_ref, rows, 0)
-    apply_tiles(SAME, tiles_ref, rows, None, total_ref)
-
-
-def apply_side_kernel(step, last, tiles_ref, lower_ref, upper_ref, before_ref, aux_ref, *refs):
-    count = step + 1
-    fields, next_ref, rest = refs[:count], refs[count], refs[count + 1 :]
-    if last:
-        gram_ref, rest = rest[0], rest[1:]
-    rows, total, image = rest
+    apply_tiles(SAME, 9, 0, tiles_ref, rows, None, total_ref)
+
+
+def apply_side_kernel(step, tiles_ref, lower_ref, upper_ref, before_ref, aux_ref, *refs):
+    fields, (next_ref, rows, total, image) = refs[: step + 1], refs[step + 1 :]
     fill_fields(lower_ref, rows, 0)
     fill_fields(upper_ref, rows, 16)
-    apply_tiles(SIDE, tiles_ref, rows, before_ref, total)
+    apply_tiles(SIDE, 18, 0, tiles_ref, rows, before_ref, total)
     reduce_rows(total, image)
-    values = [field[...] for field in fields]
-    new = next_basis(step, image[...], values[-1], values[-2], aux_ref[0:8], aux_ref[8:16])
-    next_ref[...] = new
-    if last:
-        gram_ref[...] = gram_row(values + [new])
+    before, field = fields[step - 1][...], fields[step][...]
+    next_ref[...] = next_basis(step, image[...], field, before, aux_ref[0:8], aux_ref[8:16])
+
+
+def apply_upper_kernel(tiles_ref, upper_ref, before_ref, aux_ref, *refs):
+    fields, (total_ref, gram_ref, rows, total, image) = [ref[...] for ref in refs[:4]], refs[4:]
+    fill_fields(upper_ref, rows, 16)
+    apply_tiles(UPPER, 18, 9, tiles_ref, rows, None, total)
+    part = total[...]
+    both = before_ref[...] + part
+    total_ref[...] = both
+    total[...] = both + part
+    reduce_rows(total, image)
+    value = jnp.where(aux_ref[0:8] > 0.0, image[...], 0.0) + aux_ref[8:16] * fields[3]
+    gram_ref[...] = gram_row(fields, value)
 
 
 def run_apply_same(tiles, halo):
@@ -333,22 +339,37 @@
     )(tiles, halo)
 
 
-def run_apply_side(step, last, tiles, lower, upper, before, aux, fields):
-    outs = (SHAPE((8, 128)), SHAPE((1, 128))) if last else (SHAPE((8, 128)),)
-    return pl.pallas_call(
-        functools.partial(apply_side_kernel, step, last),
-        out_shape=outs,
+SCRATCH = [
+    pltpu.VMEM((64, 8, 128), jnp.float32),
+    pltpu.VMEM((128, 8, 128), jnp.float32),
+    pltpu.VMEM((8, 128), jnp.float32),
+]
+
+
+def run_apply_side(step, tiles, lower, upper, before, aux, fields):
+    return pl.pallas_call(
+        functools.partial(apply_side_kernel, step),
+        out_shape=SHAPE((8, 128)),
         in_specs=[VMEM] * (5 + len(fields)),
-        out_specs=tuple(VMEM for _ in outs),
-        scratch_shapes=[
-            pltpu.VMEM((64, 8, 128), jnp.float32),
-            pltpu.VMEM((128, 8, 128), jnp.float32),
-            pltpu.VMEM((8, 128), jnp.float32),
-        ],
+        out_specs=VMEM,
+        scratch_shapes=SCRATCH,
         compiler_params=PARAMS,
         cost_estimate=cost(4 * 72 * 16384),
         name=f"apply_side{step}",
     )(tiles, lower, upper, before, aux, *fields)
+
+
+def run_apply_upper(tiles, upper, before, aux, fields):
+    return pl.pallas_call(
+        apply_upper_kernel,
+        out_shape=(SHAPE((128, 8, 128)), SHAPE((1, 128))),
+        in_specs=[VMEM] * (4 + len(fields)),
+        out_specs=(VMEM, VMEM),
+        scratch_shapes=SCRATCH,
+        compiler_params=PARAMS,
+        cost_estimate=cost(4 * 36 * 16384),
+        name="apply_upper",
+    )(tiles, upper, before, aux, *fields)
 
 
 def combine(coefs, fields):
@@ -358,8 +379,12 @@
     return value
 
 
-def finish_kernel(gram_ref, w0, w1, w2, w3, w4, charges_ref, residual_ref):
-    fields = [ref[...] for ref in (w0, w1, w2, w3, w4)]
+def finish_kernel(gram_ref, tiles_ref, lower_ref, before_ref, aux_ref, *refs):
+    fields, (charges_ref, residual_ref, rows, sums, last) = [ref[...] for ref in refs[:4]], refs[4:]
+    fill_fields(lower_ref, rows, 0)
+    apply_tiles(LOWER, 18, 0, tiles_ref, rows, before_ref, sums)
+    reduce_rows(sums, last)
+    fields.append(next_basis(3, last[...], fields[3], fields[2], aux_ref[0:8], aux_ref[8:16]))
     summed = spread(jnp.sum(gram_ref[...], axis=0, keepdims=True))
     lane = lax.broadcasted_iota(jnp.int32, (8, 128), 1)
     system = lax.broadcasted_iota(jnp.int32, (8, 128), 0) // 4
@@ -371,7 +396,16 @@
     gram = {}
     for number, (i, j) in enumerate(PAIRS):
         gram[i, j] = gram[j, i] = entry(number)
-    totals = [entry(len(PAIRS) + number) for number in range(4)]
+    totals = [entry(len(PAIRS) + 1 + number) for number in range(4)]
+    for i in range(4):
+        if i == 3:
+            value = entry(len(PAIRS))
+        else:
+            value = SCALE[i] * gram[i + 1, 3] + SHIFT[i] * gram[i, 3]
+            if BACK[i]:
+                value = value + SCALE[i] * BACK[i] * gram[i - 1, 3]
+        value = (value - SHIFT[3] * gram[i, 3]) * (1.0 / SCALE[3]) - BACK[3] * gram[i, 2]
+        gram[i, 4] = gram[4, i] = value
 
     def dot(left, right):
         result = None
@@ -433,16 +467,16 @@
             residual_ref[system, 0, y] = value[row : row + 2]
 
 
-def run_finish(gathered, fields):
-    shape = functools.partial(jax.ShapeDtypeStruct, dtype=jnp.float32)
+def run_finish(gram, tiles, lower, before, aux, fields):
     return pl.pallas_call(
         finish_kernel,
-        out_shape=(shape((1, 2, 2, 128)), shape((2, 1, 2, 2, 128))),
-        in_specs=[VMEM] * 6,
+        out_shape=(SHAPE((1, 2, 2, 128)), SHAPE((2, 1, 2, 2, 128))),
+        in_specs=[VMEM] * 9,
         out_specs=(VMEM, VMEM),
+        scratch_shapes=SCRATCH,
         compiler_params=PARAMS,
         name="finish",
-    )(gathered, *fields)
+    )(gram, tiles, lower, before, aux, *fields)
 
 
 def shifted(value, axis, steps):
@@ -508,12 +542,12 @@
         layers = exchange(sent, 1, indices)
         own, lower, upper = [layer.reshape(32, 128) for layer in layers]
         total = run_apply_same(tiles_same, own)
-        outs = run_apply_side(step, step == 3, tiles_side, lower, upper, total, aux, fields)
-        fields.append(outs[0])
-    gram = outs[1]
-    gram = jnp.sum(spread_all(gram, ("gy", "gz"), count_y * count_z), axis=0)
-    gram = spread_all(gram, "gx", count_x)
-    return run_finish(gram.reshape(count_x, 128), fields)
+        if step < 3:
+            fields.append(run_apply_side(step, tiles_side, lower, upper, total, aux, fields))
+    total, gram = run_apply_upper(tiles_side, upper, total, aux, fields)
+    gram = jnp.sum(spread_all(gram, ("gy", "gz"), count), axis=0)
+    gram = spread_all(gram, "gx", count_x).reshape(count_x, 128)
+    return run_finish(gram, tiles_side, lower, total, aux, fields)
 
 
 def solution(mesh):

time: 137 us -> 137 us (level)
  blocking collectives: 76.8 us -> 59.6 us
  waiting for transfers between devices: 8.51 us -> 17.5 us
  starting transfers between devices: 35.3 us -> 41.4 us
  local copies, waits for them, and re-layouts: 0.28 us -> 3.21 us
    all_to_all x3 -> x2, blocking collectives: 36 us -> 19.1 us  [spread_all(): return lax.all_to_all(sent, axes, 0, 0)]
    all_to_all x0 -> x1, starting transfers between devices: none -> 6.13 us  [spread_all(): return lax.all_to_all(sent, axes, 0, 0)]
    all_to_all x0 -> x1, waiting for transfers between devices: none -> 5.21 us  [spread_all(): return lax.all_to_all(sent, axes, 0, 0)]
    ppermute x10, waiting for transfers between devices: 8.51 us -> 12.3 us  [shifted(): return lax.ppermute(value, axis, pairs)]
    unnamed x0 -> x4, local copies, waits for them, and re-layouts: none -> 2.34 us
  transfers between devices with their start and end apart: 10 -> 11, of which waited for: 6 -> 8; matrix products, arithmetic and copies ran while one was open for 0% -> 0% of each run, Pallas kernels for 3% -> 3%
where the time goes in v7:
time: 137 us
  blocking collectives  59.6 us (44%)
  starting transfers between devices  41.4 us (30%)
  waiting for transfers between devices  17.5 us (13%)
  Pallas kernels  14 us (10%)
  local copies, waits for them, and re-layouts  3.21 us (2%)
    all_to_all x3, blocking collectives, exchange(): every = lax.all_to_all(sent, ('gy', 'gz'), 0, 0)  40.4 us
    ppermute x10, starting transfers between devices, shifted(): return lax.ppermute(value, axis, pairs)  35.3 us
    all_to_all x2, blocking collectives, spread_all(): return lax.all_to_all(sent, axes, 0, 0)  19.1 us
    ppermute x10, waiting for transfers between devices, shifted(): return lax.ppermute(value, axis, pairs)  12.3 us
    all_to_all x1, starting transfers between devices, spread_all(): return lax.all_to_all(sent, axes, 0, 0)  6.13 us
    pallas_call x1, Pallas kernels, run_side(): pl.pallas_call(side_kernel, out_shape=(SHAPE((72 * 16, 8, 128)), SHAPE((8...  5.22 us
    all_to_all x1, waiting for transfers between devices, spread_all(): return lax.all_to_all(sent, axes, 0, 0)  5.21 us
    pallas_call x1, Pallas kernels, run_same(): pl.pallas_call(same_kernel, out_shape=(SHAPE((36 * 16, 8, 128)), SHAPE((2...  3.24 us
  transfers between devices with their start and end apart: 11, of which 8 were waited for; matrix products, arithmetic and copies ran while one was open for 0% of the time, Pallas kernels for 3%

profile of v7, /device:TPU:1, one launch (start us, length us, event | category | flops | bytes accessed | tf_op | source)
XLA Modules:
  0.0 136.8 jit_solution(520984310020274517)
XLA Ops:
  0.7 1.0 pack.1
  1.7 2.7 %collective-permute-start = (f32[1,2,8,128]{3,2,1,0:T(8,128)S(1)}, f32[1,2,8,128]{3,2,1,0:T(8,128)S(1)}, u32[]{:S(2)}, u32[]{:S(2)}) collective-permute-start(f32[1,2,8,128]{3,2,1,0:T(8,128)S(1)} %get-tuple-element.53), channel_id=1, source_target_pairs={{0,4},{4,8},{8,12},{12,16},{16,20},{20,24},{24,28},{28,0},{1,5},{5... | collective-permute-start | bytes 24584 | tf_op jit(solution)/shard_map/ppermute | solution.py:485
  4.4 4.2 %collective-permute-start.1 = (f32[1,2,8,128]{3,2,1,0:T(8,128)S(1)}, f32[1,2,8,128]{3,2,1,0:T(8,128)S(1)}, u32[]{:S(2)}, u32[]{:S(2)}) collective-permute-start(f32[1,2,8,128]{3,2,1,0:T(8,128)S(1)} %get-tuple-element.54), channel_id=1, source_target_pairs={{0,28},{4,0},{8,4},{12,8},{16,12},{20,16},{24,20},{28,24},{1,29},{... | collective-permute-start | bytes 24584 | tf_op jit(solution)/shard_map/ppermute | solution.py:485
  8.6 0.6 collective-permute-done
  9.4 7.2 %all_to_all.30 = f32[4,4,2,8,128]{4,3,2,1,0:T(8,128)S(1)} all-to-all(f32[4,4,2,8,128]{4,3,2,1,0:T(8,128)S(1)} %broadcast_in_dim.20), channel_id=1, replica_groups=mesh['gx'=16,'gy'=8,'gz'=4] {'gz'}, dimensions={0} | all-to-all | bytes 262144 | tf_op jit(solution)/shard_map/all_to_all | solution.py:490
  16.7 10.6 %collective-permute-start.3 = (f32[4,4,8,128]{3,2,1,0:T(8,128)S(1)}, f32[4,4,8,128]{3,2,1,0:T(8,128)S(1)}, u32[]{:S(2)}, u32[]{:S(2)}) collective-permute-start(f32[4,4,8,128]{3,2,1,0:T(8,128)S(1)} %pad_maximum_fusion), channel_id=1, source_target_pairs={{0,480},{32,0},{64,32},{96,64},{128,96},{160,128},{192,160},{224,1... | collective-permute-start | bytes 196616 | tf_op jit(solution)/shard_map/ppermute | solution.py:485
  27.3 1.9 %collective-permute-start.2 = (f32[4,4,8,128]{3,2,1,0:T(8,128)S(1)}, f32[4,4,8,128]{3,2,1,0:T(8,128)S(1)}, u32[]{:S(2)}, u32[]{:S(2)}) collective-permute-start(f32[4,4,8,128]{3,2,1,0:T(8,128)S(1)} %pad_maximum_fusion), channel_id=1, source_target_pairs={{0,32},{32,64},{64,96},{96,128},{128,160},{160,192},{192,224},{224... | collective-permute-start | bytes 196616 | tf_op jit(solution)/shard_map/ppermute | solution.py:485
  29.2 3.2 %tiles_same.1 = (f32[576,8,128]{2,1,0:T(8,128)S(1)}, f32[256,8,128]{2,1,0:T(8,128)S(1)}, f32[128,8,128]{2,1,0:T(8,128)S(1)}, f32[8,128]{1,0:T(8,128)S(1)}, f32[16,128]{1,0:T(8,128)S(1)}) custom-call(f32[16,8,128]{2,1,0:T(8,128)S(1)} %bitcast.70), custom_call_target="tpu_custom_call" | custom-call | flops 23592960 | bytes 4194304 | tf_op jit(solution)/shard_map/tiles_same/pallas_call | solution.py:219
  32.5 1.0 collective-permute-done.2
  33.5 5.2 %tiles_side.1 = (f32[1152,8,128]{2,1,0:T(8,128)S(1)}, f32[8,128]{1,0:T(8,128)S(1)}) custom-call(f32[16,8,128]{2,1,0:T(8,128)S(1)} %bitcast.71, f32[16,8,128]{2,1,0:T(8,128)S(1)} %bitcast.76, f32[16,8,128]{2,1,0:T(8,128)S(1)} %bitcast.75, f32[256,8,128]{2,1,0:T(8,128)S(1)} %get-tuple-element.23.cols_ref, f32[128,8,128]{2,1,0:T(8,128)S(1)} %get-tuple-element.24.before_ref, ...), custom_call_target="tpu_custom_call" | custom-call | flops 47185920 | bytes 4194304 | tf_op jit(solution)/shard_map/tiles_side/pallas_call | solution.py:241
  38.8 15.0 %all_to_all.31 = f32[32,2,2,2,128]{4,3,2,1,0:T(2,128)S(1)} all-to-all(f32[32,2,2,2,128]{4,3,2,1,0:T(2,128)S(1)} %broadcast_in_dim.43), channel_id=1, replica_groups=mesh['gx'=16,'gy'=8,'gz'=4] {'gy','gz'}, dimensions={0} | all-to-all | bytes 262144 | tf_op jit(solution)/shard_map/all_to_all | solution.py:513
  53.9 3.4 %collective-permute-start.5 = (f32[2,4,4,128]{3,2,1,0:T(4,128)S(1)}, f32[2,4,4,128]{3,2,1,0:T(4,128)S(1)}, u32[]{:S(2)}, u32[]{:S(2)}) collective-permute-start(f32[2,4,4,128]{3,2,1,0:T(4,128)S(1)} %pad_maximum_fusion.5), channel_id=1, source_target_pairs={{0,480},{32,0},{64,32},{96,64},{128,96},{160,128},{192,160},{224,1... | collective-permute-start | bytes 49160 | tf_op jit(solution)/shard_map/ppermute | solution.py:485
  57.3 1.9 %collective-permute-start.4 = (f32[2,4,4,128]{3,2,1,0:T(4,128)S(1)}, f32[2,4,4,128]{3,2,1,0:T(4,128)S(1)}, u32[]{:S(2)}, u32[]{:S(2)}) collective-permute-start(f32[2,4,4,128]{3,2,1,0:T(4,128)S(1)} %pad_maximum_fusion.5), channel_id=1, source_target_pairs={{0,32},{32,64},{64,96},{96,128},{128,160},{160,192},{192,224},{224... | collective-permute-start | bytes 49160 | tf_op jit(solution)/shard_map/ppermute | solution.py:485
  59.5 3.5 %collective-permute-done.4 = f32[2,4,4,128]{3,2,1,0:T(4,128)S(1)} collective-permute-done((f32[2,4,4,128]{3,2,1,0:T(4,128)S(1)}, f32[2,4,4,128]{3,2,1,0:T(4,128)S(1)}, u32[]{:S(2)}, u32[]{:S(2)}) %collective-permute-start.4) | collective-permute-done | bytes 16416 | tf_op jit(solution)/shard_map/ppermute | solution.py:485
  63.0 0.9 apply_side1.1.refs_2_
  64.0 12.9 %all_to_all.32 = f32[32,2,2,2,128]{4,3,2,1,0:T(2,128)S(1)} all-to-all(f32[32,2,2,2,128]{4,3,2,1,0:T(2,128)S(1)} %broadcast_in_dim.45), channel_id=1, replica_groups=mesh['gx'=16,'gy'=8,'gz'=4] {'gy','gz'}, dimensions={0} | all-to-all | bytes 262144 | tf_op jit(solution)/shard_map/all_to_all | solution.py:513
  77.0 1.9 %collective-permute-start.7 = (f32[2,4,4,128]{3,2,1,0:T(4,128)S(1)}, f32[2,4,4,128]{3,2,1,0:T(4,128)S(1)}, u32[]{:S(2)}, u32[]{:S(2)}) collective-permute-start(f32[2,4,4,128]{3,2,1,0:T(4,128)S(1)} %pad_maximum_fusion.6), channel_id=1, source_target_pairs={{0,480},{32,0},{64,32},{96,64},{128,96},{160,128},{192,160},{224,1... | collective-permute-start | bytes 49160 | tf_op jit(solution)/shard_map/ppermute | solution.py:485
  78.9 3.4 %collective-permute-start.6 = (f32[2,4,4,128]{3,2,1,0:T(4,128)S(1)}, f32[2,4,4,128]{3,2,1,0:T(4,128)S(1)}, u32[]{:S(2)}, u32[]{:S(2)}) collective-permute-start(f32[2,4,4,128]{3,2,1,0:T(4,128)S(1)} %pad_maximum_fusion.6), channel_id=1, source_target_pairs={{0,32},{32,64},{64,96},{96,128},{128,160},{160,192},{192,224},{224... | collective-permute-start | bytes 49160 | tf_op jit(solution)/shard_map/ppermute | solution.py:485
  82.6 2.0 %collective-permute-done.6 = f32[2,4,4,128]{3,2,1,0:T(4,128)S(1)} collective-permute-done((f32[2,4,4,128]{3,2,1,0:T(4,128)S(1)}, f32[2,4,4,128]{3,2,1,0:T(4,128)S(1)}, u32[]{:S(2)}, u32[]{:S(2)}) %collective-permute-start.6) | collective-permute-done | bytes 16416 | tf_op jit(solution)/shard_map/ppermute | solution.py:485
  84.6 1.0 apply_side2.1.refs_3_
  85.6 12.6 %all_to_all.33 = f32[32,2,2,2,128]{4,3,2,1,0:T(2,128)S(1)} all-to-all(f32[32,2,2,2,128]{4,3,2,1,0:T(2,128)S(1)} %broadcast_in_dim.47), channel_id=1, replica_groups=mesh['gx'=16,'gy'=8,'gz'=4] {'gy','gz'}, dimensions={0} | all-to-all | bytes 262144 | tf_op jit(solution)/shard_map/all_to_all | solution.py:513
  98.4 1.9 %collective-permute-start.8 = (f32[2,4,4,128]{3,2,1,0:T(4,128)S(1)}, f32[2,4,4,128]{3,2,1,0:T(4,128)S(1)}, u32[]{:S(2)}, u32[]{:S(2)}) collective-permute-start(f32[2,4,4,128]{3,2,1,0:T(4,128)S(1)} %pad_maximum_fusion.7), channel_id=1, source_target_pairs={{0,480},{32,0},{64,32},{96,64},{128,96},{160,128},{192,160},{224,1... | collective-permute-start | bytes 49160 | tf_op jit(solution)/shard_map/ppermute | solution.py:485
  100.6 2.2 %collective-permute-done.8 = f32[2,4,4,128]{3,2,1,0:T(4,128)S(1)} collective-permute-done((f32[2,4,4,128]{3,2,1,0:T(4,128)S(1)}, f32[2,4,4,128]{3,2,1,0:T(4,128)S(1)}, u32[]{:S(2)}, u32[]{:S(2)}) %collective-permute-start.8) | collective-permute-done | bytes 16416 | tf_op jit(solution)/shard_map/ppermute | solution.py:485
  102.8 0.6 apply_upper.1
  103.5 11.9 %all_to_all.34 = f32[32,1,128]{2,1,0:T(1,128)S(1)} all-to-all(f32[32,1,128]{2,1,0:T(1,128)S(1)} %broadcast_in_dim.49), channel_id=1, replica_groups=mesh['gx'=16,'gy'=8,'gz'=4] {'gy','gz'}, dimensions={0} | all-to-all | bytes 32768 | tf_op jit(solution)/shard_map/all_to_all | solution.py:490
  115.4 0.6 broadcast_in_dim.50
  116.0 6.1 %all-to-all-start.5 = ((f32[16,1,128]{2,1,0:T(1,128)}), f32[16,1,128]{2,1,0:T(1,128)S(1)}, u32[]{:S(2)}, u32[]{:S(2)}) async-start(f32[16,1,128]{2,1,0:T(1,128)} %broadcast_in_dim.50), calls=%async_computation.5 | async-start | bytes 16384 | tf_op jit(solution)/shard_map/all_to_all | solution.py:490
  122.1 3.3 %collective-permute-start.9 = (f32[2,4,4,128]{3,2,1,0:T(4,128)S(1)}, f32[2,4,4,128]{3,2,1,0:T(4,128)S(1)}, u32[]{:S(2)}, u32[]{:S(2)}) collective-permute-start(f32[2,4,4,128]{3,2,1,0:T(4,128)S(1)} %pad_maximum_fusion.7), channel_id=1, source_target_pairs={{0,32},{32,64},{64,96},{96,128},{128,160},{160,192},{192,224},{224... | collective-permute-start | bytes 49160 | tf_op jit(solution)/shard_map/ppermute | solution.py:485
  125.4 2.7 %collective-permute-done.9 = f32[2,4,4,128]{3,2,1,0:T(4,128)S(1)} collective-permute-done((f32[2,4,4,128]{3,2,1,0:T(4,128)S(1)}, f32[2,4,4,128]{3,2,1,0:T(4,128)S(1)}, u32[]{:S(2)}, u32[]{:S(2)}) %collective-permute-start.9) | collective-permute-done | bytes 16416 | tf_op jit(solution)/shard_map/ppermute | solution.py:485
  128.2 5.2 %all-to-all-done.5 = f32[16,1,128]{2,1,0:T(1,128)S(1)} async-done(((f32[16,1,128]{2,1,0:T(1,128)}), f32[16,1,128]{2,1,0:T(1,128)S(1)}, u32[]{:S(2)}, u32[]{:S(2)}) %all-to-all-start.5) | async-done | bytes 8224 | tf_op jit(solution)/shard_map/all_to_all | solution.py:490
  133.4 2.3 %copy-done.1 = f32[1152,8,128]{2,1,0:T(8,128)S(1)} copy-done((f32[1152,8,128]{2,1,0:T(8,128)S(1)}, f32[1152,8,128]{2,1,0:T(8,128)}, u32[]{:S(2)}) %copy-start.1) | copy-done | bytes 4718616
  135.7 1.1 finish.1
  (46 shorter events, 1.5 us)
Async XLA Ops:
  1.7 7.6 %collective-permute-start = (f32[1,2,8,128]{3,2,1,0:T(8,128)S(1)}, f32[1,2,8,128]{3,2,1,0:T(8,128)S(1)}, u32[]{:S(2)}, u32[]{:S(2)}) collective-permute-start(f32[1,2,8,128]{3,2,1,0:T(8,128)S(1)} %get-tuple-element.53), channel_id=1, source_target_pairs={{0,4},{4,8},{8,12},{12,16},{16,20},{20,24},{24,28},{28,0},{1,5},{5... | collective-permute-start | bytes 24584 | tf_op jit(solution)/shard_map/ppermute | solution.py:485
  4.4 5.0 %collective-permute-start.1 = (f32[1,2,8,128]{3,2,1,0:T(8,128)S(1)}, f32[1,2,8,128]{3,2,1,0:T(8,128)S(1)}, u32[]{:S(2)}, u32[]{:S(2)}) collective-permute-start(f32[1,2,8,128]{3,2,1,0:T(8,128)S(1)} %get-tuple-element.54), channel_id=1, source_target_pairs={{0,28},{4,0},{8,4},{12,8},{16,12},{20,16},{24,20},{28,24},{1,29},{... | collective-permute-start | bytes 24584 | tf_op jit(solution)/shard_map/ppermute | solution.py:485
  16.7 15.8 %collective-permute-start.3 = (f32[4,4,8,128]{3,2,1,0:T(8,128)S(1)}, f32[4,4,8,128]{3,2,1,0:T(8,128)S(1)}, u32[]{:S(2)}, u32[]{:S(2)}) collective-permute-start(f32[4,4,8,128]{3,2,1,0:T(8,128)S(1)} %pad_maximum_fusion), channel_id=1, source_target_pairs={{0,480},{32,0},{64,32},{96,64},{128,96},{160,128},{192,160},{224,1... | collective-permute-start | bytes 196616 | tf_op jit(solution)/shard_map/ppermute | solution.py:485
  27.3 6.2 %collective-permute-start.2 = (f32[4,4,8,128]{3,2,1,0:T(8,128)S(1)}, f32[4,4,8,128]{3,2,1,0:T(8,128)S(1)}, u32[]{:S(2)}, u32[]{:S(2)}) collective-permute-start(f32[4,4,8,128]{3,2,1,0:T(8,128)S(1)} %pad_maximum_fusion), channel_id=1, source_target_pairs={{0,32},{32,64},{64,96},{96,128},{128,160},{160,192},{192,224},{224... | collective-permute-start | bytes 196616 | tf_op jit(solution)/shard_map/ppermute | solution.py:485
  38.7 64.1 %copy-start = (f32[1152,8,128]{2,1,0:T(8,128)}, f32[1152,8,128]{2,1,0:T(8,128)S(1)}, u32[]{:S(2)}) copy-start(f32[1152,8,128]{2,1,0:T(8,128)S(1)} %get-tuple-element.27.tiles_ref) | copy-start | bytes 14155780
  53.9 5.7 %collective-permute-start.5 = (f32[2,4,4,128]{3,2,1,0:T(4,128)S(1)}, f32[2,4,4,128]{3,2,1,0:T(4,128)S(1)}, u32[]{:S(2)}, u32[]{:S(2)}) collective-permute-start(f32[2,4,4,128]{3,2,1,0:T(4,128)S(1)} %pad_maximum_fusion.5), channel_id=1, source_target_pairs={{0,480},{32,0},{64,32},{96,64},{128,96},{160,128},{192,160},{224,1... | collective-permute-start | bytes 49160 | tf_op jit(solution)/shard_map/ppermute | solution.py:485
  57.3 5.7 %collective-permute-start.4 = (f32[2,4,4,128]{3,2,1,0:T(4,128)S(1)}, f32[2,4,4,128]{3,2,1,0:T(4,128)S(1)}, u32[]{:S(2)}, u32[]{:S(2)}) collective-permute-start(f32[2,4,4,128]{3,2,1,0:T(4,128)S(1)} %pad_maximum_fusion.5), channel_id=1, source_target_pairs={{0,32},{32,64},{64,96},{96,128},{128,160},{160,192},{192,224},{224... | collective-permute-start | bytes 49160 | tf_op jit(solution)/shard_map/ppermute | solution.py:485
  77.0 5.6 %collective-permute-start.7 = (f32[2,4,4,128]{3,2,1,0:T(4,128)S(1)}, f32[2,4,4,128]{3,2,1,0:T(4,128)S(1)}, u32[]{:S(2)}, u32[]{:S(2)}) collective-permute-start(f32[2,4,4,128]{3,2,1,0:T(4,128)S(1)} %pad_maximum_fusion.6), channel_id=1, source_target_pairs={{0,480},{32,0},{64,32},{96,64},{128,96},{160,128},{192,160},{224,1... | collective-permute-start | bytes 49160 | tf_op jit(solution)/shard_map/ppermute | solution.py:485
  78.9 5.7 %collective-permute-start.6 = (f32[2,4,4,128]{3,2,1,0:T(4,128)S(1)}, f32[2,4,4,128]{3,2,1,0:T(4,128)S(1)}, u32[]{:S(2)}, u32[]{:S(2)}) collective-permute-start(f32[2,4,4,128]{3,2,1,0:T(4,128)S(1)} %pad_maximum_fusion.6), channel_id=1, source_target_pairs={{0,32},{32,64},{64,96},{96,128},{128,160},{160,192},{192,224},{224... | collective-permute-start | bytes 49160 | tf_op jit(solution)/shard_map/ppermute | solution.py:485
  98.4 4.5 %collective-permute-start.8 = (f32[2,4,4,128]{3,2,1,0:T(4,128)S(1)}, f32[2,4,4,128]{3,2,1,0:T(4,128)S(1)}, u32[]{:S(2)}, u32[]{:S(2)}) collective-permute-start(f32[2,4,4,128]{3,2,1,0:T(4,128)S(1)} %pad_maximum_fusion.7), channel_id=1, source_target_pairs={{0,480},{32,0},{64,32},{96,64},{128,96},{160,128},{192,160},{224,1... | collective-permute-start | bytes 49160 | tf_op jit(solution)/shard_map/ppermute | solution.py:485
  116.0 17.4 %all-to-all-start.5 = ((f32[16,1,128]{2,1,0:T(1,128)}), f32[16,1,128]{2,1,0:T(1,128)S(1)}, u32[]{:S(2)}, u32[]{:S(2)}) async-start(f32[16,1,128]{2,1,0:T(1,128)} %broadcast_in_dim.50), calls=%async_computation.5 | async-start | bytes 16384 | tf_op jit(solution)/shard_map/all_to_all | solution.py:490
  122.1 6.0 %collective-permute-start.9 = (f32[2,4,4,128]{3,2,1,0:T(4,128)S(1)}, f32[2,4,4,128]{3,2,1,0:T(4,128)S(1)}, u32[]{:S(2)}, u32[]{:S(2)}) collective-permute-start(f32[2,4,4,128]{3,2,1,0:T(4,128)S(1)} %pad_maximum_fusion.7), channel_id=1, source_target_pairs={{0,32},{32,64},{64,96},{96,128},{128,160},{160,192},{192,224},{224... | collective-permute-start | bytes 49160 | tf_op jit(solution)/shard_map/ppermute | solution.py:485
  133.4 2.3 %copy-start.1 = (f32[1152,8,128]{2,1,0:T(8,128)S(1)}, f32[1152,8,128]{2,1,0:T(8,128)}, u32[]{:S(2)}) copy-start(f32[1152,8,128]{2,1,0:T(8,128)} %copy-done) | copy-start | bytes 14155780

commit v8 on v7

--- a/solution.py
+++ b/solution.py
@@ -339,6 +339,13 @@
     )(tiles, halo)
 
 
+def apply_lower_kernel(tiles_ref, lower_ref, before_ref, aux_ref, w2_ref, w3_ref, next_ref, rows, total, image):
+    fill_fields(lower_ref, rows, 0)
+    apply_tiles(LOWER, 18, 0, tiles_ref, rows, before_ref, total)
+    reduce_rows(total, image)
+    next_ref[...] = next_basis(3, image[...], w3_ref[...], w2_ref[...], aux_ref[0:8], aux_ref[8:16])
+
+
 SCRATCH = [
     pltpu.VMEM((64, 8, 128), jnp.float32),
     pltpu.VMEM((128, 8, 128), jnp.float32),
@@ -372,6 +379,19 @@
     )(tiles, upper, before, aux, *fields)
 
 
+def run_apply_lower(*inputs):
+    return pl.pallas_call(
+        apply_lower_kernel,
+        out_shape=SHAPE((8, 128)),
+        in_specs=[VMEM] * 6,
+        out_specs=VMEM,
+        scratch_shapes=SCRATCH,
+        compiler_params=PARAMS,
+        cost_estimate=cost(4 * 36 * 16384),
+        name="apply_lower",
+    )(*inputs)
+
+
 def combine(coefs, fields):
     value = coefs[0] * fields[0]
     for coef, field in zip(coefs[1:], fields[1:]):
@@ -379,12 +399,8 @@
     return value
 
 
-def finish_kernel(gram_ref, tiles_ref, lower_ref, before_ref, aux_ref, *refs):
-    fields, (charges_ref, residual_ref, rows, sums, last) = [ref[...] for ref in refs[:4]], refs[4:]
-    fill_fields(lower_ref, rows, 0)
-    apply_tiles(LOWER, 18, 0, tiles_ref, rows, before_ref, sums)
-    reduce_rows(sums, last)
-    fields.append(next_basis(3, last[...], fields[3], fields[2], aux_ref[0:8], aux_ref[8:16]))
+def finish_kernel(gram_ref, *refs):
+    fields, (charges_ref, residual_ref) = [ref[...] for ref in refs[:5]], refs[5:]
     summed = spread(jnp.sum(gram_ref[...], axis=0, keepdims=True))
     lane = lax.broadcasted_iota(jnp.int32, (8, 128), 1)
     system = lax.broadcasted_iota(jnp.int32, (8, 128), 0) // 4
@@ -467,16 +483,15 @@
             residual_ref[system, 0, y] = value[row : row + 2]
 
 
-def run_finish(gram, tiles, lower, before, aux, fields):
+def run_finish(gram, fields):
     return pl.pallas_call(
         finish_kernel,
         out_shape=(SHAPE((1, 2, 2, 128)), SHAPE((2, 1, 2, 2, 128))),
-        in_specs=[VMEM] * 9,
+        in_specs=[VMEM] * 6,
         out_specs=(VMEM, VMEM),
-        scratch_shapes=SCRATCH,
         compiler_params=PARAMS,
         name="finish",
-    )(gram, tiles, lower, before, aux, *fields)
+    )(gram, *fields)
 
 
 def shifted(value, axis, steps):
@@ -547,7 +562,8 @@
     total, gram = run_apply_upper(tiles_side, upper, total, aux, fields)
     gram = jnp.sum(spread_all(gram, ("gy", "gz"), count), axis=0)
     gram = spread_all(gram, "gx", count_x).reshape(count_x, 128)
-    return run_finish(gram, tiles_side, lower, total, aux, fields)
+    fields.append(run_apply_lower(tiles_side, lower, total, aux, fields[2], fields[3]))
+    return run_finish(gram, fields)
 
 
 def solution(mesh):

time: 137 us -> 134 us (0.978)
  waiting for transfers between devices: 17.5 us -> 14.7 us
    all_to_all x1, waiting for transfers between devices: 5.21 us -> 2.4 us  [spread_all(): return lax.all_to_all(sent, axes, 0, 0)]
where the time goes in v8:
time: 134 us; the launch traced here: 133 us
  blocking collectives  60.3 us (45%)
  starting transfers between devices  40.2 us (30%)
  waiting for transfers between devices  14.7 us (11%)
  Pallas kernels  13.6 us (10%)
  local copies, waits for them, and re-layouts  3.21 us (2%)
    all_to_all x3, blocking collectives, exchange(): every = lax.all_to_all(sent, ('gy', 'gz'), 0, 0)  41.2 us
    ppermute x10, starting transfers between devices, shifted(): return lax.ppermute(value, axis, pairs)  35.2 us
    all_to_all x2, blocking collectives, spread_all(): return lax.all_to_all(sent, axes, 0, 0)  19.1 us
    ppermute x10, waiting for transfers between devices, shifted(): return lax.ppermute(value, axis, pairs)  12.3 us
    all_to_all x1, starting transfers between devices, spread_all(): return lax.all_to_all(sent, axes, 0, 0)  5.04 us
    pallas_call x1, Pallas kernels, run_side(): pl.pallas_call(side_kernel, out_shape=(SHAPE((72 * 16, 8, 128)), SHAPE((8...  4.86 us
    pallas_call x1, Pallas kernels, run_same(): pl.pallas_call(same_kernel, out_shape=(SHAPE((36 * 16, 8, 128)), SHAPE((2...  3.05 us
  transfers between devices with their start and end apart: 11, of which 8 were waited for; matrix products, arithmetic and copies ran while one was open for 0% of the time, Pallas kernels for 3%

profile of v8, /device:TPU:1, one launch (start us, length us, event | category | flops | bytes accessed | tf_op | source)
XLA Modules:
  0.0 133.1 jit_solution(7265293364192654460)
XLA Ops:
  0.7 1.0 pack.1
  1.7 2.7 %collective-permute-start = (f32[1,2,8,128]{3,2,1,0:T(8,128)S(1)}, f32[1,2,8,128]{3,2,1,0:T(8,128)S(1)}, u32[]{:S(2)}, u32[]{:S(2)}) collective-permute-start(f32[1,2,8,128]{3,2,1,0:T(8,128)S(1)} %get-tuple-element.53), channel_id=1, source_target_pairs={{0,4},{4,8},{8,12},{12,16},{16,20},{20,24},{24,28},{28,0},{1,5},{5... | collective-permute-start | bytes 24584 | tf_op jit(solution)/shard_map/ppermute | solution.py:500
  4.4 4.2 %collective-permute-start.1 = (f32[1,2,8,128]{3,2,1,0:T(8,128)S(1)}, f32[1,2,8,128]{3,2,1,0:T(8,128)S(1)}, u32[]{:S(2)}, u32[]{:S(2)}) collective-permute-start(f32[1,2,8,128]{3,2,1,0:T(8,128)S(1)} %get-tuple-element.54), channel_id=1, source_target_pairs={{0,28},{4,0},{8,4},{12,8},{16,12},{20,16},{24,20},{28,24},{1,29},{... | collective-permute-start | bytes 24584 | tf_op jit(solution)/shard_map/ppermute | solution.py:500
  8.6 0.6 collective-permute-done
  9.4 7.2 %all_to_all.30 = f32[4,4,2,8,128]{4,3,2,1,0:T(8,128)S(1)} all-to-all(f32[4,4,2,8,128]{4,3,2,1,0:T(8,128)S(1)} %broadcast_in_dim.20), channel_id=1, replica_groups=mesh['gx'=16,'gy'=8,'gz'=4] {'gz'}, dimensions={0} | all-to-all | bytes 262144 | tf_op jit(solution)/shard_map/all_to_all | solution.py:505
  16.7 10.6 %collective-permute-start.3 = (f32[4,4,8,128]{3,2,1,0:T(8,128)S(1)}, f32[4,4,8,128]{3,2,1,0:T(8,128)S(1)}, u32[]{:S(2)}, u32[]{:S(2)}) collective-permute-start(f32[4,4,8,128]{3,2,1,0:T(8,128)S(1)} %pad_maximum_fusion), channel_id=1, source_target_pairs={{0,480},{32,0},{64,32},{96,64},{128,96},{160,128},{192,160},{224,1... | collective-permute-start | bytes 196616 | tf_op jit(solution)/shard_map/ppermute | solution.py:500
  27.3 1.9 %collective-permute-start.2 = (f32[4,4,8,128]{3,2,1,0:T(8,128)S(1)}, f32[4,4,8,128]{3,2,1,0:T(8,128)S(1)}, u32[]{:S(2)}, u32[]{:S(2)}) collective-permute-start(f32[4,4,8,128]{3,2,1,0:T(8,128)S(1)} %pad_maximum_fusion), channel_id=1, source_target_pairs={{0,32},{32,64},{64,96},{96,128},{128,160},{160,192},{192,224},{224... | collective-permute-start | bytes 196616 | tf_op jit(solution)/shard_map/ppermute | solution.py:500
  29.2 3.0 %tiles_same.1 = (f32[576,8,128]{2,1,0:T(8,128)S(1)}, f32[256,8,128]{2,1,0:T(8,128)S(1)}, f32[128,8,128]{2,1,0:T(8,128)S(1)}, f32[8,128]{1,0:T(8,128)S(1)}, f32[16,128]{1,0:T(8,128)S(1)}) custom-call(f32[16,8,128]{2,1,0:T(8,128)S(1)} %bitcast.70), custom_call_target="tpu_custom_call" | custom-call | flops 23592960 | bytes 4194304 | tf_op jit(solution)/shard_map/tiles_same/pallas_call | solution.py:219
  32.3 1.2 collective-permute-done.2
  33.5 4.9 %tiles_side.1 = (f32[1152,8,128]{2,1,0:T(8,128)S(1)}, f32[8,128]{1,0:T(8,128)S(1)}) custom-call(f32[16,8,128]{2,1,0:T(8,128)S(1)} %bitcast.71, f32[16,8,128]{2,1,0:T(8,128)S(1)} %bitcast.77, f32[16,8,128]{2,1,0:T(8,128)S(1)} %bitcast.76, f32[256,8,128]{2,1,0:T(8,128)S(1)} %get-tuple-element.23.cols_ref, f32[128,8,128]{2,1,0:T(8,128)S(1)} %get-tuple-element.24.before_ref, ...), custom_call_target="tpu_custom_call" | custom-call | flops 47185920 | bytes 4194304 | tf_op jit(solution)/shard_map/tiles_side/pallas_call | solution.py:241
  38.4 15.7 %all_to_all.31 = f32[32,2,2,2,128]{4,3,2,1,0:T(2,128)S(1)} all-to-all(f32[32,2,2,2,128]{4,3,2,1,0:T(2,128)S(1)} %broadcast_in_dim.43), channel_id=1, replica_groups=mesh['gx'=16,'gy'=8,'gz'=4] {'gy','gz'}, dimensions={0} | all-to-all | bytes 262144 | tf_op jit(solution)/shard_map/all_to_all | solution.py:528
  54.2 3.1 %collective-permute-start.5 = (f32[2,4,4,128]{3,2,1,0:T(4,128)S(1)}, f32[2,4,4,128]{3,2,1,0:T(4,128)S(1)}, u32[]{:S(2)}, u32[]{:S(2)}) collective-permute-start(f32[2,4,4,128]{3,2,1,0:T(4,128)S(1)} %pad_maximum_fusion.5), channel_id=1, source_target_pairs={{0,480},{32,0},{64,32},{96,64},{128,96},{160,128},{192,160},{224,1... | collective-permute-start | bytes 49160 | tf_op jit(solution)/shard_map/ppermute | solution.py:500
  57.4 2.2 %collective-permute-start.4 = (f32[2,4,4,128]{3,2,1,0:T(4,128)S(1)}, f32[2,4,4,128]{3,2,1,0:T(4,128)S(1)}, u32[]{:S(2)}, u32[]{:S(2)}) collective-permute-start(f32[2,4,4,128]{3,2,1,0:T(4,128)S(1)} %pad_maximum_fusion.5), channel_id=1, source_target_pairs={{0,32},{32,64},{64,96},{96,128},{128,160},{160,192},{192,224},{224... | collective-permute-start | bytes 49160 | tf_op jit(solution)/shard_map/ppermute | solution.py:500
  59.8 3.2 %collective-permute-done.4 = f32[2,4,4,128]{3,2,1,0:T(4,128)S(1)} collective-permute-done((f32[2,4,4,128]{3,2,1,0:T(4,128)S(1)}, f32[2,4,4,128]{3,2,1,0:T(4,128)S(1)}, u32[]{:S(2)}, u32[]{:S(2)}) %collective-permute-start.4) | collective-permute-done | bytes 16416 | tf_op jit(solution)/shard_map/ppermute | solution.py:500
  63.1 0.9 apply_side1.1.refs_2_.w2_ref
  64.0 12.9 %all_to_all.32 = f32[32,2,2,2,128]{4,3,2,1,0:T(2,128)S(1)} all-to-all(f32[32,2,2,2,128]{4,3,2,1,0:T(2,128)S(1)} %broadcast_in_dim.45), channel_id=1, replica_groups=mesh['gx'=16,'gy'=8,'gz'=4] {'gy','gz'}, dimensions={0} | all-to-all | bytes 262144 | tf_op jit(solution)/shard_map/all_to_all | solution.py:528
  77.0 1.9 %collective-permute-start.7 = (f32[2,4,4,128]{3,2,1,0:T(4,128)S(1)}, f32[2,4,4,128]{3,2,1,0:T(4,128)S(1)}, u32[]{:S(2)}, u32[]{:S(2)}) collective-permute-start(f32[2,4,4,128]{3,2,1,0:T(4,128)S(1)} %pad_maximum_fusion.6), channel_id=1, source_target_pairs={{0,480},{32,0},{64,32},{96,64},{128,96},{160,128},{192,160},{224,1... | collective-permute-start | bytes 49160 | tf_op jit(solution)/shard_map/ppermute | solution.py:500
  79.0 3.4 %collective-permute-start.6 = (f32[2,4,4,128]{3,2,1,0:T(4,128)S(1)}, f32[2,4,4,128]{3,2,1,0:T(4,128)S(1)}, u32[]{:S(2)}, u32[]{:S(2)}) collective-permute-start(f32[2,4,4,128]{3,2,1,0:T(4,128)S(1)} %pad_maximum_fusion.6), channel_id=1, source_target_pairs={{0,32},{32,64},{64,96},{96,128},{128,160},{160,192},{192,224},{224... | collective-permute-start | bytes 49160 | tf_op jit(solution)/shard_map/ppermute | solution.py:500
  82.7 2.0 %collective-permute-done.6 = f32[2,4,4,128]{3,2,1,0:T(4,128)S(1)} collective-permute-done((f32[2,4,4,128]{3,2,1,0:T(4,128)S(1)}, f32[2,4,4,128]{3,2,1,0:T(4,128)S(1)}, u32[]{:S(2)}, u32[]{:S(2)}) %collective-permute-start.6) | collective-permute-done | bytes 16416 | tf_op jit(solution)/shard_map/ppermute | solution.py:500
  84.7 1.0 apply_side2.1.refs_3_.w3_ref
  85.7 12.6 %all_to_all.33 = f32[32,2,2,2,128]{4,3,2,1,0:T(2,128)S(1)} all-to-all(f32[32,2,2,2,128]{4,3,2,1,0:T(2,128)S(1)} %broadcast_in_dim.47), channel_id=1, replica_groups=mesh['gx'=16,'gy'=8,'gz'=4] {'gy','gz'}, dimensions={0} | all-to-all | bytes 262144 | tf_op jit(solution)/shard_map/all_to_all | solution.py:528
  98.4 1.9 %collective-permute-start.8 = (f32[2,4,4,128]{3,2,1,0:T(4,128)S(1)}, f32[2,4,4,128]{3,2,1,0:T(4,128)S(1)}, u32[]{:S(2)}, u32[]{:S(2)}) collective-permute-start(f32[2,4,4,128]{3,2,1,0:T(4,128)S(1)} %pad_maximum_fusion.7), channel_id=1, source_target_pairs={{0,480},{32,0},{64,32},{96,64},{128,96},{160,128},{192,160},{224,1... | collective-permute-start | bytes 49160 | tf_op jit(solution)/shard_map/ppermute | solution.py:500
  100.6 2.3 %collective-permute-done.8 = f32[2,4,4,128]{3,2,1,0:T(4,128)S(1)} collective-permute-done((f32[2,4,4,128]{3,2,1,0:T(4,128)S(1)}, f32[2,4,4,128]{3,2,1,0:T(4,128)S(1)}, u32[]{:S(2)}, u32[]{:S(2)}) %collective-permute-start.8) | collective-permute-done | bytes 16416 | tf_op jit(solution)/shard_map/ppermute | solution.py:500
  102.9 0.6 apply_upper.1
  103.5 11.9 %all_to_all.34 = f32[32,1,128]{2,1,0:T(1,128)S(1)} all-to-all(f32[32,1,128]{2,1,0:T(1,128)S(1)} %broadcast_in_dim.49), channel_id=1, replica_groups=mesh['gx'=16,'gy'=8,'gz'=4] {'gy','gz'}, dimensions={0} | all-to-all | bytes 32768 | tf_op jit(solution)/shard_map/all_to_all | solution.py:505
  115.5 0.6 broadcast_in_dim.50
  116.1 5.0 %all-to-all-start.5 = ((f32[16,1,128]{2,1,0:T(1,128)}), f32[16,1,128]{2,1,0:T(1,128)S(1)}, u32[]{:S(2)}, u32[]{:S(2)}) async-start(f32[16,1,128]{2,1,0:T(1,128)} %broadcast_in_dim.50), calls=%async_computation.5 | async-start | bytes 16384 | tf_op jit(solution)/shard_map/all_to_all | solution.py:505
  121.1 3.3 %collective-permute-start.9 = (f32[2,4,4,128]{3,2,1,0:T(4,128)S(1)}, f32[2,4,4,128]{3,2,1,0:T(4,128)S(1)}, u32[]{:S(2)}, u32[]{:S(2)}) collective-permute-start(f32[2,4,4,128]{3,2,1,0:T(4,128)S(1)} %pad_maximum_fusion.7), channel_id=1, source_target_pairs={{0,32},{32,64},{64,96},{96,128},{128,160},{160,192},{192,224},{224... | collective-permute-start | bytes 49160 | tf_op jit(solution)/shard_map/ppermute | solution.py:500
  124.4 2.7 %collective-permute-done.9 = f32[2,4,4,128]{3,2,1,0:T(4,128)S(1)} collective-permute-done((f32[2,4,4,128]{3,2,1,0:T(4,128)S(1)}, f32[2,4,4,128]{3,2,1,0:T(4,128)S(1)}, u32[]{:S(2)}, u32[]{:S(2)}) %collective-permute-start.9) | collective-permute-done | bytes 16416 | tf_op jit(solution)/shard_map/ppermute | solution.py:500
  127.1 2.3 %copy-done.1 = f32[1152,8,128]{2,1,0:T(8,128)S(1)} copy-done((f32[1152,8,128]{2,1,0:T(8,128)S(1)}, f32[1152,8,128]{2,1,0:T(8,128)}, u32[]{:S(2)}) %copy-start.1) | copy-done | bytes 4718616
  129.9 2.4 %all-to-all-done.5 = f32[16,1,128]{2,1,0:T(1,128)S(1)} async-done(((f32[16,1,128]{2,1,0:T(1,128)}), f32[16,1,128]{2,1,0:T(1,128)S(1)}, u32[]{:S(2)}, u32[]{:S(2)}) %all-to-all-start.5) | async-done | bytes 8224 | tf_op jit(solution)/shard_map/all_to_all | solution.py:505
  132.3 0.8 finish.1
  (47 shorter events, 2.0 us)
Async XLA Ops:
  1.7 7.6 %collective-permute-start = (f32[1,2,8,128]{3,2,1,0:T(8,128)S(1)}, f32[1,2,8,128]{3,2,1,0:T(8,128)S(1)}, u32[]{:S(2)}, u32[]{:S(2)}) collective-permute-start(f32[1,2,8,128]{3,2,1,0:T(8,128)S(1)} %get-tuple-element.53), channel_id=1, source_target_pairs={{0,4},{4,8},{8,12},{12,16},{16,20},{20,24},{24,28},{28,0},{1,5},{5... | collective-permute-start | bytes 24584 | tf_op jit(solution)/shard_map/ppermute | solution.py:500
  4.4 5.0 %collective-permute-start.1 = (f32[1,2,8,128]{3,2,1,0:T(8,128)S(1)}, f32[1,2,8,128]{3,2,1,0:T(8,128)S(1)}, u32[]{:S(2)}, u32[]{:S(2)}) collective-permute-start(f32[1,2,8,128]{3,2,1,0:T(8,128)S(1)} %get-tuple-element.54), channel_id=1, source_target_pairs={{0,28},{4,0},{8,4},{12,8},{16,12},{20,16},{24,20},{28,24},{1,29},{... | collective-permute-start | bytes 24584 | tf_op jit(solution)/shard_map/ppermute | solution.py:500
  16.7 15.6 %collective-permute-start.3 = (f32[4,4,8,128]{3,2,1,0:T(8,128)S(1)}, f32[4,4,8,128]{3,2,1,0:T(8,128)S(1)}, u32[]{:S(2)}, u32[]{:S(2)}) collective-permute-start(f32[4,4,8,128]{3,2,1,0:T(8,128)S(1)} %pad_maximum_fusion), channel_id=1, source_target_pairs={{0,480},{32,0},{64,32},{96,64},{128,96},{160,128},{192,160},{224,1... | collective-permute-start | bytes 196616 | tf_op jit(solution)/shard_map/ppermute | solution.py:500
  27.3 6.2 %collective-permute-start.2 = (f32[4,4,8,128]{3,2,1,0:T(8,128)S(1)}, f32[4,4,8,128]{3,2,1,0:T(8,128)S(1)}, u32[]{:S(2)}, u32[]{:S(2)}) collective-permute-start(f32[4,4,8,128]{3,2,1,0:T(8,128)S(1)} %pad_maximum_fusion), channel_id=1, source_target_pairs={{0,32},{32,64},{64,96},{96,128},{128,160},{160,192},{192,224},{224... | collective-permute-start | bytes 196616 | tf_op jit(solution)/shard_map/ppermute | solution.py:500
  38.4 64.5 %copy-start = (f32[1152,8,128]{2,1,0:T(8,128)}, f32[1152,8,128]{2,1,0:T(8,128)S(1)}, u32[]{:S(2)}) copy-start(f32[1152,8,128]{2,1,0:T(8,128)S(1)} %get-tuple-element.27.tiles_ref) | copy-start | bytes 14155780
  54.2 5.6 %collective-permute-start.5 = (f32[2,4,4,128]{3,2,1,0:T(4,128)S(1)}, f32[2,4,4,128]{3,2,1,0:T(4,128)S(1)}, u32[]{:S(2)}, u32[]{:S(2)}) collective-permute-start(f32[2,4,4,128]{3,2,1,0:T(4,128)S(1)} %pad_maximum_fusion.5), channel_id=1, source_target_pairs={{0,480},{32,0},{64,32},{96,64},{128,96},{160,128},{192,160},{224,1... | collective-permute-start | bytes 49160 | tf_op jit(solution)/shard_map/ppermute | solution.py:500
  57.4 5.7 %collective-permute-start.4 = (f32[2,4,4,128]{3,2,1,0:T(4,128)S(1)}, f32[2,4,4,128]{3,2,1,0:T(4,128)S(1)}, u32[]{:S(2)}, u32[]{:S(2)}) collective-permute-start(f32[2,4,4,128]{3,2,1,0:T(4,128)S(1)} %pad_maximum_fusion.5), channel_id=1, source_target_pairs={{0,32},{32,64},{64,96},{96,128},{128,160},{160,192},{192,224},{224... | collective-permute-start | bytes 49160 | tf_op jit(solution)/shard_map/ppermute | solution.py:500
  77.0 5.6 %collective-permute-start.7 = (f32[2,4,4,128]{3,2,1,0:T(4,128)S(1)}, f32[2,4,4,128]{3,2,1,0:T(4,128)S(1)}, u32[]{:S(2)}, u32[]{:S(2)}) collective-permute-start(f32[2,4,4,128]{3,2,1,0:T(4,128)S(1)} %pad_maximum_fusion.6), channel_id=1, source_target_pairs={{0,480},{32,0},{64,32},{96,64},{128,96},{160,128},{192,160},{224,1... | collective-permute-start | bytes 49160 | tf_op jit(solution)/shard_map/ppermute | solution.py:500
  79.0 5.7 %collective-permute-start.6 = (f32[2,4,4,128]{3,2,1,0:T(4,128)S(1)}, f32[2,4,4,128]{3,2,1,0:T(4,128)S(1)}, u32[]{:S(2)}, u32[]{:S(2)}) collective-permute-start(f32[2,4,4,128]{3,2,1,0:T(4,128)S(1)} %pad_maximum_fusion.6), channel_id=1, source_target_pairs={{0,32},{32,64},{64,96},{96,128},{128,160},{160,192},{192,224},{224... | collective-permute-start | bytes 49160 | tf_op jit(solution)/shard_map/ppermute | solution.py:500
  98.4 4.5 %collective-permute-start.8 = (f32[2,4,4,128]{3,2,1,0:T(4,128)S(1)}, f32[2,4,4,128]{3,2,1,0:T(4,128)S(1)}, u32[]{:S(2)}, u32[]{:S(2)}) collective-permute-start(f32[2,4,4,128]{3,2,1,0:T(4,128)S(1)} %pad_maximum_fusion.7), channel_id=1, source_target_pairs={{0,480},{32,0},{64,32},{96,64},{128,96},{160,128},{192,160},{224,1... | collective-permute-start | bytes 49160 | tf_op jit(solution)/shard_map/ppermute | solution.py:500
  116.1 16.3 %all-to-all-start.5 = ((f32[16,1,128]{2,1,0:T(1,128)}), f32[16,1,128]{2,1,0:T(1,128)S(1)}, u32[]{:S(2)}, u32[]{:S(2)}) async-start(f32[16,1,128]{2,1,0:T(1,128)} %broadcast_in_dim.50), calls=%async_computation.5 | async-start | bytes 16384 | tf_op jit(solution)/shard_map/all_to_all | solution.py:505
  121.1 6.0 %collective-permute-start.9 = (f32[2,4,4,128]{3,2,1,0:T(4,128)S(1)}, f32[2,4,4,128]{3,2,1,0:T(4,128)S(1)}, u32[]{:S(2)}, u32[]{:S(2)}) collective-permute-start(f32[2,4,4,128]{3,2,1,0:T(4,128)S(1)} %pad_maximum_fusion.7), channel_id=1, source_target_pairs={{0,32},{32,64},{64,96},{96,128},{128,160},{160,192},{192,224},{224... | collective-permute-start | bytes 49160 | tf_op jit(solution)/shard_map/ppermute | solution.py:500
  127.1 2.3 %copy-start.1 = (f32[1152,8,128]{2,1,0:T(8,128)S(1)}, f32[1152,8,128]{2,1,0:T(8,128)}, u32[]{:S(2)}) copy-start(f32[1152,8,128]{2,1,0:T(8,128)} %copy-done) | copy-start | bytes 14155780

commit v9 on v8

--- a/solution.py
+++ b/solution.py
@@ -199,11 +199,16 @@
     build_tiles(SAME, own_ref, rows, cols_ref, away, tiles_ref, None, total_ref)
 
 
-def side_kernel(own_ref, lower_ref, upper_ref, cols_ref, before_ref, field_ref, aux_ref, tiles_ref, next_ref, rows, away, total, image):
+def upper_kernel(own_ref, upper_ref, cols_ref, before_ref, tiles_ref, total_ref, rows, away):
+    fill_rows(upper_ref, rows, 16, 1)
+    fill_away(UPPER, own_ref, own_ref, rows, away)
+    build_tiles(UPPER, own_ref, rows, cols_ref, away, tiles_ref, before_ref, total_ref)
+
+
+def lower_kernel(own_ref, lower_ref, cols_ref, before_ref, field_ref, aux_ref, tiles_ref, next_ref, rows, away, total, image):
     fill_rows(lower_ref, rows, 0, -1)
-    fill_rows(upper_ref, rows, 16, 1)
-    fill_away(SIDE, own_ref, lower_ref, rows, away)
-    build_tiles(SIDE, own_ref, rows, cols_ref, away, tiles_ref, before_ref, total)
+    fill_away(LOWER, own_ref, lower_ref, rows, away)
+    build_tiles(LOWER, own_ref, rows, cols_ref, away, tiles_ref, before_ref, total)
     reduce_rows(total, image)
     next_ref[...] = next_basis(0, image[...], field_ref[...], None, aux_ref[0:8], aux_ref[8:16])
 
@@ -237,21 +242,32 @@
     )(own)
 
 
-def run_side(*inputs):
-    return pl.pallas_call(
-        side_kernel,
-        out_shape=(SHAPE((72 * 16, 8, 128)), SHAPE((8, 128))),
-        in_specs=[VMEM] * 7,
+PLACES = [pltpu.VMEM((32, 6, 8, 128), jnp.float32), pltpu.VMEM((36, 8, 128), jnp.float32)]
+
+
+def run_upper(*inputs):
+    return pl.pallas_call(
+        upper_kernel,
+        out_shape=(SHAPE((36 * 16, 8, 128)), SHAPE((128, 8, 128))),
+        in_specs=[VMEM] * 4,
         out_specs=(VMEM,) * 2,
-        scratch_shapes=[
-            pltpu.VMEM((32, 6, 8, 128), jnp.float32),
-            pltpu.VMEM((72, 8, 128), jnp.float32),
-            pltpu.VMEM((128, 8, 128), jnp.float32),
-            pltpu.VMEM((8, 128), jnp.float32),
-        ],
-        compiler_params=PARAMS,
-        cost_estimate=cost(40 * 72 * 16384),
-        name="tiles_side",
+        scratch_shapes=PLACES,
+        compiler_params=PARAMS,
+        cost_estimate=cost(40 * 36 * 16384),
+        name="tiles_upper",
+    )(*inputs)
+
+
+def run_lower(*inputs):
+    return pl.pallas_call(
+        lower_kernel,
+        out_shape=(SHAPE((36 * 16, 8, 128)), SHAPE((8, 128))),
+        in_specs=[VMEM] * 6,
+        out_specs=(VMEM,) * 2,
+        scratch_shapes=PLACES + [pltpu.VMEM((128, 8, 128), jnp.float32), pltpu.VMEM((8, 128), jnp.float32)],
+        compiler_params=PARAMS,
+        cost_estimate=cost(40 * 36 * 16384),
+        name="tiles_lower",
     )(*inputs)
 
 
@@ -303,20 +319,15 @@
     apply_tiles(SAME, 9, 0, tiles_ref, rows, None, total_ref)
 
 
-def apply_side_kernel(step, tiles_ref, lower_ref, upper_ref, before_ref, aux_ref, *refs):
-    fields, (next_ref, rows, total, image) = refs[: step + 1], refs[step + 1 :]
-    fill_fields(lower_ref, rows, 0)
+def apply_half_kernel(tiles_ref, upper_ref, before_ref, total_ref, rows):
     fill_fields(upper_ref, rows, 16)
-    apply_tiles(SIDE, 18, 0, tiles_ref, rows, before_ref, total)
-    reduce_rows(total, image)
-    before, field = fields[step - 1][...], fields[step][...]
-    next_ref[...] = next_basis(step, image[...], field, before, aux_ref[0:8], aux_ref[8:16])
+    apply_tiles(UPPER, 9, 0, tiles_ref, rows, before_ref, total_ref)
 
 
 def apply_upper_kernel(tiles_ref, upper_ref, before_ref, aux_ref, *refs):
     fields, (total_ref, gram_ref, rows, total, image) = [ref[...] for ref in refs[:4]], refs[4:]
     fill_fields(upper_ref, rows, 16)
-    apply_tiles(UPPER, 18, 9, tiles_ref, rows, None, total)
+    apply_tiles(UPPER, 9, 0, tiles_ref, rows, None, total)
     part = total[...]
     both = before_ref[...] + part
     total_ref[...] = both
@@ -339,11 +350,11 @@
     )(tiles, halo)
 
 
-def apply_lower_kernel(tiles_ref, lower_ref, before_ref, aux_ref, w2_ref, w3_ref, next_ref, rows, total, image):
+def apply_lower_kernel(step, tiles_ref, lower_ref, before_ref, aux_ref, past_ref, field_ref, next_ref, rows, total, image):
     fill_fields(lower_ref, rows, 0)
-    apply_tiles(LOWER, 18, 0, tiles_ref, rows, before_ref, total)
+    apply_tiles(LOWER, 9, 0, tiles_ref, rows, before_ref, total)
     reduce_rows(total, image)
-    next_ref[...] = next_basis(3, image[...], w3_ref[...], w2_ref[...], aux_ref[0:8], aux_ref[8:16])
+    next_ref[...] = next_basis(step, image[...], field_ref[...], past_ref[...], aux_ref[0:8], aux_ref[8:16])
 
 
 SCRATCH = [
@@ -353,17 +364,17 @@
 ]
 
 
-def run_apply_side(step, tiles, lower, upper, before, aux, fields):
-    return pl.pallas_call(
-        functools.partial(apply_side_kernel, step),
-        out_shape=SHAPE((8, 128)),
-        in_specs=[VMEM] * (5 + len(fields)),
+def run_apply_half(tiles, upper, before):
+    return pl.pallas_call(
+        apply_half_kernel,
+        out_shape=SHAPE((128, 8, 128)),
+        in_specs=[VMEM] * 3,
         out_specs=VMEM,
-        scratch_shapes=SCRATCH,
-        compiler_params=PARAMS,
-        cost_estimate=cost(4 * 72 * 16384),
-        name=f"apply_side{step}",
-    )(tiles, lower, upper, before, aux, *fields)
+        scratch_shapes=SCRATCH[:1],
+        compiler_params=PARAMS,
+        cost_estimate=cost(4 * 36 * 16384),
+        name="apply_half",
+    )(tiles, upper, before)
 
 
 def run_apply_upper(tiles, upper, before, aux, fields):
@@ -379,16 +390,16 @@
     )(tiles, upper, before, aux, *fields)
 
 
-def run_apply_lower(*inputs):
-    return pl.pallas_call(
-        apply_lower_kernel,
+def run_apply_lower(step, *inputs):
+    return pl.pallas_call(
+        functools.partial(apply_lower_kernel, step),
         out_shape=SHAPE((8, 128)),
         in_specs=[VMEM] * 6,
         out_specs=VMEM,
         scratch_shapes=SCRATCH,
         compiler_params=PARAMS,
         cost_estimate=cost(4 * 36 * 16384),
-        name="apply_lower",
+        name=f"apply_lower{step}",
     )(*inputs)
 
 
@@ -550,7 +561,8 @@
     layers = exchange_cells(packed.reshape(2, 2, 8, 128), indices)
     own, lower, upper = [layer.reshape(16, 8, 128) for layer in layers]
     tiles_same, cols, total, w0, aux = run_same(own)
-    tiles_side, w1 = run_side(own, lower, upper, cols, total, w0, aux)
+    tiles_upper, total = run_upper(own, upper, cols, total)
+    tiles_lower, w1 = run_lower(own, lower, cols, total, w0, aux)
     fields = [w0, w1]
     for step in (1, 2, 3):
         sent = jnp.broadcast_to(fields[-1].reshape(1, 2, 2, 2, 128), (count, 2, 2, 2, 128))
@@ -558,11 +570,12 @@
         own, lower, upper = [layer.reshape(32, 128) for layer in layers]
         total = run_apply_same(tiles_same, own)
         if step < 3:
-            fields.append(run_apply_side(step, tiles_side, lower, upper, total, aux, fields))
-    total, gram = run_apply_upper(tiles_side, upper, total, aux, fields)
+            total = run_apply_half(tiles_upper, upper, total)
+            fields.append(run_apply_lower(step, tiles_lower, lower, total, aux, fields[-2], fields[-1]))
+    total, gram = run_apply_upper(tiles_upper, upper, total, aux, fields)
     gram = jnp.sum(spread_all(gram, ("gy", "gz"), count), axis=0)
     gram = spread_all(gram, "gx", count_x).reshape(count_x, 128)
-    fields.append(run_apply_lower(tiles_side, lower, total, aux, fields[2], fields[3]))
+    fields.append(run_apply_lower(3, tiles_lower, lower, total, aux, fields[2], fields[3]))
     return run_finish(gram, fields)
 
 

time: 134 us -> 135 us (level)
  local copies, waits for them, and re-layouts: 3.21 us -> 0.87 us
  starting transfers between devices: 40.2 us -> 42.2 us
  blocking collectives: 60.3 us -> 58.6 us
  Pallas kernels: 13.6 us -> 15.1 us
    all_to_all x1, waiting for transfers between devices: 2.4 us -> 4.75 us  [spread_all(): return lax.all_to_all(sent, axes, 0, 0)]
    unnamed x4 -> x0, local copies, waits for them, and re-layouts: 2.34 us -> none
    ppermute x10, waiting for transfers between devices: 12.3 us -> 10.6 us  [shifted(): return lax.ppermute(value, axis, pairs)]
    all_to_all x3, blocking collectives: 41.2 us -> 39.5 us  [exchange(): every = lax.all_to_all(sent, ('gy', 'gz'), 0, 0)]
    pallas_call x4 -> x7, Pallas kernels: 7.25 us -> 8.51 us  [the longest x1 3.32 us: run_lower(): pl.pallas_call(lower_kernel, out_shape=(SHAPE((36 * 16, 8, 128)), SHAPE((...]
  transfers between devices with their start and end apart: 11 -> 11, of which waited for: 8 -> 7; matrix products, arithmetic and copies ran while one was open for 0% -> 0% of each run, Pallas kernels for 3% -> 6%
where the time goes in v9:
time: 135 us; the launch traced here: 133 us
  blocking collectives  58.6 us (43%)
  starting transfers between devices  42.2 us (31%)
  waiting for transfers between devices  15.4 us (11%)
  Pallas kernels  15.1 us (11%)
    all_to_all x3, blocking collectives, exchange(): every = lax.all_to_all(sent, ('gy', 'gz'), 0, 0)  39.5 us
    ppermute x10, starting transfers between devices, shifted(): return lax.ppermute(value, axis, pairs)  36.4 us
    all_to_all x2, blocking collectives, spread_all(): return lax.all_to_all(sent, axes, 0, 0)  19.1 us
    ppermute x10, waiting for transfers between devices, shifted(): return lax.ppermute(value, axis, pairs)  10.6 us
    all_to_all x1, starting transfers between devices, spread_all(): return lax.all_to_all(sent, axes, 0, 0)  5.81 us
    all_to_all x1, waiting for transfers between devices, spread_all(): return lax.all_to_all(sent, axes, 0, 0)  4.75 us
    pallas_call x1, Pallas kernels, run_same(): pl.pallas_call(same_kernel, out_shape=(SHAPE((36 * 16, 8, 128)), SHAPE((2...  3.36 us
    pallas_call x1, Pallas kernels, run_lower(): pl.pallas_call(lower_kernel, out_shape=(SHAPE((36 * 16, 8, 128)), SHAPE((...  3.32 us
  transfers between devices with their start and end apart: 11, of which 7 were waited for; matrix products, arithmetic and copies ran while one was open for 0% of the time, Pallas kernels for 6%

profile of v9, /device:TPU:1, one launch (start us, length us, event | category | flops | bytes accessed | tf_op | source)
XLA Modules:
  0.0 133.4 jit_solution(7858549868228177015)
XLA Ops:
  0.7 1.0 pack.1
  1.7 2.7 %collective-permute-start = (f32[1,2,8,128]{3,2,1,0:T(8,128)S(1)}, f32[1,2,8,128]{3,2,1,0:T(8,128)S(1)}, u32[]{:S(2)}, u32[]{:S(2)}) collective-permute-start(f32[1,2,8,128]{3,2,1,0:T(8,128)S(1)} %get-tuple-element.57), channel_id=1, source_target_pairs={{0,4},{4,8},{8,12},{12,16},{16,20},{20,24},{24,28},{28,0},{1,5},{5... | collective-permute-start | bytes 24584 | tf_op jit(solution)/shard_map/ppermute | solution.py:511
  4.4 4.2 %collective-permute-start.1 = (f32[1,2,8,128]{3,2,1,0:T(8,128)S(1)}, f32[1,2,8,128]{3,2,1,0:T(8,128)S(1)}, u32[]{:S(2)}, u32[]{:S(2)}) collective-permute-start(f32[1,2,8,128]{3,2,1,0:T(8,128)S(1)} %get-tuple-element.58), channel_id=1, source_target_pairs={{0,28},{4,0},{8,4},{12,8},{16,12},{20,16},{24,20},{28,24},{1,29},{... | collective-permute-start | bytes 24584 | tf_op jit(solution)/shard_map/ppermute | solution.py:511
  8.6 0.6 collective-permute-done
  9.4 7.2 %all_to_all.30 = f32[4,4,2,8,128]{4,3,2,1,0:T(8,128)S(1)} all-to-all(f32[4,4,2,8,128]{4,3,2,1,0:T(8,128)S(1)} %broadcast_in_dim.20), channel_id=1, replica_groups=mesh['gx'=16,'gy'=8,'gz'=4] {'gz'}, dimensions={0} | all-to-all | bytes 262144 | tf_op jit(solution)/shard_map/all_to_all | solution.py:516
  16.7 10.6 %collective-permute-start.2 = (f32[4,4,8,128]{3,2,1,0:T(8,128)S(1)}, f32[4,4,8,128]{3,2,1,0:T(8,128)S(1)}, u32[]{:S(2)}, u32[]{:S(2)}) collective-permute-start(f32[4,4,8,128]{3,2,1,0:T(8,128)S(1)} %pad_maximum_fusion), channel_id=1, source_target_pairs={{0,480},{32,0},{64,32},{96,64},{128,96},{160,128},{192,160},{224,1... | collective-permute-start | bytes 196616 | tf_op jit(solution)/shard_map/ppermute | solution.py:511
  27.3 1.9 %collective-permute-start.3 = (f32[4,4,8,128]{3,2,1,0:T(8,128)S(1)}, f32[4,4,8,128]{3,2,1,0:T(8,128)S(1)}, u32[]{:S(2)}, u32[]{:S(2)}) collective-permute-start(f32[4,4,8,128]{3,2,1,0:T(8,128)S(1)} %pad_maximum_fusion), channel_id=1, source_target_pairs={{0,32},{32,64},{64,96},{96,128},{128,160},{160,192},{192,224},{224... | collective-permute-start | bytes 196616 | tf_op jit(solution)/shard_map/ppermute | solution.py:511
  29.2 3.4 %tiles_same.1 = (f32[576,8,128]{2,1,0:T(8,128)S(1)}, f32[256,8,128]{2,1,0:T(8,128)S(1)}, f32[128,8,128]{2,1,0:T(8,128)S(1)}, f32[8,128]{1,0:T(8,128)S(1)}, f32[16,128]{1,0:T(8,128)S(1)}) custom-call(f32[16,8,128]{2,1,0:T(8,128)S(1)} %bitcast.70), custom_call_target="tpu_custom_call" | custom-call | flops 23592960 | bytes 4194304 | tf_op jit(solution)/shard_map/tiles_same/pallas_call | solution.py:224
  32.6 3.1 %tiles_upper.1 = (f32[576,8,128]{2,1,0:T(8,128)S(1)}, f32[128,8,128]{2,1,0:T(8,128)S(1)}) custom-call(f32[16,8,128]{2,1,0:T(8,128)S(1)} %bitcast.71, f32[16,8,128]{2,1,0:T(8,128)S(1)} %bitcast.81, f32[256,8,128]{2,1,0:T(8,128)S(1)} %get-tuple-element.25.cols_ref, f32[128,8,128]{2,1,0:T(8,128)S(1)} %get-tuple-element.26.before_ref), custom_call_target="tpu_custom_call" | custom-call | flops 23592960 | bytes 4194304 | tf_op jit(solution)/shard_map/tiles_upper/pallas_call | solution.py:249
  35.7 3.3 %tiles_lower.1 = (f32[576,8,128]{2,1,0:T(8,128)S(1)}, f32[8,128]{1,0:T(8,128)S(1)}) custom-call(f32[16,8,128]{2,1,0:T(8,128)S(1)} %bitcast.72, f32[16,8,128]{2,1,0:T(8,128)S(1)} %bitcast.80, f32[256,8,128]{2,1,0:T(8,128)S(1)} %get-tuple-element.25.cols_ref, f32[128,8,128]{2,1,0:T(8,128)S(1)} %get-tuple-element.28.before_ref, ...), custom_call_target="tpu_custom_call" | custom-call | flops 23592960 | bytes 4194304 | tf_op jit(solution)/shard_map/tiles_lower/pallas_call | solution.py:262
  39.1 14.0 %all_to_all.31 = f32[32,2,2,2,128]{4,3,2,1,0:T(2,128)S(1)} all-to-all(f32[32,2,2,2,128]{4,3,2,1,0:T(2,128)S(1)} %broadcast_in_dim.43), channel_id=1, replica_groups=mesh['gx'=16,'gy'=8,'gz'=4] {'gy','gz'}, dimensions={0} | all-to-all | bytes 262144 | tf_op jit(solution)/shard_map/all_to_all | solution.py:539
  53.2 4.6 %collective-permute-start.5 = (f32[2,4,4,128]{3,2,1,0:T(4,128)S(1)}, f32[2,4,4,128]{3,2,1,0:T(4,128)S(1)}, u32[]{:S(2)}, u32[]{:S(2)}) collective-permute-start(f32[2,4,4,128]{3,2,1,0:T(4,128)S(1)} %pad_maximum_fusion.5), channel_id=1, source_target_pairs={{0,480},{32,0},{64,32},{96,64},{128,96},{160,128},{192,160},{224,1... | collective-permute-start | bytes 49160 | tf_op jit(solution)/shard_map/ppermute | solution.py:511
  57.9 1.9 %collective-permute-start.4 = (f32[2,4,4,128]{3,2,1,0:T(4,128)S(1)}, f32[2,4,4,128]{3,2,1,0:T(4,128)S(1)}, u32[]{:S(2)}, u32[]{:S(2)}) collective-permute-start(f32[2,4,4,128]{3,2,1,0:T(4,128)S(1)} %pad_maximum_fusion.5), channel_id=1, source_target_pairs={{0,32},{32,64},{64,96},{96,128},{128,160},{160,192},{192,224},{224... | collective-permute-start | bytes 49160 | tf_op jit(solution)/shard_map/ppermute | solution.py:511
  60.4 3.1 %collective-permute-done.4 = f32[2,4,4,128]{3,2,1,0:T(4,128)S(1)} collective-permute-done((f32[2,4,4,128]{3,2,1,0:T(4,128)S(1)}, f32[2,4,4,128]{3,2,1,0:T(4,128)S(1)}, u32[]{:S(2)}, u32[]{:S(2)}) %collective-permute-start.4) | collective-permute-done | bytes 16416 | tf_op jit(solution)/shard_map/ppermute | solution.py:511
  63.5 0.5 apply_lower1.1.field_ref.refs_2_.past_ref
  64.1 12.9 %all_to_all.32 = f32[32,2,2,2,128]{4,3,2,1,0:T(2,128)S(1)} all-to-all(f32[32,2,2,2,128]{4,3,2,1,0:T(2,128)S(1)} %broadcast_in_dim.45), channel_id=1, replica_groups=mesh['gx'=16,'gy'=8,'gz'=4] {'gy','gz'}, dimensions={0} | all-to-all | bytes 262144 | tf_op jit(solution)/shard_map/all_to_all | solution.py:539
  77.1 1.9 %collective-permute-start.7 = (f32[2,4,4,128]{3,2,1,0:T(4,128)S(1)}, f32[2,4,4,128]{3,2,1,0:T(4,128)S(1)}, u32[]{:S(2)}, u32[]{:S(2)}) collective-permute-start(f32[2,4,4,128]{3,2,1,0:T(4,128)S(1)} %pad_maximum_fusion.6), channel_id=1, source_target_pairs={{0,480},{32,0},{64,32},{96,64},{128,96},{160,128},{192,160},{224,1... | collective-permute-start | bytes 49160 | tf_op jit(solution)/shard_map/ppermute | solution.py:511
  79.0 3.4 %collective-permute-start.6 = (f32[2,4,4,128]{3,2,1,0:T(4,128)S(1)}, f32[2,4,4,128]{3,2,1,0:T(4,128)S(1)}, u32[]{:S(2)}, u32[]{:S(2)}) collective-permute-start(f32[2,4,4,128]{3,2,1,0:T(4,128)S(1)} %pad_maximum_fusion.6), channel_id=1, source_target_pairs={{0,32},{32,64},{64,96},{96,128},{128,160},{160,192},{192,224},{224... | collective-permute-start | bytes 49160 | tf_op jit(solution)/shard_map/ppermute | solution.py:511
  83.0 1.7 %collective-permute-done.6 = f32[2,4,4,128]{3,2,1,0:T(4,128)S(1)} collective-permute-done((f32[2,4,4,128]{3,2,1,0:T(4,128)S(1)}, f32[2,4,4,128]{3,2,1,0:T(4,128)S(1)}, u32[]{:S(2)}, u32[]{:S(2)}) %collective-permute-start.6) | collective-permute-done | bytes 16416 | tf_op jit(solution)/shard_map/ppermute | solution.py:511
  84.7 0.5 apply_lower2.1.refs_3_.field_ref
  85.2 12.6 %all_to_all.33 = f32[32,2,2,2,128]{4,3,2,1,0:T(2,128)S(1)} all-to-all(f32[32,2,2,2,128]{4,3,2,1,0:T(2,128)S(1)} %broadcast_in_dim.47), channel_id=1, replica_groups=mesh['gx'=16,'gy'=8,'gz'=4] {'gy','gz'}, dimensions={0} | all-to-all | bytes 262144 | tf_op jit(solution)/shard_map/all_to_all | solution.py:539
  97.9 1.9 %collective-permute-start.8 = (f32[2,4,4,128]{3,2,1,0:T(4,128)S(1)}, f32[2,4,4,128]{3,2,1,0:T(4,128)S(1)}, u32[]{:S(2)}, u32[]{:S(2)}) collective-permute-start(f32[2,4,4,128]{3,2,1,0:T(4,128)S(1)} %pad_maximum_fusion.7), channel_id=1, source_target_pairs={{0,480},{32,0},{64,32},{96,64},{128,96},{160,128},{192,160},{224,1... | collective-permute-start | bytes 49160 | tf_op jit(solution)/shard_map/ppermute | solution.py:511
  100.2 2.3 %collective-permute-done.8 = f32[2,4,4,128]{3,2,1,0:T(4,128)S(1)} collective-permute-done((f32[2,4,4,128]{3,2,1,0:T(4,128)S(1)}, f32[2,4,4,128]{3,2,1,0:T(4,128)S(1)}, u32[]{:S(2)}, u32[]{:S(2)}) %collective-permute-start.8) | collective-permute-done | bytes 16416 | tf_op jit(solution)/shard_map/ppermute | solution.py:511
  102.4 0.6 apply_upper.1
  103.1 11.9 %all_to_all.34 = f32[32,1,128]{2,1,0:T(1,128)S(1)} all-to-all(f32[32,1,128]{2,1,0:T(1,128)S(1)} %broadcast_in_dim.49), channel_id=1, replica_groups=mesh['gx'=16,'gy'=8,'gz'=4] {'gy','gz'}, dimensions={0} | all-to-all | bytes 32768 | tf_op jit(solution)/shard_map/all_to_all | solution.py:516
  115.0 0.6 broadcast_in_dim.50
  115.6 5.8 %all-to-all-start.5 = ((f32[16,1,128]{2,1,0:T(1,128)}), f32[16,1,128]{2,1,0:T(1,128)S(1)}, u32[]{:S(2)}, u32[]{:S(2)}) async-start(f32[16,1,128]{2,1,0:T(1,128)} %broadcast_in_dim.50), calls=%async_computation.5 | async-start | bytes 16384 | tf_op jit(solution)/shard_map/all_to_all | solution.py:516
  121.4 3.3 %collective-permute-start.9 = (f32[2,4,4,128]{3,2,1,0:T(4,128)S(1)}, f32[2,4,4,128]{3,2,1,0:T(4,128)S(1)}, u32[]{:S(2)}, u32[]{:S(2)}) collective-permute-start(f32[2,4,4,128]{3,2,1,0:T(4,128)S(1)} %pad_maximum_fusion.7), channel_id=1, source_target_pairs={{0,32},{32,64},{64,96},{96,128},{128,160},{160,192},{192,224},{224... | collective-permute-start | bytes 49160 | tf_op jit(solution)/shard_map/ppermute | solution.py:511
  124.7 2.7 %collective-permute-done.9 = f32[2,4,4,128]{3,2,1,0:T(4,128)S(1)} collective-permute-done((f32[2,4,4,128]{3,2,1,0:T(4,128)S(1)}, f32[2,4,4,128]{3,2,1,0:T(4,128)S(1)}, u32[]{:S(2)}, u32[]{:S(2)}) %collective-permute-start.9) | collective-permute-done | bytes 16416 | tf_op jit(solution)/shard_map/ppermute | solution.py:511
  127.4 0.5 apply_lower3.1.refs_4_
  127.9 4.7 %all-to-all-done.5 = f32[16,1,128]{2,1,0:T(1,128)S(1)} async-done(((f32[16,1,128]{2,1,0:T(1,128)}), f32[16,1,128]{2,1,0:T(1,128)S(1)}, u32[]{:S(2)}, u32[]{:S(2)}) %all-to-all-start.5) | async-done | bytes 8224 | tf_op jit(solution)/shard_map/all_to_all | solution.py:516
  132.6 0.8 finish.1
  (46 shorter events, 2.2 us)
Async XLA Ops:
  1.7 7.6 %collective-permute-start = (f32[1,2,8,128]{3,2,1,0:T(8,128)S(1)}, f32[1,2,8,128]{3,2,1,0:T(8,128)S(1)}, u32[]{:S(2)}, u32[]{:S(2)}) collective-permute-start(f32[1,2,8,128]{3,2,1,0:T(8,128)S(1)} %get-tuple-element.57), channel_id=1, source_target_pairs={{0,4},{4,8},{8,12},{12,16},{16,20},{20,24},{24,28},{28,0},{1,5},{5... | collective-permute-start | bytes 24584 | tf_op jit(solution)/shard_map/ppermute | solution.py:511
  4.4 5.0 %collective-permute-start.1 = (f32[1,2,8,128]{3,2,1,0:T(8,128)S(1)}, f32[1,2,8,128]{3,2,1,0:T(8,128)S(1)}, u32[]{:S(2)}, u32[]{:S(2)}) collective-permute-start(f32[1,2,8,128]{3,2,1,0:T(8,128)S(1)} %get-tuple-element.58), channel_id=1, source_target_pairs={{0,28},{4,0},{8,4},{12,8},{16,12},{20,16},{24,20},{28,24},{1,29},{... | collective-permute-start | bytes 24584 | tf_op jit(solution)/shard_map/ppermute | solution.py:511
  16.7 15.9 %collective-permute-start.2 = (f32[4,4,8,128]{3,2,1,0:T(8,128)S(1)}, f32[4,4,8,128]{3,2,1,0:T(8,128)S(1)}, u32[]{:S(2)}, u32[]{:S(2)}) collective-permute-start(f32[4,4,8,128]{3,2,1,0:T(8,128)S(1)} %pad_maximum_fusion), channel_id=1, source_target_pairs={{0,480},{32,0},{64,32},{96,64},{128,96},{160,128},{192,160},{224,1... | collective-permute-start | bytes 196616 | tf_op jit(solution)/shard_map/ppermute | solution.py:511
  27.3 8.4 %collective-permute-start.3 = (f32[4,4,8,128]{3,2,1,0:T(8,128)S(1)}, f32[4,4,8,128]{3,2,1,0:T(8,128)S(1)}, u32[]{:S(2)}, u32[]{:S(2)}) collective-permute-start(f32[4,4,8,128]{3,2,1,0:T(8,128)S(1)} %pad_maximum_fusion), channel_id=1, source_target_pairs={{0,32},{32,64},{64,96},{96,128},{128,160},{160,192},{192,224},{224... | collective-permute-start | bytes 196616 | tf_op jit(solution)/shard_map/ppermute | solution.py:511
  53.2 6.8 %collective-permute-start.5 = (f32[2,4,4,128]{3,2,1,0:T(4,128)S(1)}, f32[2,4,4,128]{3,2,1,0:T(4,128)S(1)}, u32[]{:S(2)}, u32[]{:S(2)}) collective-permute-start(f32[2,4,4,128]{3,2,1,0:T(4,128)S(1)} %pad_maximum_fusion.5), channel_id=1, source_target_pairs={{0,480},{32,0},{64,32},{96,64},{128,96},{160,128},{192,160},{224,1... | collective-permute-start | bytes 49160 | tf_op jit(solution)/shard_map/ppermute | solution.py:511
  57.9 5.7 %collective-permute-start.4 = (f32[2,4,4,128]{3,2,1,0:T(4,128)S(1)}, f32[2,4,4,128]{3,2,1,0:T(4,128)S(1)}, u32[]{:S(2)}, u32[]{:S(2)}) collective-permute-start(f32[2,4,4,128]{3,2,1,0:T(4,128)S(1)} %pad_maximum_fusion.5), channel_id=1, source_target_pairs={{0,32},{32,64},{64,96},{96,128},{128,160},{160,192},{192,224},{224... | collective-permute-start | bytes 49160 | tf_op jit(solution)/shard_map/ppermute | solution.py:511
  77.1 5.6 %collective-permute-start.7 = (f32[2,4,4,128]{3,2,1,0:T(4,128)S(1)}, f32[2,4,4,128]{3,2,1,0:T(4,128)S(1)}, u32[]{:S(2)}, u32[]{:S(2)}) collective-permute-start(f32[2,4,4,128]{3,2,1,0:T(4,128)S(1)} %pad_maximum_fusion.6), channel_id=1, source_target_pairs={{0,480},{32,0},{64,32},{96,64},{128,96},{160,128},{192,160},{224,1... | collective-permute-start | bytes 49160 | tf_op jit(solution)/shard_map/ppermute | solution.py:511
  79.0 5.7 %collective-permute-start.6 = (f32[2,4,4,128]{3,2,1,0:T(4,128)S(1)}, f32[2,4,4,128]{3,2,1,0:T(4,128)S(1)}, u32[]{:S(2)}, u32[]{:S(2)}) collective-permute-start(f32[2,4,4,128]{3,2,1,0:T(4,128)S(1)} %pad_maximum_fusion.6), channel_id=1, source_target_pairs={{0,32},{32,64},{64,96},{96,128},{128,160},{160,192},{192,224},{224... | collective-permute-start | bytes 49160 | tf_op jit(solution)/shard_map/ppermute | solution.py:511
  97.9 4.5 %collective-permute-start.8 = (f32[2,4,4,128]{3,2,1,0:T(4,128)S(1)}, f32[2,4,4,128]{3,2,1,0:T(4,128)S(1)}, u32[]{:S(2)}, u32[]{:S(2)}) collective-permute-start(f32[2,4,4,128]{3,2,1,0:T(4,128)S(1)} %pad_maximum_fusion.7), channel_id=1, source_target_pairs={{0,480},{32,0},{64,32},{96,64},{128,96},{160,128},{192,160},{224,1... | collective-permute-start | bytes 49160 | tf_op jit(solution)/shard_map/ppermute | solution.py:511
  115.6 17.0 %all-to-all-start.5 = ((f32[16,1,128]{2,1,0:T(1,128)}), f32[16,1,128]{2,1,0:T(1,128)S(1)}, u32[]{:S(2)}, u32[]{:S(2)}) async-start(f32[16,1,128]{2,1,0:T(1,128)} %broadcast_in_dim.50), calls=%async_computation.5 | async-start | bytes 16384 | tf_op jit(solution)/shard_map/all_to_all | solution.py:516
  121.4 6.0 %collective-permute-start.9 = (f32[2,4,4,128]{3,2,1,0:T(4,128)S(1)}, f32[2,4,4,128]{3,2,1,0:T(4,128)S(1)}, u32[]{:S(2)}, u32[]{:S(2)}) collective-permute-start(f32[2,4,4,128]{3,2,1,0:T(4,128)S(1)} %pad_maximum_fusion.7), channel_id=1, source_target_pairs={{0,32},{32,64},{64,96},{96,128},{128,160},{160,192},{192,224},{224... | collective-permute-start | bytes 49160 | tf_op jit(solution)/shard_map/ppermute | solution.py:511
